TPU v7x, 32 devices: a whole 2x2x4 slice. The times are simulated.
32 devices in a mesh: dp: 4 (over x, core), blk: 8 (over z, y).
Axes of the slice: x: 2, y: 2, z: 4, core: 2. Of those that a mesh axis runs over, the one named last changes fastest.
Arguments:
- hidden: bfloat16 [8, 3, 1024, 1024], P('dp', None, 'blk'), may hold values from -6 to 6
- encoder: bfloat16 [8, 1024, 1024], P('dp', 'blk'), may hold values from -6 to 6
- lengths: int32 [8, 8], P('dp'), may hold values from 0 to 1024, as said below
- qkv_self: float32 [3, 1024, 1024], P(None, 'dp'), may hold values from -0.1875 to 0.1875
- out_self: float32 [1024, 1024], P('dp'), may hold values from -0.75 to 0.75
- rel_table: float32 [16, 32], replicated, may hold values from -4 to 4
- qkv_cross: float32 [3, 1024, 1024], P(None, 'dp'), may hold values from -0.1875 to 0.1875
- out_cross: float32 [1024, 1024], P('dp'), may hold values from -0.75 to 0.75
- ffn_in: float32 [1024, 4096], P('dp'), may hold values from -0.1875 to 0.1875
- ffn_out: float32 [4096, 1024], P('dp'), may hold values from -0.09375 to 0.09375
- norm_gain: float32 [3, 1024], replicated, may hold values from 0.5 to 1.5
- norm_bias: float32 [3, 1024], replicated, may hold values from -3 to 3
- cotangent: bfloat16 [8, 3, 1024, 1024], P('dp', None, 'blk'), may hold values from -6 to 6
Outputs:
- output: bfloat16 [8, 3, 1024, 1024], P('dp', None, 'blk')
- d_hidden: float32 [8, 3, 1024, 1024], P('dp', None, 'blk')
- d_encoder: float32 [8, 1024, 1024], P('dp', 'blk')
- g_qkv_self: float32 [3, 1024, 1024], P(None, ('dp', 'blk'))
- g_out_self: float32 [1024, 1024], P(('dp', 'blk'))
- g_rel_table: float32 [16, 32], replicated
- g_qkv_cross: float32 [3, 1024, 1024], P(None, ('dp', 'blk'))
- g_out_cross: float32 [1024, 1024], P(('dp', 'blk'))
- g_ffn_in: float32 [1024, 4096], P(('dp', 'blk'))
- g_ffn_out: float32 [4096, 1024], P(('dp', 'blk'))
- g_norm_gain: float32 [3, 1024], replicated
- g_norm_bias: float32 [3, 1024], replicated
Inputs may be any that keep to these rules, and one draw needn't show every extreme that they name: `lengths`: each row sums to 1024, nonzero entries first. In each group of 2 streams of one index of dp, one stream, drawn from the seed, is a single document of 1024 positions; the other streams hold documents of 128, 256 and 512 positions.
All inputs are finite; a program needn't handle non-finite values.
Results may differ from a plain program's by a relative error of at most 0.025.
The roundings to bfloat16 on the way count: a program that leaves them out, or rounds other values in their place, can miss the bound.
Values may be sent and summed in bfloat16 or wider, within the bound.
No kernel may reach another device: no remote copies, remote signals or barrier semaphores. Data moves between devices by JAX's collectives and lax.ppermute only.
A program may use at most 576 MiB of HBM per device.

v0:
```python
from functools import partial
import math

import jax
import jax.numpy as jnp
from jax import lax
from jax.sharding import PartitionSpec as P

highest = lax.Precision.HIGHEST
bucket_edges = tuple((math.ceil(16 * 8 ** (power / 16)) for power in range(1, 16)))


def segments_of(lengths, length_all):
    doc_ends = jnp.cumsum(lengths, axis=-1)
    places = jnp.arange(length_all, dtype=jnp.int32)
    return jnp.sum((places[None, :, None] >= doc_ends[:, None, :]).astype(jnp.int32), axis=-1)


def bucket_of(distance):
    nearby = jnp.maximum(distance, 0)
    distant = 16 + sum(((nearby >= edge).astype(jnp.int32) for edge in bucket_edges))
    return jnp.where(nearby < 16, nearby, distant)


def norm_parts(values_in):
    centred = values_in - jnp.mean(values_in, axis=-1, keepdims=True)
    inv_scale = lax.rsqrt(jnp.mean(centred * centred, axis=-1, keepdims=True) + 1e-05)
    return (centred * inv_scale, inv_scale)


def norm_back(grad_in, normed, inv_scale, gain_row):
    scaled = grad_in * gain_row
    return inv_scale * (
        scaled
        - jnp.mean(scaled, axis=-1, keepdims=True)
        - normed * jnp.mean(scaled * normed, axis=-1, keepdims=True)
    )


def matmul(left_side, right_side):
    return jnp.einsum("...i,ij->...j", left_side, right_side, preferred_element_type=jnp.float32)


def matmul_t(left_side, right_side):
    return jnp.einsum("...j,ij->...i", left_side, right_side, preferred_element_type=jnp.float32)


def outer_sum(left_side, right_side):
    return jnp.einsum("...i,...j->ij", left_side, right_side, preferred_element_type=jnp.float32)


def self_mask(same_doc, distance):
    later = same_doc & (distance > 0)
    return jnp.stack([same_doc & (distance >= 0), later, later])[:, None]


def split_heads(values_in, head_count):
    return values_in.reshape(values_in.shape[:-1] + (head_count, -1))


def self_scores(query_all, keys_all, keys_own, allowed, table_bias, rel_table, head_count):
    query_heads = split_heads(query_all, head_count)
    main_scores = (
        jnp.einsum(
            "clhe,she->chls",
            query_heads,
            split_heads(keys_all, head_count),
            preferred_element_type=jnp.float32,
        )
        * 0.125
        + table_bias[None]
    )
    own_scores = (
        jnp.einsum(
            "clhe,clhe->chl",
            query_heads,
            split_heads(keys_own, head_count),
            preferred_element_type=jnp.float32,
        )
        * 0.125
        + rel_table[:, 0][None, :, None]
    )
    streams_ok = (jnp.arange(3) > 0)[:, None, None]
    return (jnp.where(allowed, main_scores, -1e30), jnp.where(streams_ok, own_scores, -1e30))


def softmax_with_own(main_scores, own_scores):
    row_max = jnp.maximum(jnp.max(main_scores, axis=-1), own_scores)
    main_exp = jnp.exp(main_scores - row_max[..., None])
    own_exp = jnp.exp(own_scores - row_max)
    row_total = jnp.sum(main_exp, axis=-1) + own_exp
    return (main_exp / row_total[..., None], own_exp / row_total)


def self_forward(
    query_all,
    keys_all,
    values_all,
    keys_own,
    values_own,
    allowed,
    table_bias,
    rel_table,
    head_count,
):
    main_scores, own_scores = self_scores(
        query_all, keys_all, keys_own, allowed, table_bias, rel_table, head_count
    )
    main_prob, own_prob = softmax_with_own(main_scores, own_scores)
    own_weight = jnp.transpose(own_prob.astype(jnp.bfloat16), (0, 2, 1))[..., None].astype(
        jnp.float32
    )
    mixture = jnp.einsum(
        "chls,she->clhe",
        main_prob.astype(jnp.bfloat16),
        split_heads(values_all, head_count),
        preferred_element_type=jnp.float32,
    )
    mixture = mixture + own_weight * split_heads(values_own, head_count).astype(jnp.float32)
    return mixture.reshape(query_all.shape).astype(jnp.bfloat16)


def self_backward(
    query_all,
    keys_all,
    values_all,
    keys_own,
    values_own,
    allowed,
    table_bias,
    rel_table,
    head_count,
    grad_mixed,
):
    main_scores, own_scores = self_scores(
        query_all, keys_all, keys_own, allowed, table_bias, rel_table, head_count
    )
    main_prob, own_prob = softmax_with_own(main_scores, own_scores)
    grad_heads = split_heads(grad_mixed, head_count)
    main_grad = jnp.einsum(
        "clhe,she->chls",
        grad_heads,
        split_heads(values_all, head_count),
        preferred_element_type=jnp.float32,
    )
    own_grad = jnp.einsum(
        "clhe,clhe->chl",
        grad_heads,
        split_heads(values_own, head_count),
        preferred_element_type=jnp.float32,
    )
    centre = jnp.sum(main_prob * main_grad, axis=-1) + own_prob * own_grad
    main_low = (main_prob * (main_grad - centre[..., None])).astype(jnp.bfloat16)
    own_low = (own_prob * (own_grad - centre)).astype(jnp.bfloat16)
    own_wide = jnp.transpose(own_low.astype(jnp.float32), (0, 2, 1))[..., None]
    query_grad = jnp.einsum(
        "chls,she->clhe",
        main_low,
        split_heads(keys_all, head_count),
        preferred_element_type=jnp.float32,
    )
    query_grad = 0.125 * (
        query_grad + own_wide * split_heads(keys_own, head_count).astype(jnp.float32)
    )
    key_grad = 0.125 * own_wide * split_heads(query_all, head_count).astype(jnp.float32)
    prob_wide = jnp.transpose(own_prob.astype(jnp.bfloat16), (0, 2, 1))[..., None].astype(
        jnp.float32
    )
    value_grad = prob_wide * grad_heads.astype(jnp.float32)
    row_shape = query_all.shape
    return (
        query_grad.reshape(row_shape),
        key_grad.reshape(row_shape),
        value_grad.reshape(row_shape),
        main_low,
        own_low,
        main_prob.astype(jnp.bfloat16),
    )


def cross_probs(query_all, keys_all, allowed, head_count):
    scores = (
        jnp.einsum(
            "clhe,she->chls",
            split_heads(query_all, head_count),
            split_heads(keys_all, head_count),
            preferred_element_type=jnp.float32,
        )
        * 0.125
    )
    scores = jnp.where(allowed, scores, -1e30)
    row_max = jnp.max(scores, axis=-1, keepdims=True)
    exps = jnp.exp(scores - row_max)
    return exps / jnp.sum(exps, axis=-1, keepdims=True)


def cross_forward(query_all, keys_all, values_all, allowed, head_count):
    probs = cross_probs(query_all, keys_all, allowed, head_count)
    mixture = jnp.einsum(
        "chls,she->clhe",
        probs.astype(jnp.bfloat16),
        split_heads(values_all, head_count),
        preferred_element_type=jnp.float32,
    )
    return mixture.reshape(query_all.shape).astype(jnp.bfloat16)


def cross_backward(query_all, keys_all, values_all, allowed, head_count, grad_mixed):
    probs = cross_probs(query_all, keys_all, allowed, head_count)
    grad_heads = split_heads(grad_mixed, head_count)
    prob_grad = jnp.einsum(
        "clhe,she->chls",
        grad_heads,
        split_heads(values_all, head_count),
        preferred_element_type=jnp.float32,
    )
    centre = jnp.sum(probs * prob_grad, axis=-1, keepdims=True)
    score_low = (probs * (prob_grad - centre)).astype(jnp.bfloat16)
    query_grad = 0.125 * jnp.einsum(
        "chls,she->clhe",
        score_low,
        split_heads(keys_all, head_count),
        preferred_element_type=jnp.float32,
    )
    return (query_grad.reshape(query_all.shape), score_low, probs.astype(jnp.bfloat16))


def key_value_terms(score_low, prob_low, query_heads, grad_heads, row_count):
    key_term = 0.125 * jnp.einsum(
        "bchls,bclhe->sbhe", score_low, query_heads, preferred_element_type=jnp.float32
    )
    value_term = jnp.einsum(
        "bchls,bclhe->sbhe", prob_low, grad_heads, preferred_element_type=jnp.float32
    )
    stream_count = query_heads.shape[0]
    return jnp.concatenate(
        [
            key_term.reshape(row_count, stream_count, -1),
            value_term.reshape(row_count, stream_count, -1),
        ],
        axis=-1,
    )


def shards(
    hidden,
    encoder,
    lengths,
    qkv_self,
    out_self,
    rel_table,
    qkv_cross,
    out_cross,
    ffn_in,
    ffn_out,
    norm_gain,
    norm_bias,
    cotangent,
):
    stream_count = hidden.shape[0]
    local_rows = hidden.shape[2]
    model_width = hidden.shape[3]
    head_count = rel_table.shape[0]
    bucket_count = rel_table.shape[1]
    length_all = local_rows * lax.axis_size("blk")
    first_row = lax.axis_index("blk") * local_rows
    w_qkv, w_out, c_qkv, c_out, w_first, w_second = (
        lax.all_gather(qkv_self.astype(jnp.bfloat16), "dp", axis=1, tiled=True),
        lax.all_gather(out_self.astype(jnp.bfloat16), "dp", axis=0, tiled=True),
        lax.all_gather(qkv_cross.astype(jnp.bfloat16), "dp", axis=1, tiled=True),
        lax.all_gather(out_cross.astype(jnp.bfloat16), "dp", axis=0, tiled=True),
        lax.all_gather(ffn_in.astype(jnp.bfloat16), "dp", axis=0, tiled=True),
        lax.all_gather(ffn_out.astype(jnp.bfloat16), "dp", axis=0, tiled=True),
    )
    places = jnp.arange(length_all, dtype=jnp.int32)
    query_rows = first_row + jnp.arange(local_rows, dtype=jnp.int32)
    distance = query_rows[:, None] - places[None, :]
    onehot_wide = (
        bucket_of(distance)[..., None] == jnp.arange(bucket_count, dtype=jnp.int32)
    ).astype(jnp.float32)
    table_bias = jnp.einsum("lsk,hk->hls", onehot_wide, rel_table, precision=highest)
    onehot_low = onehot_wide.astype(jnp.bfloat16)
    segment = segments_of(lengths, length_all)
    local_segment = lax.dynamic_slice_in_dim(segment, first_row, local_rows, 1)
    same_doc = local_segment[:, :, None] == segment[:, None, :]
    projected = jnp.einsum(
        "bcld,kde->kbcle", hidden, w_qkv, preferred_element_type=jnp.float32
    ).astype(jnp.bfloat16)
    query_all, key_local, value_local = (projected[0], projected[1], projected[2])
    cross_kv = jnp.einsum(
        "bld,kde->kble", encoder, c_qkv[1:], preferred_element_type=jnp.float32
    ).astype(jnp.bfloat16)
    main_keys, main_values, enc_keys, enc_values = (
        lax.all_gather(key_local[:, 0], "blk", axis=1, tiled=True),
        lax.all_gather(value_local[:, 0], "blk", axis=1, tiled=True),
        lax.all_gather(cross_kv[0], "blk", axis=1, tiled=True),
        lax.all_gather(cross_kv[1], "blk", axis=1, tiled=True),
    )
    attended = jnp.stack(
        [
            self_forward(
                query_all[stream],
                main_keys[stream],
                main_values[stream],
                key_local[stream],
                value_local[stream],
                self_mask(same_doc[stream], distance),
                table_bias,
                rel_table,
                head_count,
            )
            for stream in range(stream_count)
        ]
    )
    first_norm, first_scale = norm_parts(hidden.astype(jnp.float32) + matmul(attended, w_out))
    first_out = first_norm * norm_gain[0] + norm_bias[0]
    first_low = first_out.astype(jnp.bfloat16)
    cross_query = matmul(first_low, c_qkv[0]).astype(jnp.bfloat16)
    cross_att = jnp.stack(
        [
            cross_forward(
                cross_query[stream],
                enc_keys[stream],
                enc_values[stream],
                same_doc[stream][None, None],
                head_count,
            )
            for stream in range(stream_count)
        ]
    )
    second_norm, second_scale = norm_parts(first_out + matmul(cross_att, c_out))
    second_out = second_norm * norm_gain[1] + norm_bias[1]
    second_low = second_out.astype(jnp.bfloat16)
    inner_act = matmul(second_low, w_first)
    activated = jax.nn.gelu(inner_act, approximate=False).astype(jnp.bfloat16)
    third_norm, third_scale = norm_parts(second_out + matmul(activated, w_second))
    output = (third_norm * norm_gain[2] + norm_bias[2]).astype(jnp.bfloat16)
    row_axes = (0, 1, 2)
    grad_out = cotangent.astype(jnp.float32)
    gain_three = jnp.sum(grad_out * third_norm, axis=row_axes)
    bias_three = jnp.sum(grad_out, axis=row_axes)
    third_grad = norm_back(grad_out, third_norm, third_scale, norm_gain[2])
    third_low = third_grad.astype(jnp.bfloat16)
    grad_second_w = outer_sum(activated, third_low)
    act_grad = matmul_t(third_low, w_second)
    gelu_values, gelu_pull = jax.vjp(partial(jax.nn.gelu, approximate=False), inner_act)
    inner_grad = gelu_pull(act_grad)[0].astype(jnp.bfloat16)
    grad_first_w = outer_sum(second_low, inner_grad)
    second_total = third_grad + matmul_t(inner_grad, w_first)
    gain_two = jnp.sum(second_total * second_norm, axis=row_axes)
    bias_two = jnp.sum(second_total, axis=row_axes)
    second_grad = norm_back(second_total, second_norm, second_scale, norm_gain[1])
    cross_low = second_grad.astype(jnp.bfloat16)
    grad_cross_out = outer_sum(cross_att, cross_low)
    cross_mix_grad = matmul_t(cross_low, c_out).astype(jnp.bfloat16)
    back_keys, back_values, back_enc_keys, back_enc_values = (
        lax.all_gather(key_local[:, 0], "blk", axis=1, tiled=True),
        lax.all_gather(value_local[:, 0], "blk", axis=1, tiled=True),
        lax.all_gather(cross_kv[0], "blk", axis=1, tiled=True),
        lax.all_gather(cross_kv[1], "blk", axis=1, tiled=True),
    )
    cross_parts = [
        cross_backward(
            cross_query[stream],
            back_enc_keys[stream],
            back_enc_values[stream],
            same_doc[stream][None, None],
            head_count,
            cross_mix_grad[stream],
        )
        for stream in range(stream_count)
    ]
    cross_query_grad = jnp.stack([piece[0] for piece in cross_parts]).astype(jnp.bfloat16)
    cross_score_all = jnp.stack([piece[1] for piece in cross_parts])
    cross_prob_all = jnp.stack([piece[2] for piece in cross_parts])
    cross_query_heads = split_heads(cross_query, head_count)
    cross_grad_heads = split_heads(cross_mix_grad, head_count)
    cross_back = lax.psum_scatter(
        key_value_terms(
            cross_score_all,
            cross_prob_all,
            cross_query_heads,
            cross_grad_heads,
            local_rows * lax.axis_size("blk"),
        ).astype(jnp.bfloat16),
        "blk",
        scatter_dimension=0,
        tiled=True,
    ).astype(jnp.float32)
    cross_kv_grad = jnp.transpose(cross_back, (1, 0, 2)).astype(jnp.bfloat16)
    enc_key_grad = cross_kv_grad[..., :model_width]
    enc_value_grad = cross_kv_grad[..., model_width:]
    grad_cross = jnp.stack(
        [
            outer_sum(first_low, cross_query_grad),
            outer_sum(encoder, enc_key_grad),
            outer_sum(encoder, enc_value_grad),
        ]
    )
    encoder_grad = matmul_t(enc_key_grad, c_qkv[1]) + matmul_t(enc_value_grad, c_qkv[2])
    first_total = second_grad + matmul_t(cross_query_grad, c_qkv[0])
    gain_one = jnp.sum(first_total * first_norm, axis=row_axes)
    bias_one = jnp.sum(first_total, axis=row_axes)
    first_grad = norm_back(first_total, first_norm, first_scale, norm_gain[0])
    out_low = first_grad.astype(jnp.bfloat16)
    grad_self_out = outer_sum(attended, out_low)
    mix_grad = matmul_t(out_low, w_out).astype(jnp.bfloat16)
    self_parts = [
        self_backward(
            query_all[stream],
            back_keys[stream],
            back_values[stream],
            key_local[stream],
            value_local[stream],
            self_mask(same_doc[stream], distance),
            table_bias,
            rel_table,
            head_count,
            mix_grad[stream],
        )
        for stream in range(stream_count)
    ]
    query_grad = jnp.stack([piece[0] for piece in self_parts]).astype(jnp.bfloat16)
    own_key_grad = jnp.stack([piece[1] for piece in self_parts])
    own_value_grad = jnp.stack([piece[2] for piece in self_parts])
    score_all = jnp.stack([piece[3] for piece in self_parts])
    prob_all = jnp.stack([piece[5] for piece in self_parts])
    rel_grad = jnp.einsum(
        "bchls,lsk->hk", score_all, onehot_low, preferred_element_type=jnp.float32
    )
    own_total = sum((jnp.sum(piece[4].astype(jnp.float32), axis=(0, 2)) for piece in self_parts))
    rel_grad = (
        rel_grad + own_total[:, None] * (jnp.arange(bucket_count) == 0).astype(jnp.float32)[None, :]
    )
    query_heads = split_heads(query_all, head_count)
    grad_heads = split_heads(mix_grad, head_count)
    self_back = lax.psum_scatter(
        key_value_terms(
            score_all, prob_all, query_heads, grad_heads, local_rows * lax.axis_size("blk")
        ).astype(jnp.bfloat16),
        "blk",
        scatter_dimension=0,
        tiled=True,
    ).astype(jnp.float32)
    main_kv_grad = jnp.transpose(self_back, (1, 0, 2))
    key_grad = jnp.concatenate(
        [main_kv_grad[:, None, :, :model_width], own_key_grad[:, 1:]], axis=1
    ).astype(jnp.bfloat16)
    value_grad = jnp.concatenate(
        [main_kv_grad[:, None, :, model_width:], own_value_grad[:, 1:]], axis=1
    ).astype(jnp.bfloat16)
    grad_qkv = jnp.stack(
        [outer_sum(hidden, query_grad), outer_sum(hidden, key_grad), outer_sum(hidden, value_grad)]
    )
    hidden_grad = (
        first_grad
        + matmul_t(query_grad, w_qkv[0])
        + matmul_t(key_grad, w_qkv[1])
        + matmul_t(value_grad, w_qkv[2])
    )
    shares = (
        lax.psum_scatter(grad_qkv, ("dp", "blk"), scatter_dimension=1, tiled=True),
        lax.psum_scatter(grad_self_out, ("dp", "blk"), scatter_dimension=0, tiled=True),
        lax.psum_scatter(grad_cross, ("dp", "blk"), scatter_dimension=1, tiled=True),
        lax.psum_scatter(grad_cross_out, ("dp", "blk"), scatter_dimension=0, tiled=True),
        lax.psum_scatter(grad_first_w, ("dp", "blk"), scatter_dimension=0, tiled=True),
        lax.psum_scatter(grad_second_w, ("dp", "blk"), scatter_dimension=0, tiled=True),
    )
    small_sums = lax.psum(
        (
            rel_grad,
            jnp.stack([gain_one, gain_two, gain_three]),
            jnp.stack([bias_one, bias_two, bias_three]),
        ),
        ("dp", "blk"),
    )
    return (
        output,
        hidden_grad,
        encoder_grad,
        shares[0],
        shares[1],
        small_sums[0],
        shares[2],
        shares[3],
        shares[4],
        shares[5],
        small_sums[1],
        small_sums[2],
    )


def solution(mesh):
    in_specs = (
        P("dp", None, "blk", None),
        P("dp", "blk", None),
        P("dp", None),
        P(None, "dp", None),
        P("dp", None),
        P(),
        P(None, "dp", None),
        P("dp", None),
        P("dp", None),
        P("dp", None),
        P(),
        P(),
        P("dp", None, "blk", None),
    )
    out_specs = (
        P("dp", None, "blk", None),
        P("dp", None, "blk", None),
        P("dp", "blk", None),
        P(None, ("dp", "blk"), None),
        P(("dp", "blk"), None),
        P(),
        P(None, ("dp", "blk"), None),
        P(("dp", "blk"), None),
        P(("dp", "blk"), None),
        P(("dp", "blk"), None),
        P(),
        P(),
    )
    return jax.shard_map(shards, mesh=mesh, in_specs=in_specs, out_specs=out_specs, check_vma=False)
```

profile of v0, /device:TPU:0, one launch (start us, length us, event | category | flops | bytes accessed | tf_op | source)
XLA Modules:
  0.0 2811.4 jit_solution(10405627544595996936)
XLA Ops:
  13.6 46.8 %all-gather.15.cloned.1.call-done = bf16[3,1024,1024]{1,2,0:T(8,128)(2,1)} async-done(((bf16[3,256,1024]{1,2,0:T(8,128)(2,1)}), bf16[3,1024,1024]{1,2,0:T(8,128)(2,1)}) %all-gather.15.cloned.1.call-update) | async-done | bytes 6291472 | tf_op jit(solution)/shard_map/all_gather | solution.py:268
  73.4 36.4 %all-gather.19.cloned.1.call-done = bf16[3,1024,1024]{1,2,0:T(8,128)(2,1)} async-done(((bf16[3,256,1024]{1,2,0:T(8,128)(2,1)}), bf16[3,1024,1024]{1,2,0:T(8,128)(2,1)}) %all-gather.19.cloned.1.call-update) | async-done | bytes 6291472 | tf_op jit(solution)/shard_map/all_gather | solution.py:270
  153.8 33.1 %all-gather.29.cloned.1.call-done = bf16[2,1,1024,1024]{2,3,1,0:T(8,128)(2,1)} async-done(((bf16[2,1,128,1024]{2,3,1,0:T(8,128)(2,1)}), bf16[2,1,1024,1024]{2,3,1,0:T(8,128)(2,1)}) %all-gather.29.cloned.1.call-update) | async-done | bytes 4194320 | tf_op jit(solution)/shard_map/all_gather | solution.py:294
  191.1 14.1 fusion.35
  206.0 28.0 fusion.29
  234.8 11.6 fusion.31
  248.6 13.5 all-gather.27.cloned.1.call-done
  266.1 17.0 fusion.146
  287.2 14.6 fusion.144
  313.9 48.5 %all-gather.33.cloned.1.call-done = bf16[1,2,1024,1024]{2,3,1,0:T(8,128)(2,1)} async-done(((bf16[1,2,128,1024]{2,3,1,0:T(8,128)(2,1)}), bf16[1,2,1024,1024]{2,3,1,0:T(8,128)(2,1)}) %all-gather.33.cloned.1.call-update) | async-done | bytes 4194320 | tf_op jit(solution)/shard_map/all_gather | solution.py:296
  366.3 14.5 fusion.295
  380.9 56.8 %all-gather.31.cloned.1.call-done = bf16[1,2,1024,1024]{2,3,1,0:T(8,128)(2,1)} async-done(((bf16[1,2,128,1024]{2,3,1,0:T(8,128)(2,1)}), bf16[1,2,1024,1024]{2,3,1,0:T(8,128)(2,1)}) %all-gather.31.cloned.1.call-update) | async-done | bytes 4194320 | tf_op jit(solution)/shard_map/all_gather | solution.py:297
  440.3 12.6 fusion.171
  452.9 13.8 fusion.290
  466.8 13.9 fusion.168
  491.5 28.9 %all-gather.23.cloned.1.call-done = bf16[1024,4096]{1,0:T(8,128)(2,1)} async-done(((bf16[256,4096]{1,0:T(8,128)(2,1)}), bf16[1024,4096]{1,0:T(8,128)(2,1)}) %all-gather.23.cloned.1.call-update) | async-done | bytes 8388624 | tf_op jit(solution)/shard_map/all_gather | solution.py:272
  520.5 15.5 fusion.95
  540.5 30.7 %multiply_convert_fusion = (bf16[2,3,128,4096]{3,2,1,0:T(8,128)(2,1)}, f32[2,3,128,4096]{3,2,1,0:T(8,128)}) fusion(f32[2,3,128,4096]{3,2,1,0:T(8,128)S(1)} %get-tuple-element.196, u8[2,128,4096]{2,1,0:T(8,128)(4,1)} %get-tuple-element.85, u8[2,128,4096]{2,1,0:T(8,128)(4,1)} %get-tuple-element.84), kind=kLoop, calls=%fused_computation.68 | loop fusion | flops 220200960 | bytes 33554432 | tf_op jit(solution)/shard_map/convert_element_type | solution.py:335
  580.2 11.7 fusion.301
  599.0 20.3 add_convert_fusion
  619.3 16.1 multiply_reduce_fusion
  643.5 13.4 fusion.185
  656.9 21.4 convert_bitcast_fusion.1
  684.0 14.3 fusion.25
  707.7 10.2 fusion.183
  718.0 21.4 convert_bitcast_fusion
  745.1 14.4 fusion.22
  783.1 10.2 fusion.179
  795.7 39.1 %fusion.17 = (f32[3,16,128]{2,0,1:T(4,128)S(1)}, f32[3,16,128]{2,0,1:T(4,128)S(1)}, f32[16,1024,3,128]{3,1,2,0:T(8,128)}) fusion(f32[3,16,128]{2,0,1:T(4,128)} %copy-done.93, f32[3,16,128]{2,0,1:T(4,128)} %copy-done.91, f32[16,128,1024]{1,2,0:T(8,128)} %copy.437, f32[16,1024,3,128]{3,1,2,0:T(8,128)} %get-tuple-element.186, ...), kind=kOutput, calls=%fused_computation.23 | convolution fusion | flops 893374464 | bytes 112869376 | tf_op jit(solution)/shard_map/clhe,she->chls/dot_general | solution.py:140
  836.9 52.0 %fusion.19 = (bf16[3,16,128,1024]{2,3,0,1:T(8,128)(2,1)}, bf16[1,3,16,128,1024]{3,4,1,2,0:T(8,128)(2,1)}, bf16[1,3,16,128,1024]{3,4,1,2,0:T(8,128)(2,1)}, bf16[3,16,128,1024]{2,3,0,1:T(8,128)(2,1)}) fusion(f32[16,1024,3,128]{3,1,2,0:T(8,128)} %get-tuple-element.201, f32[3,16,128]{2,0,1:T(4,128)S(1)} %copy.487, f32[3,16,128]{2,0,1:T(4,128)} %copy-done.93, ...), kind=kLoop, calls=%fused_computation.25 | loop fusion | flops 113246208 | bytes 160317440 | tf_op jit(solution)/shard_map/convert_element_type | solution.py:153
  888.9 14.1 fusion.52
  903.0 14.4 bitcast_convert_fusion.1
  925.2 11.5 copy.642
  942.0 15.1 fusion.51
  963.4 14.2 bitcast_convert_fusion
  1028.1 57.9 %reduce-scatter.22.cloned.1.call-done = bf16[128,4096]{1,0:T(8,128)(2,1)} async-done(((bf16[1024,4096]{1,0:T(8,128)(2,1)}), bf16[128,4096]{1,0:T(8,128)(2,1)}) %reduce-scatter.22.cloned.1.call-update) | async-done | bytes 1048592
  1099.9 18.4 copy.530
  1133.4 13.8 convolution_bitcast_fusion.1
  1148.7 13.5 convolution_bitcast_fusion
  1169.8 68.1 %reduce-scatter.10.cloned.1.call-done = bf16[128,2,2048]{2,0,1:T(8,128)(2,1)} async-done(((bf16[1024,2,2048]{2,0,1:T(8,128)(2,1)}), bf16[128,2,2048]{2,0,1:T(8,128)(2,1)}) %reduce-scatter.10.cloned.1.call-update) | async-done | bytes 1048592 | tf_op jit(solution)/shard_map/reduce_scatter | solution.py:378
  1246.9 13.4 convert_reduce_fusion
  1272.0 41.4 %all-reduce.1 = (f32[16,32]{1,0:T(8,128)}, f32[3,1024]{1,0:T(4,128)}, f32[3,1024]{1,0:T(4,128)}) all-reduce(f32[16,32]{1,0:T(8,128)S(1)} %fusion.177, f32[3,1024]{1,0:T(4,128)S(1)} %pad_maximum_fusion.20, f32[3,1024]{1,0:T(4,128)S(1)} %pad_maximum_fusion.21), channel_id=1, replica_groups=mesh['dp'=4,'blk'=8] {'dp','blk'}, use_global_device_ids=true, to_apply=%region_33.34 | all-reduce | flops 6656 | bytes 53248 | tf_op jit(solution)/shard_map/psum | solution.py:469
  1328.8 193.6 %all-reduce.4.cloned.1.call-done = f32[3,1024,1024]{2,0,1:T(4,128)} async-done(((f32[3,1024,1024]{2,0,1:T(4,128)}), f32[3,1024,1024]{2,0,1:T(4,128)}) %all-reduce.4.cloned.1.call-update) | async-done | bytes 12582928
  1524.5 144.8 %reduce-scatter.12.cloned.1.call-done = f32[32,1024]{1,0:T(8,128)} async-done(((f32[1024,1024]{1,0:T(8,128)}), f32[32,1024]{1,0:T(8,128)}) %reduce-scatter.12.cloned.1.call-update) | async-done | bytes 131088 | tf_op jit(solution)/shard_map/reduce_scatter | solution.py:463
  1669.3 143.3 %reduce-scatter.16.cloned.1.call-done = f32[32,1024]{1,0:T(8,128)} async-done(((f32[1024,1024]{1,0:T(8,128)}), f32[32,1024]{1,0:T(8,128)}) %reduce-scatter.16.cloned.1.call-update) | async-done | bytes 131088 | tf_op jit(solution)/shard_map/reduce_scatter | solution.py:465
  1812.7 358.4 %reduce-scatter.18.cloned.1.call-done = f32[32,4096]{1,0:T(8,128)} async-done(((f32[1024,4096]{1,0:T(8,128)}), f32[32,4096]{1,0:T(8,128)}) %reduce-scatter.18.cloned.1.call-update) | async-done | bytes 524304 | tf_op jit(solution)/shard_map/reduce_scatter | solution.py:466
  2171.1 360.1 %reduce-scatter.20.cloned.1.call-done = f32[128,1024]{1,0:T(8,128)} async-done(((f32[4096,1024]{1,0:T(8,128)}), f32[128,1024]{1,0:T(8,128)}) %reduce-scatter.20.cloned.1.call-update) | async-done | bytes 524304 | tf_op jit(solution)/shard_map/reduce_scatter | solution.py:467
  2531.1 273.2 %reduce-scatter.14.cloned.1.call-done = f32[3,32,1024]{2,1,0:T(8,128)} async-done(((f32[3,1024,1024]{2,1,0:T(8,128)}), f32[3,32,1024]{2,1,0:T(8,128)}) %reduce-scatter.14.cloned.1.call-update) | async-done | bytes 393232 | tf_op jit(solution)/shard_map/reduce_scatter | solution.py:464
  (454 shorter events, 330.9 us)
Async XLA Ops:
  7.2 102.6 %copy-start = (bf16[2,128,1024]{2,1,0:T(8,128)(2,1)S(1)}, bf16[2,128,1024]{2,1,0:T(8,128)(2,1)}, u32[]{:S(2)}) copy-start(bf16[2,128,1024]{2,1,0:T(8,128)(2,1)} %param.14) | copy-start | bytes 1572868
  7.2 53.2 %all-gather.15.cloned.1.call-start = ((), (), s32[]{:S(2)}) async-start(), calls=%async_computation.7 | async-start | bytes 7864320 | tf_op jit(solution)/shard_map/all_gather | solution.py:268
  10.3 50.1 %copy-start.127 = (bf16[2,3,128,1024]{3,2,1,0:T(8,128)(2,1)S(1)}, bf16[2,3,128,1024]{3,2,1,0:T(8,128)(2,1)}, u32[]{:S(2)}) copy-start(bf16[2,3,128,1024]{3,2,1,0:T(8,128)(2,1)} %param.13) | copy-start | bytes 4718596
  10.4 99.4 %all-gather.19.cloned.1.call-start = ((), (), s32[]{:S(2)}) async-start(), calls=%async_computation.9 | async-start | bytes 7864320 | tf_op jit(solution)/shard_map/all_gather | solution.py:270
  13.6 173.3 %all-gather.29.cloned.1.call-start = ((), (), s32[]{:S(2)}) async-start(), calls=%async_computation.20 | async-start | bytes 4718592 | tf_op jit(solution)/shard_map/all_gather | solution.py:294
  71.4 190.6 %all-gather.27.cloned.1.call-start = ((), (), s32[]{:S(2)}) async-start(), calls=%async_computation.19 | async-start | bytes 4718592 | tf_op jit(solution)/shard_map/all_gather | solution.py:295
  72.4 229.9 %all-gather.17.cloned.1.call-start = ((), (), s32[]{:S(2)}) async-start(), calls=%async_computation.8 | async-start | bytes 2621440 | tf_op jit(solution)/shard_map/all_gather | solution.py:269
  73.3 41.8 %copy-start.54 = (f32[256,1024]{1,0:T(8,128)S(1)}, f32[256,1024]{1,0:T(8,128)}, u32[]{:S(2)}) copy-start(f32[256,1024]{1,0:T(8,128)} %param.20) | copy-start | bytes 3145732
  73.3 289.0 %all-gather.33.cloned.1.call-start = ((), (), s32[]{:S(2)}) async-start(), calls=%async_computation.22 | async-start | bytes 4718592 | tf_op jit(solution)/shard_map/all_gather | solution.py:296
  114.3 323.3 %all-gather.31.cloned.1.call-start = ((), (), s32[]{:S(2)}) async-start(), calls=%async_computation.21 | async-start | bytes 4718592 | tf_op jit(solution)/shard_map/all_gather | solution.py:297
  115.1 369.2 %all-gather.21.cloned.1.call-start = ((), (), s32[]{:S(2)}) async-start(), calls=%async_computation.10 | async-start | bytes 2621440 | tf_op jit(solution)/shard_map/all_gather | solution.py:271
  116.0 404.4 %all-gather.23.cloned.1.call-start = ((), (), s32[]{:S(2)}) async-start(), calls=%async_computation.11 | async-start | bytes 10485760 | tf_op jit(solution)/shard_map/all_gather | solution.py:272
  120.0 460.2 %all-gather.25.cloned.1.call-start = ((), (), s32[]{:S(2)}) async-start(), calls=%async_computation.12 | async-start | bytes 10485760 | tf_op jit(solution)/shard_map/all_gather | solution.py:273
  124.1 961.9 %reduce-scatter.22.cloned.1.call-start = ((), (), s32[]{:S(2)}) async-start(), calls=%async_computation.23 | async-start | bytes 9437184
  145.7 338.6 %copy-start.106 = (f32[1,1024]{1,0:T(1,128)}, f32[1,1024]{1,0:T(1,128)S(1)}, u32[]{:S(2)}) copy-start(f32[1,1024]{1,0:T(1,128)S(1)} %get-tuple-element.177) | copy-start | bytes 12292
  147.2 118.9 %copy-start.38 = (pred[3,128,1024]{1,2,0:T(8,128)(4,1)}, pred[3,128,1024]{1,2,0:T(8,128)(4,1)S(1)}, u32[]{:S(2)}) copy-start(pred[3,128,1024]{1,2,0:T(8,128)(4,1)S(1)} %get-tuple-element.202) | copy-start | bytes 1179652
  186.9 19.1 slice-start
  206.0 28.1 copy-start.91
  206.0 28.1 copy-start.112
  206.0 28.1 copy-start.115
  206.0 28.8 %copy-start.40 = (pred[3,128,1024]{1,2,0:T(8,128)(4,1)S(1)}, pred[3,128,1024]{1,2,0:T(8,128)(4,1)}, u32[]{:S(2)}) copy-start(pred[3,128,1024]{1,2,0:T(8,128)(4,1)} %get-tuple-element.203) | copy-start | bytes 1179652
  266.1 21.1 copy-start.9
  266.1 21.1 copy-start.83
  266.1 21.1 copy-start.81
  306.7 177.6 %copy-start.98 = (f32[2,3,128]{2,1,0:T(4,128)}, f32[2,3,128]{2,1,0:T(4,128)S(1)}, u32[]{:S(2)}) copy-start(f32[2,3,128]{2,1,0:T(4,128)S(1)} %broadcast_multiply_fusion.10) | copy-start | bytes 9220
  307.2 177.1 %copy-start.103 = (f32[2,3,128]{2,1,0:T(4,128)}, f32[2,3,128]{2,1,0:T(4,128)S(1)}, u32[]{:S(2)}) copy-start(f32[2,3,128]{2,1,0:T(4,128)S(1)} %add_rsqrt_fusion.2) | copy-start | bytes 9220
  380.8 59.5 %copy-start.89 = (f32[3,16,128]{2,0,1:T(4,128)}, f32[3,16,128]{2,0,1:T(4,128)S(1)}, u32[]{:S(2)}) copy-start(f32[3,16,128]{2,0,1:T(4,128)S(1)} %get-tuple-element.192) | copy-start | bytes 73732
  484.3 36.2 %copy-start.74 = (f32[1,1024]{1,0:T(1,128)S(1)}, f32[1,1024]{1,0:T(1,128)}, u32[]{:S(2)}) copy-start(f32[1,1024]{1,0:T(1,128)} %get-tuple-element.178) | copy-start | bytes 12292
  484.3 36.2 %copy-start.78 = (f32[1,1024]{1,0:T(1,128)S(1)}, f32[1,1024]{1,0:T(1,128)}, u32[]{:S(2)}) copy-start(f32[1,1024]{1,0:T(1,128)} %get-tuple-element.181) | copy-start | bytes 12292
  489.4 146.0 %copy-start.72 = (f32[2,3,128]{2,1,0:T(4,128)}, f32[2,3,128]{2,1,0:T(4,128)S(1)}, u32[]{:S(2)}) copy-start(f32[2,3,128]{2,1,0:T(4,128)S(1)} %broadcast_multiply_fusion.9) | copy-start | bytes 9220
  491.5 143.9 %copy-start.76 = (f32[2,3,128]{2,1,0:T(4,128)}, f32[2,3,128]{2,1,0:T(4,128)S(1)}, u32[]{:S(2)}) copy-start(f32[2,3,128]{2,1,0:T(4,128)S(1)} %add_rsqrt_fusion.1) | copy-start | bytes 9220
  656.9 27.1 copy-start.1
  718.0 27.1 copy-start.2
  795.6 39.2 %copy-start.47 = (bf16[1,1,3,128,1024]{3,4,2,1,0:T(8,128)(2,1)S(1)}, bf16[1,1,3,128,1024]{3,4,2,1,0:T(8,128)(2,1)}, u32[]{:S(2)}) copy-start(bf16[1,1,3,128,1024]{3,4,2,1,0:T(8,128)(2,1)} %get-tuple-element.139) | copy-start | bytes 2359300
  795.6 39.5 %copy-start.96 = (f32[3,16,128]{2,1,0:T(8,128)S(1)}, f32[3,16,128]{2,1,0:T(8,128)}, u32[]{:S(2)}) copy-start(f32[3,16,128]{2,1,0:T(8,128)} %get-tuple-element.115) | copy-start | bytes 73732
  795.6 40.2 %copy-start.46 = (bf16[1,1,3,128,1024]{3,4,2,1,0:T(8,128)(2,1)S(1)}, bf16[1,1,3,128,1024]{3,4,2,1,0:T(8,128)(2,1)}, u32[]{:S(2)}) copy-start(bf16[1,1,3,128,1024]{3,4,2,1,0:T(8,128)(2,1)} %get-tuple-element.138) | copy-start | bytes 2359300
  795.6 40.2 %copy-start.49 = (bf16[1,3,128,1024]{2,3,1,0:T(8,128)(2,1)S(1)}, bf16[1,3,128,1024]{2,3,1,0:T(8,128)(2,1)}, u32[]{:S(2)}) copy-start(bf16[1,3,128,1024]{2,3,1,0:T(8,128)(2,1)} %copy.484) | copy-start | bytes 2359300
  795.6 40.6 %copy-start.97 = (f32[3,16,128]{2,1,0:T(8,128)S(1)}, f32[3,16,128]{2,1,0:T(8,128)}, u32[]{:S(2)}) copy-start(f32[3,16,128]{2,1,0:T(8,128)} %get-tuple-element.113) | copy-start | bytes 73732
  795.6 41.2 %copy-start.39 = (pred[3,128,1024]{1,2,0:T(8,128)(4,1)S(1)}, pred[3,128,1024]{1,2,0:T(8,128)(4,1)}, u32[]{:S(2)}) copy-start(pred[3,128,1024]{1,2,0:T(8,128)(4,1)} %copy-done.38) | copy-start | bytes 1179652
  795.7 41.2 %copy-start.41 = (pred[3,128,1024]{1,2,0:T(8,128)(4,1)S(1)}, pred[3,128,1024]{1,2,0:T(8,128)(4,1)}, u32[]{:S(2)}) copy-start(pred[3,128,1024]{1,2,0:T(8,128)(4,1)} %get-tuple-element.203) | copy-start | bytes 1179652
  836.9 52.0 %copy-start.51 = (bf16[1,2,3,128,1024]{3,4,2,1,0:T(8,128)(2,1)S(1)}, bf16[1,2,3,128,1024]{3,4,2,1,0:T(8,128)(2,1)}, u32[]{:S(2)}) copy-start(bf16[1,2,3,128,1024]{3,4,2,1,0:T(8,128)(2,1)} %get-tuple-element.135) | copy-start | bytes 4718596
  936.8 301.1 %reduce-scatter.10.cloned.1.call-start = ((), (), s32[]{:S(2)}) async-start(), calls=%async_computation.13 | async-start | bytes 9437184 | tf_op jit(solution)/shard_map/reduce_scatter | solution.py:378
  992.3 530.1 %all-reduce.4.cloned.1.call-start = ((), (), s32[]{:S(2)}) async-start(), calls=%async_computation.24 | async-start | bytes 33554432
  1118.4 551.0 %reduce-scatter.12.cloned.1.call-start = ((), (), s32[]{:S(2)}) async-start(), calls=%async_computation.14 | async-start | bytes 4325376 | tf_op jit(solution)/shard_map/reduce_scatter | solution.py:463
  1125.5 687.2 %reduce-scatter.16.cloned.1.call-start = ((), (), s32[]{:S(2)}) async-start(), calls=%async_computation.16 | async-start | bytes 4325376 | tf_op jit(solution)/shard_map/reduce_scatter | solution.py:465
  1132.8 1038.3 %reduce-scatter.18.cloned.1.call-start = ((), (), s32[]{:S(2)}) async-start(), calls=%async_computation.17 | async-start | bytes 17301504 | tf_op jit(solution)/shard_map/reduce_scatter | solution.py:466
  1147.3 1383.9 %reduce-scatter.20.cloned.1.call-start = ((), (), s32[]{:S(2)}) async-start(), calls=%async_computation.18 | async-start | bytes 17301504 | tf_op jit(solution)/shard_map/reduce_scatter | solution.py:467
  1162.3 1642.0 %reduce-scatter.14.cloned.1.call-start = ((), (), s32[]{:S(2)}) async-start(), calls=%async_computation.15 | async-start | bytes 12976128 | tf_op jit(solution)/shard_map/reduce_scatter | solution.py:464
  (104 other events, 584.1 us)
Sparse Core Ops, SparseCore 0:
  10.5 49.8 all-gather.14
  62.5 47.2 all-gather.18
  111.8 75.0 all-gather.28
  188.8 73.1 all-gather.26
  264.0 20.7 all-gather.16
  287.3 75.0 all-gather.32
  364.4 73.1 all-gather.30
  439.8 20.7 all-gather.20
  462.1 58.2 all-gather.22
  521.9 58.2 all-gather.24
  936.9 149.0 reduce-scatter.21
  1089.8 148.0 reduce-scatter.9
  1243.9 278.3 all-reduce.3
  1525.1 144.2 reduce-scatter.11
  1672.0 140.5 reduce-scatter.15
  1815.4 355.6 reduce-scatter.17
  2173.8 357.3 reduce-scatter.19
  2533.9 270.3 reduce-scatter.13
where the time goes:
time: 2820 us; the launch traced here: 2810 us
  waiting for transfers between devices  1870 us (66%)
  matrix products  469 us (17%)
  other arithmetic  240 us (9%)
  local copies, waits for them, and re-layouts  170 us (6%)
  blocking collectives  41.4 us (1%)
    reduce_scatter x1, waiting for transfers between devices, shards(): lax.psum_scatter(grad_second_w, ('dp', 'blk'), scatter_dimension=0, tiled...  360 us
    reduce_scatter x1, waiting for transfers between devices, shards(): lax.psum_scatter(grad_first_w, ('dp', 'blk'), scatter_dimension=0, tiled=...  358 us
    reduce_scatter x1, waiting for transfers between devices, shards(): lax.psum_scatter(grad_cross, ('dp', 'blk'), scatter_dimension=1, tiled=True)  273 us
    unnamed x20, waiting for transfers between devices  252 us
    reduce_scatter x1, waiting for transfers between devices, shards(): lax.psum_scatter(grad_self_out, ('dp', 'blk'), scatter_dimension=0, tiled...  145 us
    reduce_scatter x1, waiting for transfers between devices, shards(): lax.psum_scatter(grad_cross_out, ('dp', 'blk'), scatter_dimension=0, tile...  143 us
    reduce_scatter x1, waiting for transfers between devices, shards(): lax.psum_scatter(key_value_terms(cross_score_all, cross_prob_all, cross_q...  68.1 us
    dot_general x10, matrix products, matmul_t(): jnp.einsum('...j,ij->...i', left_side, right_side, preferred_element_type...  61.3 us
  transfers between devices with their start and end apart: 18, of which 16 were waited for; matrix products, arithmetic and copies ran while one was open for 18% of the time, Pallas kernels for 0%

commit v1 on v0

v1 whole, which is shorter than its diff:
```python
from functools import partial
import math
import jax
import jax.numpy as jnp
from jax import lax
from jax.experimental import pallas as pl
from jax.experimental.pallas import tpu as pltpu
from jax.sharding import PartitionSpec as P

bucket_edges = tuple((math.ceil(16 * 8 ** (power / 16)) for power in range(1, 16)))
score_unit = 0.125 * math.log2(math.e)
masked_out = -1e30


def fold_rows(values_in, combine):
    return combine(values_in.reshape(values_in.shape[0] // 8, 8, values_in.shape[1]), axis=0)


def two_heads(tile, half):
    wide = tile.astype(jnp.float32)
    low_lanes = lax.broadcasted_iota(jnp.int32, wide.shape, 1) < half
    tall = jnp.concatenate([jnp.where(low_lanes, wide, 0.0), jnp.where(low_lanes, 0.0, wide)], axis=0)
    return tall.astype(jnp.bfloat16)


def turned_twice(tile):
    return jnp.concatenate([tile.astype(jnp.float32)] * 2, axis=0).T


def join_heads(tall, half):
    rows = tall.shape[0] // 2
    low_lanes = lax.broadcasted_iota(jnp.int32, (rows, tall.shape[1]), 1) < half
    return jnp.where(low_lanes, tall[:rows], tall[rows:])


def dot_00(left_side, right_side):
    return lax.dot_general(left_side, right_side, (((0,), (0,)), ((), ())), preferred_element_type=jnp.float32)


def dot_10(left_side, right_side):
    return lax.dot_general(left_side, right_side, (((1,), (0,)), ((), ())), preferred_element_type=jnp.float32)


def slot_of(place, block, blocks):
    gap = place ^ block
    return (gap >> 1) + (blocks // 2) * (gap & 1)


def tile_of(bounds_ref, stream, block, near_tiles):
    first, place = bounds_ref[stream, 0], bounds_ref[stream, 1]
    gap = place - block
    outside = (block < first) | (gap < 0)
    plain = jnp.where(outside, near_tiles + 2, jnp.minimum(gap, near_tiles) + 1)
    return jnp.where(gap == 0, 0, plain), plain


def shift_of(bounds_ref, stream, block):
    inside = (block >= bounds_ref[stream, 0]) & (block <= bounds_ref[stream, 1])
    return jnp.where(inside, 0.0, masked_out)


def forward_kernel(is_self, rows, near_tiles, *refs):
    if is_self:
        bounds_ref, q_ref, k_ref, v_ref, ko_ref, vo_ref, bias_ref, own_bias_ref, o_ref, lse_ref, score_ref, total_ref = refs
    else:
        bounds_ref, q_ref, k_ref, v_ref, o_ref, lse_ref, score_ref, total_ref = refs
    stream = pl.program_id(1)
    half = q_ref.shape[3] // 2
    wide = 2 * rows
    first_chunk = bounds_ref[stream, 0] // 2
    past_chunk = bounds_ref[stream, 1] // 2 + 1
    place, blocks = bounds_ref[stream, 2], k_ref.shape[0]
    q_turned = [two_heads(q_ref[0, c], half).T for c in range(3)]

    def score_step(chunk, tops):
        tops = list(tops)
        for part in range(2):
            block = 2 * chunk + part
            key_rows = pl.ds(pl.multiple_of(block * rows, rows), rows)
            keys = k_ref[slot_of(place, block, blocks), 0]
            if is_self:
                diag_tile, plain_tile = tile_of(bounds_ref, stream, block, near_tiles)
                later_tile = jnp.where(diag_tile == 0, 1, plain_tile)
                tile_index = (jnp.where(diag_tile == 0, 0, plain_tile), later_tile, later_tile)
            for c in range(3):
                scores = dot_10(keys, q_turned[c])
                if is_self:
                    scores = scores + bias_ref[0, tile_index[c]]
                else:
                    scores = scores + shift_of(bounds_ref, stream, block)
                score_ref[key_rows, pl.ds(c * wide, wide)] = scores
                tops[c] = jnp.maximum(tops[c], fold_rows(scores, jnp.max))
        return tuple(tops)

    tops = lax.fori_loop(
        first_chunk, past_chunk, score_step, tuple((jnp.full((8, wide), masked_out, jnp.float32) for _ in range(3)))
    )
    row_top = [jnp.max(tops[c], axis=0, keepdims=True) for c in range(3)]
    if is_self:
        own_turned = [None] + [turned_twice(ko_ref[0, c]) for c in range(2)]
        own_score = [None] + [
            jnp.sum(q_turned[c].astype(jnp.float32) * own_turned[c], axis=0, keepdims=True)
            + own_bias_ref[0]
            for c in (1, 2)
        ]
        row_top = [row_top[0]] + [jnp.maximum(row_top[c], own_score[c]) for c in (1, 2)]
    total_ref[...] = jnp.zeros_like(total_ref)

    def value_step(chunk, sums):
        sums = list(sums)
        chunk_rows = pl.ds(pl.multiple_of(chunk * wide, wide), wide)
        values = jnp.concatenate(
            [v_ref[slot_of(place, 2 * chunk + part, blocks), 0] for part in range(2)], axis=0
        )
        for c in range(3):
            lanes = pl.ds(c * wide, wide)
            weights = jnp.exp2((score_ref[chunk_rows, lanes] - row_top[c]) * score_unit)
            sums[c] = sums[c] + fold_rows(weights, jnp.sum)
            total_ref[:, lanes] += dot_00(values, weights.astype(jnp.bfloat16))
        return tuple(sums)

    sums = lax.fori_loop(
        first_chunk, past_chunk, value_step, tuple((jnp.zeros((8, wide), jnp.float32) for _ in range(3)))
    )
    for c in range(3):
        row_sum = jnp.sum(sums[c], axis=0, keepdims=True)
        mixed = total_ref[:, c * wide : (c + 1) * wide]
        if is_self and c > 0:
            own_weight = jnp.exp2((own_score[c] - row_top[c]) * score_unit)
            row_sum = row_sum + own_weight
            value_turned = turned_twice(vo_ref[0, c - 1])
            mixed = mixed + own_weight * value_turned
        mixed = mixed / row_sum
        o_ref[0, c] = join_heads(mixed.T, half).astype(jnp.bfloat16)
        lse_ref[0, 0, :, c * wide : (c + 1) * wide] = row_top[c] * score_unit + jnp.log2(row_sum)


def backward_kernel(is_self, rows, near_tiles, *refs):
    if is_self:
        (bounds_ref, q_ref, k_ref, v_ref, o_ref, do_ref, lse_ref, ko_ref, vo_ref, bias_ref, own_bias_ref,
         dq_ref, dk_ref, dv_ref, dko_ref, dvo_ref, tiles_ref, own_sum_ref, prob_ref, grad_ref, total_ref) = refs
    else:
        (bounds_ref, q_ref, k_ref, v_ref, o_ref, do_ref, lse_ref,
         dq_ref, dk_ref, dv_ref, prob_ref, grad_ref, total_ref) = refs
    stream = pl.program_id(1)
    half = q_ref.shape[3] // 2
    wide = 2 * rows
    first_chunk = bounds_ref[stream, 0] // 2
    past_chunk = bounds_ref[stream, 1] // 2 + 1
    place, blocks = bounds_ref[stream, 2], k_ref.shape[0]
    chunk_count = blocks // 2
    q_tall = [two_heads(q_ref[0, c], half) for c in range(3)]
    do_tall = [two_heads(do_ref[0, c], half) for c in range(3)]
    q_turned = [tall.T for tall in q_tall]
    do_turned = [tall.T for tall in do_tall]
    lse = [lse_ref[0, 0, :, c * wide : (c + 1) * wide] for c in range(3)]
    centre = []
    for c in range(3):
        o_turned = turned_twice(o_ref[0, c])
        centre.append(jnp.sum(do_turned[c].astype(jnp.float32) * o_turned, axis=0, keepdims=True))
    q_all = jnp.concatenate(q_tall, axis=0)
    do_all = jnp.concatenate(do_tall, axis=0)
    total_ref[...] = jnp.zeros_like(total_ref)

    if is_self:

        @pl.when(stream == 0)
        def _():
            tiles_ref[...] = jnp.zeros_like(tiles_ref)
            own_sum_ref[...] = jnp.zeros_like(own_sum_ref)

    def blank_step(chunk, carry):
        for part in range(2):
            slot = slot_of(place, 2 * chunk + part, blocks)
            dk_ref[slot, 0] = jnp.zeros((rows, 2 * half), jnp.bfloat16)
            dv_ref[slot, 0] = jnp.zeros((rows, 2 * half), jnp.bfloat16)
        return carry

    lax.fori_loop(0, first_chunk, blank_step, 0)
    lax.fori_loop(past_chunk, chunk_count, blank_step, 0)

    def chunk_step(chunk, carry):
        for part in range(2):
            block = 2 * chunk + part
            part_rows = pl.ds(part * rows, rows)
            keys = k_ref[slot_of(place, block, blocks), 0]
            values = v_ref[slot_of(place, block, blocks), 0]
            if is_self:
                diag_tile, plain_tile = tile_of(bounds_ref, stream, block, near_tiles)
                later_tile = jnp.where(diag_tile == 0, 1, plain_tile)
                tile_index = (jnp.where(diag_tile == 0, 0, plain_tile), later_tile, later_tile)
            grad_sum = None
            for c in range(3):
                lanes = pl.ds(c * wide, wide)
                scores = dot_10(keys, q_turned[c])
                if is_self:
                    scores = scores + bias_ref[0, tile_index[c]]
                else:
                    scores = scores + shift_of(bounds_ref, stream, block)
                probs = jnp.exp2(scores * score_unit - lse[c])
                prob_ref[part_rows, lanes] = probs.astype(jnp.bfloat16)
                grads = probs * (dot_10(values, do_turned[c]) - centre[c])
                grad_ref[part_rows, lanes] = grads.astype(jnp.bfloat16)
                if is_self:
                    grad_sum = grads if grad_sum is None else grad_sum + grads
            if is_self:
                tiles_ref[0, tile_index[1]] += grad_sum
        slots = [slot_of(place, 2 * chunk + part, blocks) for part in range(2)]
        value_grads = dot_10(prob_ref[...], do_all).astype(jnp.bfloat16)
        key_grads = (0.125 * dot_10(grad_ref[...], q_all)).astype(jnp.bfloat16)
        for part in range(2):
            dv_ref[slots[part], 0] = value_grads[part * rows : (part + 1) * rows]
            dk_ref[slots[part], 0] = key_grads[part * rows : (part + 1) * rows]
        total_ref[...] += dot_00(jnp.concatenate([k_ref[slot, 0] for slot in slots], axis=0), grad_ref[...])
        return carry

    lax.fori_loop(first_chunk, past_chunk, chunk_step, 0)
    for c in range(3):
        turned = total_ref[:, c * wide : (c + 1) * wide]
        if is_self and c > 0:
            own_turned = turned_twice(ko_ref[0, c - 1])
            value_turned = turned_twice(vo_ref[0, c - 1])
            q_wide = q_turned[c].astype(jnp.float32)
            do_wide = do_turned[c].astype(jnp.float32)
            own_score = jnp.sum(q_wide * own_turned, axis=0, keepdims=True) + own_bias_ref[0]
            own_prob = jnp.exp2(own_score * score_unit - lse[c])
            own_dp = jnp.sum(do_wide * value_turned, axis=0, keepdims=True)
            own_grad = own_prob * (own_dp - centre[c])
            own_sum_ref[0] += own_grad
            own_grad = own_grad.astype(jnp.bfloat16).astype(jnp.float32)
            own_low = own_prob.astype(jnp.bfloat16).astype(jnp.float32)
            turned = turned + own_grad * own_turned
            dko = (0.125 * own_grad * q_wide).T
            dko_ref[0, c - 1] = (dko[:rows] + dko[rows:]).astype(jnp.bfloat16)
            dvo = (own_low * do_wide).T
            dvo_ref[0, c - 1] = (dvo[:rows] + dvo[rows:]).astype(jnp.bfloat16)
        dq_ref[0, c] = (0.125 * join_heads(turned.T, half)).astype(jnp.bfloat16)


def attend_forward(bounds, query, keys, values, own=None, near_tiles=0, head_size=64):
    streams, _, rows, width = query.shape
    blocks = keys.shape[0]
    length = blocks * rows
    lanes = 2 * head_size
    pairs = width // lanes
    is_self = own is not None
    row_spec = pl.BlockSpec((1, 3, rows, lanes), lambda p, n, s: (n, 0, 0, p))
    key_spec = pl.BlockSpec((blocks, 1, rows, lanes), lambda p, n, s: (0, n, 0, p))
    in_specs = [row_spec, key_spec, key_spec]
    args = [query, keys, values]
    if is_self:
        own_keys, own_values, tiles, own_bias = own
        own_spec = pl.BlockSpec((1, 2, rows, lanes), lambda p, n, s: (n, 0, 0, p))
        in_specs += [
            own_spec,
            own_spec,
            pl.BlockSpec((1,) + tiles.shape[1:], lambda p, n, s: (p, 0, 0, 0)),
            pl.BlockSpec((1, 1, 2 * rows), lambda p, n, s: (p, 0, 0)),
        ]
        args += [own_keys, own_values, tiles, own_bias]
    flops = 2 * 2 * streams * 3 * rows * length * width
    return pl.pallas_call(
        partial(forward_kernel, is_self, rows, near_tiles),
        grid_spec=pltpu.PrefetchScalarGridSpec(
            num_scalar_prefetch=1,
            grid=(pairs, streams),
            in_specs=in_specs,
            out_specs=[row_spec, pl.BlockSpec((1, 1, 1, 6 * rows), lambda p, n, s: (p, n, 0, 0))],
            scratch_shapes=[
                pltpu.VMEM((length, 6 * rows), jnp.float32),
                pltpu.VMEM((lanes, 6 * rows), jnp.float32),
            ],
        ),
        out_shape=[
            jax.ShapeDtypeStruct(query.shape, jnp.bfloat16),
            jax.ShapeDtypeStruct((pairs, streams, 1, 6 * rows), jnp.float32),
        ],
        compiler_params=pltpu.CompilerParams(vmem_limit_bytes=20 * 1024 * 1024),
        cost_estimate=pl.CostEstimate(flops=4 * flops, bytes_accessed=20_000_000, transcendentals=0),
    )(bounds, *args)


def attend_backward(bounds, query, keys, values, mixed, mix_grad, lse, own=None, near_tiles=0, head_size=64):
    streams, _, rows, width = query.shape
    blocks = keys.shape[0]
    length = blocks * rows
    lanes = 2 * head_size
    pairs = width // lanes
    is_self = own is not None
    row_spec = pl.BlockSpec((1, 3, rows, lanes), lambda p, n, s: (n, 0, 0, p))
    key_spec = pl.BlockSpec((blocks, 1, rows, lanes), lambda p, n, s: (0, n, 0, p))
    in_specs = [row_spec, key_spec, key_spec, row_spec, row_spec,
                pl.BlockSpec((1, 1, 1, 6 * rows), lambda p, n, s: (p, n, 0, 0))]
    args = [query, keys, values, mixed, mix_grad, lse]
    out_specs = [row_spec, key_spec, key_spec]
    out_shape = [jax.ShapeDtypeStruct(query.shape, jnp.bfloat16)] + [jax.ShapeDtypeStruct(keys.shape, jnp.bfloat16)] * 2
    if is_self:
        own_keys, own_values, tiles, own_bias = own
        own_spec = pl.BlockSpec((1, 2, rows, lanes), lambda p, n, s: (n, 0, 0, p))
        tile_spec = pl.BlockSpec((1,) + tiles.shape[1:], lambda p, n, s: (p, 0, 0, 0))
        own_bias_spec = pl.BlockSpec((1, 1, 2 * rows), lambda p, n, s: (p, 0, 0))
        in_specs += [own_spec, own_spec, tile_spec, own_bias_spec]
        args += [own_keys, own_values, tiles, own_bias]
        out_specs += [own_spec, own_spec, tile_spec, own_bias_spec]
        out_shape += [jax.ShapeDtypeStruct(own_keys.shape, jnp.bfloat16)] * 2
        out_shape += [jax.ShapeDtypeStruct(tiles.shape, jnp.float32), jax.ShapeDtypeStruct(own_bias.shape, jnp.float32)]
    flops = 5 * 2 * streams * 3 * rows * length * width
    return pl.pallas_call(
        partial(backward_kernel, is_self, rows, near_tiles),
        grid_spec=pltpu.PrefetchScalarGridSpec(
            num_scalar_prefetch=1,
            grid=(pairs, streams),
            in_specs=in_specs,
            out_specs=out_specs,
            scratch_shapes=[
                pltpu.VMEM((2 * rows, 6 * rows), jnp.bfloat16),
                pltpu.VMEM((2 * rows, 6 * rows), jnp.bfloat16),
                pltpu.VMEM((lanes, 6 * rows), jnp.float32),
            ],
        ),
        out_shape=out_shape,
        compiler_params=pltpu.CompilerParams(vmem_limit_bytes=20 * 1024 * 1024),
        cost_estimate=pl.CostEstimate(flops=4 * flops, bytes_accessed=40_000_000, transcendentals=0),
    )(bounds, *args)


def bucket_of(distance):
    nearby = jnp.maximum(distance, 0)
    distant = 16 + sum(((nearby >= edge).astype(jnp.int32) for edge in bucket_edges))
    return jnp.where(nearby < 16, nearby, distant)


def near_count(rows):
    gap = 1
    while rows * gap - (rows - 1) < bucket_edges[-1]:
        gap += 1
    return gap


def bias_tiles(rel_table, rows):
    heads, buckets = rel_table.shape
    near_tiles = near_count(rows)
    places = jnp.arange(rows, dtype=jnp.int32)
    distance = places[None, None, :] - places[None, :, None] + rows * jnp.arange(near_tiles, dtype=jnp.int32)[:, None, None]
    onehot = (bucket_of(distance)[..., None] == jnp.arange(buckets, dtype=jnp.int32)).astype(jnp.float32)
    shifted = 8.0 * (rel_table - rel_table[:, buckets - 1 :])
    gap = jnp.tile(places[None, :] - places[:, None], (1, 2))[None, None]
    near = jnp.concatenate(
        [
            jnp.einsum("dstk,pk->pdst", onehot, shifted[side::2], precision=lax.Precision.HIGHEST)
            for side in range(2)
        ],
        axis=-1,
    )
    diag = near[:, :1]
    tiles = jnp.concatenate(
        [
            jnp.where(gap >= 0, diag, masked_out),
            jnp.where(gap > 0, diag, masked_out),
            near[:, 1:],
            jnp.zeros_like(diag),
            jnp.full_like(diag, masked_out),
        ],
        axis=1,
    )
    own_bias = jnp.repeat(shifted[:, 0], rows).reshape(heads // 2, 1, 2 * rows)
    return tiles, own_bias, onehot


def table_grad(tile_grads, own_sums, onehot, bucket_count):
    pairs, tile_count, rows, wide = tile_grads.shape
    near_tiles = tile_count - 3
    sides = (tile_grads[..., : wide // 2], tile_grads[..., wide // 2 :])
    near_part, far_part = (
        jnp.stack(parts, axis=1)
        for parts in zip(
            *(
                (
                    jnp.einsum(
                        "pdst,dstk->pk", side[:, 1 : 1 + near_tiles], onehot, precision=lax.Precision.HIGHEST
                    ),
                    jnp.sum(side[:, 1 + near_tiles], axis=(1, 2)),
                )
                for side in sides
            )
        )
    )
    own_part = jnp.sum(own_sums.reshape(pairs, 2, wide // 2), axis=-1)
    buckets = jnp.arange(bucket_count)
    result = near_part + far_part[..., None] * (buckets == bucket_count - 1) + own_part[..., None] * (buckets == 0)
    return result.reshape(2 * pairs, bucket_count)


def norm_parts(values_in):
    centred = values_in - jnp.mean(values_in, axis=-1, keepdims=True)
    inv_scale = lax.rsqrt(jnp.mean(centred * centred, axis=-1, keepdims=True) + 1e-05)
    return (centred * inv_scale, inv_scale)


def norm_back(grad_in, normed, inv_scale, gain_row):
    scaled = grad_in * gain_row
    return inv_scale * (
        scaled
        - jnp.mean(scaled, axis=-1, keepdims=True)
        - normed * jnp.mean(scaled * normed, axis=-1, keepdims=True)
    )


def matmul(left_side, right_side):
    return jnp.einsum("...i,ij->...j", left_side, right_side, preferred_element_type=jnp.float32)


def matmul_t(left_side, right_side):
    return jnp.einsum("...j,ij->...i", left_side, right_side, preferred_element_type=jnp.float32)


def swap_core(values_in):
    size = lax.axis_size("dp")
    return lax.ppermute(values_in, "dp", [(i, i ^ 1) for i in range(size)])


def swap_chip(values_in):
    size = lax.axis_size("dp")
    return lax.ppermute(values_in, "dp", [(i, i ^ 2) for i in range(size)])


def swap_block(values_in, bit):
    size = lax.axis_size("blk")
    return lax.ppermute(values_in, "blk", [(i, i ^ bit) for i in range(size)])


def tie(value, *earlier):
    return lax.optimization_barrier((value,) + earlier)[0]


def assemble(pieces):
    count = pieces[0].shape[0]
    place = lax.axis_index("dp")
    split_rows = len(pieces) > 4

    def ordered(at, row):
        def joined(*parts):
            shards = [[parts[0]], [parts[1]]]
            if split_rows:
                halves = (parts[2:4], parts[4:6])
                shards += [[half[row], half[1 - row]] for half in halves]
            else:
                shards += [[parts[2]], [parts[3]]]
            return [
                jnp.concatenate([part[k] for index in range(4) for part in shards[at ^ index]], axis=0)
                for k in range(count)
            ]

        return joined

    if split_rows:
        row = lax.axis_index("blk") % 2
        return lax.switch(2 * place + row, [ordered(at, r) for at in range(4) for r in range(2)], *pieces)
    return lax.switch(place, [ordered(at, 0) for at in range(4)], *pieces)


def half_rows(shard):
    rows = shard.shape[1] // 2
    return lax.dynamic_slice_in_dim(shard, (lax.axis_index("blk") % 2) * rows, rows, 1)


def outer_low(left_side, right_side):
    return jnp.einsum("ni,nj->ij", left_side, right_side, preferred_element_type=jnp.float32)


def pick(values_in, index, axis):
    return lax.dynamic_index_in_dim(values_in, index, axis, keepdims=False)


def add_low(kept, arrived):
    return (kept.astype(jnp.float32) + arrived.astype(jnp.float32)).astype(jnp.bfloat16)


def open_core(grads):
    core = lax.axis_index("dp") % 2
    blocks = lax.axis_size("blk")

    def split(core_at):
        return jnp.stack(
            [pick(g.reshape(2, 2, blocks, g.shape[0] // (4 * blocks), g.shape[1]), core_at, 1) for g in grads], axis=2
        )

    return split(1 - core), split(core)


def open_chip(values_in):
    chip = lax.axis_index("dp") // 2
    return pick(values_in, 1 - chip, 0), pick(values_in, chip, 0)


def open_block(values_in, axis, bit):
    shape = values_in.shape
    values_in = values_in.reshape(shape[:axis] + (shape[axis] // 2, 2) + shape[axis + 1 :])
    mine = (lax.axis_index("blk") // bit) % 2
    return pick(values_in, 1 - mine, axis + 1), pick(values_in, mine, axis + 1)


def start_rows(values_in):
    return [values_in] + [swap_block(values_in, gap) for gap in range(2, lax.axis_size("blk"), 2)]


def finish_rows(pieces):
    return jnp.stack(pieces + [swap_block(piece, 1) for piece in pieces])


def fold_odd(terms):
    half = terms.shape[0] // 2
    return terms[:half], swap_block(terms[half:], 1)


def fold_even(terms):
    return sum(
        [swap_block(terms[index], 2 * index).astype(jnp.float32) for index in range(1, terms.shape[0])],
        terms[0].astype(jnp.float32),
    )


def exchange_blocks(values_in):
    count = values_in.shape[0]
    mine = lax.axis_index("blk") // 2
    come = [swap_block(pick(values_in, mine ^ gap, 0), 2 * gap) for gap in range(1, count)]
    total = pick(values_in, mine, 0).astype(jnp.float32)
    for piece in come:
        total = total + piece.astype(jnp.float32)
    return total


def split_shares(share):
    share = share.astype(jnp.float32)
    return [share[k] for k in range(share.shape[0])]


def sum_everywhere(values_in):
    total = values_in + swap_core(values_in)
    total = total + swap_chip(total)
    total = total + swap_block(total, 1)
    blocks = lax.axis_size("blk")
    mine = lax.axis_index("blk") // 2
    come = jnp.stack([total] + [swap_block(total, 2 * gap) for gap in range(1, blocks // 2)])
    return sum(pick(come, mine ^ index, 0) for index in range(blocks // 2))


def shards(
    hidden,
    encoder,
    lengths,
    qkv_self,
    out_self,
    rel_table,
    qkv_cross,
    out_cross,
    ffn_in,
    ffn_out,
    norm_gain,
    norm_bias,
    cotangent,
):
    streams, _, rows, width = hidden.shape
    heads, buckets = rel_table.shape
    head_size = width // heads
    place = lax.axis_index("blk")
    main_rows = start_rows(hidden[:, 0])
    low = partial(lax.convert_element_type, new_dtype=jnp.bfloat16)
    qkv_low = low(qkv_self)
    middle_low = jnp.concatenate([low(out_self)[None], low(qkv_cross), low(out_cross)[None]])
    first_low_w, second_low_w = low(ffn_in)[None], low(ffn_out)[None]
    qkv_far = swap_chip(qkv_low)
    main_all = finish_rows(main_rows)
    w_qkv = assemble([qkv_low, swap_core(qkv_low), qkv_far, swap_core(qkv_far)])
    doc_ends = jnp.cumsum(lengths, axis=-1)
    begin = place * rows
    doc_begin = jnp.max(jnp.where(doc_ends <= begin, doc_ends, 0), axis=-1)
    doc_end = jnp.min(jnp.where(doc_ends > begin, doc_ends, rows * lax.axis_size("blk")), axis=-1)
    first_block = (doc_begin // rows).astype(jnp.int32)
    last_block = (doc_end // rows - 1).astype(jnp.int32)
    places = jnp.full_like(first_block, place)
    self_bounds = jnp.stack([first_block, places, places], axis=1)
    cross_bounds = jnp.stack([first_block, last_block, places], axis=1)
    near_tiles = near_count(rows)
    tiles, own_bias, onehot = bias_tiles(rel_table, rows)

    def flat(values_in):
        return values_in.reshape(-1, values_in.shape[-1])

    def tall(values_in):
        return values_in.reshape(streams, 3, rows, width)

    hidden_own = hidden[:, 1:]
    query = matmul(hidden, w_qkv[0]).astype(jnp.bfloat16)
    own_keys = matmul(hidden_own, w_qkv[1]).astype(jnp.bfloat16)
    own_values = matmul(hidden_own, w_qkv[2]).astype(jnp.bfloat16)
    middle_far = swap_chip(tie(middle_low, qkv_far))
    enc_all = finish_rows(start_rows(tie(encoder, main_all)))
    main_keys = matmul(main_all, w_qkv[1]).astype(jnp.bfloat16)
    main_values = matmul(main_all, w_qkv[2]).astype(jnp.bfloat16)
    own = (own_keys, own_values, tiles, own_bias)

    first_half_sent = half_rows(first_low_w)
    first_far = swap_chip(tie(first_half_sent, main_values, query))
    query = tie(query, first_half_sent)
    attended, self_lse = attend_forward(
        self_bounds, query, main_keys, main_values, own, near_tiles, head_size
    )
    second_half_sent = half_rows(second_low_w)
    second_far = swap_chip(tie(second_half_sent, attended, first_far))
    first_other = swap_block(tie(first_far, attended), 1)
    middle_pieces = [middle_low, swap_core(middle_low), middle_far, swap_core(tie(middle_far, attended))]
    w_out, *c_qkv, c_out = assemble(middle_pieces)
    first_norm, first_scale = norm_parts(
        flat(hidden).astype(jnp.float32) + matmul(flat(attended), w_out)
    )
    first_out = first_norm * norm_gain[0] + norm_bias[0]
    first_low = first_out.astype(jnp.bfloat16)
    cross_query = matmul(first_low, c_qkv[0]).astype(jnp.bfloat16)
    enc_keys = matmul(enc_all, c_qkv[1]).astype(jnp.bfloat16)
    enc_values = matmul(enc_all, c_qkv[2]).astype(jnp.bfloat16)
    cross_att, cross_lse = attend_forward(
        cross_bounds, tall(cross_query), enc_keys, enc_values, None, 0, head_size
    )
    second_other = swap_block(tie(second_far, cross_query), 1)
    w_first, w_second = (
        assemble(
            [shard, swap_core(shard), far, other, swap_core(far), swap_core(tie(other, cross_att))]
        )[0]
        for shard, far, other in (
            (first_low_w, first_far, first_other),
            (second_low_w, second_far, second_other),
        )
    )
    second_norm, second_scale = norm_parts(first_out + matmul(flat(cross_att), c_out))
    second_out = second_norm * norm_gain[1] + norm_bias[1]
    second_low = second_out.astype(jnp.bfloat16)
    inner_act = matmul(second_low, w_first)
    normal_cdf = 0.5 * (1.0 + lax.erf(inner_act * math.sqrt(0.5)))
    activated = (inner_act * normal_cdf).astype(jnp.bfloat16)
    density = jnp.exp(-0.5 * inner_act * inner_act) * (1.0 / math.sqrt(2.0 * math.pi))
    act_slope = (normal_cdf + inner_act * density).astype(jnp.bfloat16)
    third_norm, third_scale = norm_parts(second_out + matmul(activated, w_second))
    output = tall((third_norm * norm_gain[2] + norm_bias[2]).astype(jnp.bfloat16))

    grad_out = flat(cotangent).astype(jnp.float32)
    gain_three = jnp.sum(grad_out * third_norm, axis=0)
    bias_three = jnp.sum(grad_out, axis=0)
    third_grad = norm_back(grad_out, third_norm, third_scale, norm_gain[2])
    third_low = third_grad.astype(jnp.bfloat16)
    second_part = outer_low(activated, third_low).astype(jnp.bfloat16)
    second_sent, second_kept = open_core([second_part])
    second_come = swap_core(second_sent)
    inner_grad = (
        matmul_t(tie(third_low, second_sent), w_second) * act_slope.astype(jnp.float32)
    ).astype(jnp.bfloat16)
    chip_sent, chip_kept = open_chip(add_low(second_kept, second_come))
    chip_come = swap_chip(chip_sent)
    inner_grad = tie(inner_grad, chip_sent)
    first_part = outer_low(second_low, inner_grad).astype(jnp.bfloat16)
    first_sent, first_kept = open_core([first_part])
    first_come = swap_core(first_sent)
    second_total = third_grad + matmul_t(tie(inner_grad, first_sent), w_first)
    gain_two = jnp.sum(second_total * second_norm, axis=0)
    bias_two = jnp.sum(second_total, axis=0)
    second_grad = norm_back(second_total, second_norm, second_scale, norm_gain[1])
    cross_low = second_grad.astype(jnp.bfloat16)
    first_chip_sent, first_chip_kept = open_chip(add_low(first_kept, first_come))
    first_chip_come = swap_chip(first_chip_sent)
    cross_mix_grad = tall(matmul_t(tie(cross_low, first_chip_sent), c_out).astype(jnp.bfloat16))
    cross_query_grad, enc_key_grad, enc_value_grad = attend_backward(
        cross_bounds, tall(cross_query), enc_keys, enc_values, cross_att, cross_mix_grad, cross_lse,
        None, 0, head_size,
    )
    encoder_terms = (matmul_t(enc_key_grad, c_qkv[1]) + matmul_t(enc_value_grad, c_qkv[2])).astype(jnp.bfloat16)
    encoder_kept, encoder_come = fold_odd(encoder_terms)
    second_row_sent, second_row_kept = open_block(add_low(chip_kept, tie(chip_come, encoder_terms)), 0, 1)
    second_row_come = swap_block(second_row_sent, 1)
    first_row_sent, first_row_kept = open_block(add_low(first_chip_kept, tie(first_chip_come, second_row_sent)), 0, 1)
    first_row_come = swap_block(first_row_sent, 1)
    first_total = second_grad + matmul_t(flat(tie(cross_query_grad, first_row_sent)), c_qkv[0])
    gain_one = jnp.sum(first_total * first_norm, axis=0)
    bias_one = jnp.sum(first_total, axis=0)
    first_grad = norm_back(first_total, first_norm, first_scale, norm_gain[0])
    out_low = first_grad.astype(jnp.bfloat16)
    cross_parts = [
        outer_low(flat(left), flat(right)).astype(jnp.bfloat16)
        for left, right in (
            (cross_att, cross_low),
            (first_low, cross_query_grad),
            (enc_all, tie(enc_key_grad, out_low)),
            (enc_all, enc_value_grad),
            (attended, out_low),
        )
    ]
    cross_sent, cross_kept = open_core(cross_parts)
    cross_come = swap_core(cross_sent)
    mix_grad = tall(matmul_t(tie(out_low, cross_sent), w_out).astype(jnp.bfloat16))
    cross_chip_sent, cross_chip_kept = open_chip(add_low(cross_kept, tie(cross_come, mix_grad)))
    cross_chip_come = swap_chip(cross_chip_sent)
    second_half = add_low(second_row_kept, tie(second_row_come, mix_grad))
    first_half = add_low(first_row_kept, tie(first_row_come, mix_grad))
    g_second = exchange_blocks(second_half)[0]
    g_first = exchange_blocks(first_half)[0]
    encoder_half = add_low(encoder_kept, tie(encoder_come, second_half, first_half))
    d_encoder = fold_even(encoder_half)
    mix_grad = tie(mix_grad, cross_chip_sent, encoder_half)
    query_grad, key_grad, value_grad, own_key_grad, own_value_grad, tile_grads, own_sums = attend_backward(
        self_bounds, query, main_keys, main_values, attended, mix_grad, self_lse, own, near_tiles, head_size
    )
    main_terms = (matmul_t(key_grad, w_qkv[1]) + matmul_t(value_grad, w_qkv[2])).astype(jnp.bfloat16)
    main_kept, main_come = fold_odd(main_terms)
    cross_row_sent, cross_row_kept = open_block(add_low(cross_chip_kept, tie(cross_chip_come, main_terms)), 0, 1)
    cross_row_come = swap_block(cross_row_sent, 1)
    own_flat = flat(hidden_own)
    main_flat = flat(main_all)
    started = tie(query_grad, cross_row_sent)
    self_parts = [outer_low(flat(hidden), flat(started)).astype(jnp.bfloat16)] + [
        (outer_low(main_flat, flat(tie(grad, started))) + outer_low(own_flat, flat(own_grad))).astype(jnp.bfloat16)
        for grad, own_grad in ((key_grad, own_key_grad), (value_grad, own_value_grad))
    ]
    self_sent, self_kept = open_core(self_parts)
    self_come = swap_core(self_sent)
    local_grad = tall(first_grad) + matmul_t(tie(query_grad, self_sent), w_qkv[0])
    self_chip_sent, self_chip_kept = open_chip(add_low(self_kept, tie(self_come, local_grad)))
    self_chip_come = swap_chip(self_chip_sent)
    own_back = matmul_t(tie(own_key_grad, self_chip_sent), w_qkv[1]) + matmul_t(own_value_grad, w_qkv[2])
    main_half = add_low(main_kept, tie(main_come, own_back))
    main_back = fold_even(main_half)
    cross_share = exchange_blocks(add_low(cross_row_kept, tie(cross_row_come, own_back)))
    g_cross_out, *g_cross, g_self_out = split_shares(cross_share)
    g_cross = jnp.stack(g_cross)
    self_row_sent, self_row_kept = open_block(add_low(self_chip_kept, self_chip_come), 0, 1)
    self_row_come = swap_block(self_row_sent, 1)
    g_qkv = exchange_blocks(add_low(self_row_kept, self_row_come))
    d_hidden = local_grad + jnp.concatenate([main_back[:, None], own_back], axis=1)
    rel_grad = table_grad(tile_grads, own_sums, onehot, buckets)
    small = jnp.concatenate(
        [
            jnp.stack([gain_one, gain_two, gain_three, bias_one, bias_two, bias_three]),
            rel_grad.reshape(-1, width) if rel_grad.size % width == 0 else
            jnp.pad(rel_grad.reshape(1, -1), ((0, 0), (0, width - rel_grad.size))),
        ]
    )
    small = sum_everywhere(small)
    return (
        output,
        d_hidden,
        d_encoder,
        g_qkv,
        g_self_out,
        small[6:].reshape(-1)[: heads * buckets].reshape(heads, buckets),
        g_cross,
        g_cross_out,
        g_first,
        g_second,
        small[0:3],
        small[3:6],
    )


def solution(mesh):
    in_specs = (
        P("dp", None, "blk", None),
        P("dp", "blk", None),
        P("dp", None),
        P(None, "dp", None),
        P("dp", None),
        P(),
        P(None, "dp", None),
        P("dp", None),
        P("dp", None),
        P("dp", None),
        P(),
        P(),
        P("dp", None, "blk", None),
    )
    out_specs = (
        P("dp", None, "blk", None),
        P("dp", None, "blk", None),
        P("dp", "blk", None),
        P(None, ("dp", "blk"), None),
        P(("dp", "blk"), None),
        P(),
        P(None, ("dp", "blk"), None),
        P(("dp", "blk"), None),
        P(("dp", "blk"), None),
        P(("dp", "blk"), None),
        P(),
        P(),
    )
    return jax.shard_map(shards, mesh=mesh, in_specs=in_specs, out_specs=out_specs, check_vma=False)
```

time: 2820 us -> 1050 us (0.37)
  waiting for transfers between devices: 1870 us -> 329 us
  matrix products: 469 us -> 202 us
  other arithmetic: 240 us -> 91.7 us
  starting transfers between devices: 1.44 us -> 136 us
  Pallas kernels: 0 us -> 129 us
  blocking collectives: 41.4 us -> 0 us
  local copies, waits for them, and re-layouts: 170 us -> 133 us
    reduce_scatter x6 -> x0, waiting for transfers between devices: 1350 us -> none  [the longest x1 360 us: shards(): lax.psum_scatter(grad_second_w, ('dp', 'blk'), scatter_dimension=0, tiled...]
    ppermute x0 -> x68, waiting for transfers between devices: none -> 329 us  [the longest x44 308 us: swap_block(): return lax.ppermute(values_in, 'blk', [(i, i ^ bit) for i in range(size)])]
    dot_general x32 -> x16, matrix products: 339 us -> 57.6 us  [the longest x12 50.1 us: outer_low(): jnp.einsum('ni,nj->ij', left_side, right_side, preferred_element_type=jnp...]
    all_gather x10 -> x0, waiting for transfers between devices: 273 us -> none  [the longest x1 56.8 us: shards(): lax.all_gather(cross_kv[1], 'blk', axis=1, tiled=True)]
    unnamed x20 -> x0, waiting for transfers between devices: 252 us -> none
    ppermute x0 -> x68, starting transfers between devices: none -> 136 us  [the longest x44 127 us: swap_block(): return lax.ppermute(values_in, 'blk', [(i, i ^ bit) for i in range(size)])]
    pallas_call x0 -> x4, Pallas kernels: none -> 129 us  [the longest x2 76.9 us: attend_backward(): pl.pallas_call(partial(backward_kernel, is_self, rows, near_tiles), grid_...]
    convert_element_type x10 -> x23, other arithmetic: 122 us -> 58.3 us  [the longest x14 42.2 us: add_low(): (kept.astype(jnp.float32) + arrived.astype(jnp.float32)).astype(jnp.bfloa...]
  transfers between devices with their start and end apart: 18 -> 68, of which waited for: 16 -> 27; matrix products, arithmetic and copies ran while one was open for 18% -> 30% of each run, Pallas kernels for 0% -> 12%
where the time goes in v1:
time: 1050 us; the launch traced here: 1030 us
  waiting for transfers between devices  329 us (31%)
  matrix products  202 us (19%)
  starting transfers between devices  136 us (13%)
  local copies, waits for them, and re-layouts  133 us (13%)
  Pallas kernels  129 us (12%)
  other arithmetic  91.7 us (9%)
  loops' own time  10.5 us (1%)
    ppermute x44, waiting for transfers between devices, swap_block(): return lax.ppermute(values_in, 'blk', [(i, i ^ bit) for i in range(size)])  308 us
    ppermute x44, starting transfers between devices, swap_block(): return lax.ppermute(values_in, 'blk', [(i, i ^ bit) for i in range(size)])  127 us
    dot_general x12, matrix products, matmul_t(): jnp.einsum('...j,ij->...i', left_side, right_side, preferred_element_type...  79.1 us
    pallas_call x2, Pallas kernels, attend_backward(): pl.pallas_call(partial(backward_kernel, is_self, rows, near_tiles), grid_...  76.9 us
    dot_general x12, matrix products, matmul(): jnp.einsum('...i,ij->...j', left_side, right_side, preferred_element_type...  64.9 us
    unnamed x309, local copies, waits for them, and re-layouts  56.6 us
    pallas_call x2, Pallas kernels, attend_forward(): pl.pallas_call(partial(forward_kernel, is_self, rows, near_tiles), grid_s...  52.3 us
    dot_general x12, matrix products, outer_low(): jnp.einsum('ni,nj->ij', left_side, right_side, preferred_element_type=jnp...  50.1 us
  transfers between devices with their start and end apart: 68, of which 27 were waited for; matrix products, arithmetic and copies ran while one was open for 30% of the time, Pallas kernels for 12%

profile of v1, /device:TPU:0, one launch (start us, length us, event | category | flops | bytes accessed | tf_op | source)
XLA Modules:
  0.0 1034.1 jit_solution(4644354116681125244)
XLA Ops:
  42.7 5.9 collective-permute-done.1
  58.6 6.8 collective-permute-done.7
  66.3 10.4 %collective-permute-done.8 = bf16[2,128,1024]{2,1,0:T(8,128)(2,1)S(1)} collective-permute-done((bf16[2,128,1024]{2,1,0:T(8,128)(2,1)}, bf16[2,128,1024]{2,1,0:T(8,128)(2,1)S(1)}, u32[]{:S(2)}, u32[]{:S(2)}) %collective-permute-start.8) | collective-permute-done | bytes 524320 | tf_op jit(solution)/shard_map/ppermute | solution.py:429
  77.5 10.0 collective-permute-done.9
  101.1 6.9 convolution_convert_fusion.4.refs_3_
  117.4 19.2 %shard_map.220 = (bf16[2,3,128,1024]{3,2,1,0:T(8,128)(2,1)S(1)}, f32[8,2,1,768]{3,2,1,0:T(1,128)S(1)}) custom-call(s32[2,3]{1,0:T(2,128)S(1)} %get-tuple-element.778.refs_0_, bf16[2,3,128,1024]{3,2,1,0:T(8,128)(2,1)S(1)} %fusion.67.refs_1_, bf16[8,2,128,1024]{3,2,1,0:T(8,128)(2,1)S(1)} %convolution_convert_fusion.5.refs_2_, ...), custom_call_target="tpu_custom_call" | custom-call | flops 12884901888 | bytes 20000000 | tf_op jit(solution)/shard_map/pallas_call | solution.py:262
  136.6 10.5 %collective-permute-done.11 = bf16[5,256,1024]{2,1,0:T(8,128)(2,1)} collective-permute-done((bf16[5,256,1024]{2,1,0:T(8,128)(2,1)}, bf16[5,256,1024]{2,1,0:T(8,128)(2,1)}, u32[]{:S(2)}, u32[]{:S(2)}) %collective-permute-start.11) | collective-permute-done | bytes 2621472 | tf_op jit(solution)/shard_map/ppermute | solution.py:424
  150.6 9.7 collective-permute-start.14
  166.1 9.2 collective-permute-done.13
  176.9 19.0 %collective-permute-done.14 = bf16[2,128,1024]{2,1,0:T(8,128)(2,1)} collective-permute-done((bf16[2,128,1024]{2,1,0:T(8,128)(2,1)}, bf16[2,128,1024]{2,1,0:T(8,128)(2,1)}, u32[]{:S(2)}, u32[]{:S(2)}) %collective-permute-start.14) | collective-permute-done | bytes 524320 | tf_op jit(solution)/shard_map/ppermute | solution.py:429
  200.3 10.7 %collective-permute-done.17 = bf16[2,128,1024]{2,1,0:T(8,128)(2,1)S(1)} collective-permute-done((bf16[2,128,1024]{2,1,0:T(8,128)(2,1)}, bf16[2,128,1024]{2,1,0:T(8,128)(2,1)S(1)}, u32[]{:S(2)}, u32[]{:S(2)}) %collective-permute-start.17) | collective-permute-done | bytes 524320 | tf_op jit(solution)/shard_map/ppermute | solution.py:429
  211.6 7.8 collective-permute-done.18
  219.4 5.6 collective-permute-done.19
  227.0 16.9 %conditional.5 = (bf16[1024,1024]{1,0:T(8,128)(2,1)S(1)}, bf16[1024,1024]{1,0:T(8,128)(2,1)S(1)}, bf16[1024,1024]{1,0:T(8,128)(2,1)S(1)}, bf16[1024,1024]{1,0:T(8,128)(2,1)S(1)}, bf16[1024,1024]{1,0:T(8,128)(2,1)S(1)}) conditional(s32[]{:T(128)} %clamp.8, (bf16[5,256,1024]{2,1,0:T(8,128)(2,1)}, ...), branch_computations={%region_6.7_spmd, %region_7.8_spmd, %region_8.9_spmd, %region_9.10... | conditional | flops 41943040 | bytes 39845928 | solution.py:459
  250.8 6.5 convolution_convert_fusion.3.refs_2_
  264.0 33.1 %shard_map.221 = (bf16[2,3,128,1024]{3,2,1,0:T(8,128)(2,1)S(1)}, f32[8,2,1,768]{3,2,1,0:T(1,128)S(1)}) custom-call(s32[2,3]{1,0:T(2,128)S(1)} %get-tuple-element.777.refs_0_, bf16[2,3,128,1024]{3,2,1,0:T(8,128)(2,1)S(1)} %bitcast.861, bf16[8,2,128,1024]{3,2,1,0:T(8,128)(2,1)S(1)} %convolution_convert_fusion.3.refs_2_, ...), custom_call_target="tpu_custom_call" | custom-call | flops 12884901888 | bytes 20000000 | tf_op jit(solution)/shard_map/pallas_call | solution.py:262
  300.9 22.1 %collective-permute-done.27 = bf16[1,512,1024]{2,1,0:T(8,128)(2,1)} collective-permute-done((bf16[1,512,1024]{2,1,0:T(8,128)(2,1)S(1)}, bf16[1,512,1024]{2,1,0:T(8,128)(2,1)}, u32[]{:S(2)}, u32[]{:S(2)}) %collective-permute-start.27) | collective-permute-done | bytes 1048608 | tf_op jit(solution)/shard_map/ppermute | solution.py:429
  323.5 12.8 %conditional.6 = (bf16[1024,4096]{1,0:T(8,128)(2,1)}) conditional(s32[]{:T(128)} %clamp.9, (bf16[1,256,4096]{2,1,0:T(8,128)(2,1)}, bf16[1,128,4096]{2,1,0:T(8,128)(2,1)}, bf16[1,128,4096]{2,1,0:T(8,128)(2,1)}, bf16[1,128,4096]{2,1,0:T(8,128)(2,1)}, bf16[1,128,4096]{2,1,0:T(8,128)(2,1)S(1)}, ...), branch_computations={%region_15.16_spmd, %region_16.17_spmd, %region_17.18_spmd, %regio... | conditional | bytes 16777224 | solution.py:458
  336.4 15.0 %multiply_convert_fusion.1 = (bf16[768,4096]{1,0:T(8,128)(2,1)}, f32[768,4096]{1,0:T(8,128)}) fusion(bf16[1024,4096]{1,0:T(8,128)(2,1)} %get-tuple-element.825, f32[768,1024]{1,0:T(8,128)} %copy-done.50, f32[1024]{0:T(1024)S(1)} %bitcast.921, f32[1024]{0:T(1024)S(1)} %bitcast.910, f32[768]{0:T(1024)S(1)} %add_rsqrt_fusion.1, ...), kind=kOutput, calls=%fused_computation.255 | convolution fusion | flops 6462111744 | bytes 30423040 | tf_op jit(solution)/shard_map/...i,ij->...j/dot_general | solution.py:410
  351.4 12.9 %conditional.7 = (bf16[4096,1024]{1,0:T(8,128)(2,1)}) conditional(s32[]{:T(128)} %clamp.9, (bf16[1,1024,1024]{2,1,0:T(8,128)(2,1)}, bf16[1,512,1024]{2,1,0:T(8,128)(2,1)S(1)}, bf16[1,512,1024]{2,1,0:T(8,128)(2,1)}, bf16[1,512,1024]{2,1,0:T(8,128)(2,1)}, bf16[1,512,1024]{2,1,0:T(8,128)(2,1)}, ...), branch_computations={%region_23.24_spmd, %region_24.25_spmd, %region_25.26_spmd, %regio... | conditional | bytes 16777224 | solution.py:458
  364.3 11.7 %fusion.144 = (f32[768]{0:T(1024)S(1)}, f32[768,1024]{1,0:T(8,128)S(1)}) fusion(bf16[768,4096]{1,0:T(8,128)(2,1)} %get-tuple-element.783, bf16[4096,1024]{1,0:T(8,128)(2,1)} %get-tuple-element.826, f32[1024]{0:T(1024)S(1)} %bitcast.922, f32[1024]{0:T(1024)S(1)} %bitcast.911, f32[768]{0:T(1024)S(1)} %add_rsqrt_fusion.1, f32[768,1024]{1,0:T(8,128)} %copy-done.50, ...), kind=kOutput, calls=%fused_computation.558 | convolution fusion | flops 6447168512 | bytes 20988928 | tf_op jit(solution)/shard_map/...i,ij->...j/dot_general | solution.py:410
  382.2 7.1 convolution_convert_fusion.1
  393.8 14.2 %multiply_convert_fusion = bf16[768,4096]{1,0:T(8,128)(2,1)S(1)} fusion(bf16[768,1024]{1,0:T(8,128)(2,1)S(1)} %get-tuple-element.513, bf16[4096,1024]{1,0:T(8,128)(2,1)} %get-tuple-element.826, f32[768,4096]{1,0:T(8,128)} %get-tuple-element.784), kind=kOutput, calls=%fused_computation.254 | convolution fusion | flops 6480199680 | bytes 28835840 | tf_op jit(solution)/shard_map/...j,ij->...i/dot_general | solution.py:414
  408.1 6.6 fusion.6
  418.8 7.7 convolution_convert_fusion
  431.5 15.3 %multiply_reduce_fusion = (f32[1024]{0:T(1024)}, f32[768]{0:T(1024)S(1)}, f32[768]{0:T(1024)S(1)}, f32[1024]{0:T(1024)}, f32[768,1024]{1,0:T(8,128)}) fusion(f32[768,1024]{1,0:T(8,128)} %copy-done.50, f32[768]{0:T(1024)S(1)} %add_rsqrt_fusion.1, f32[768]{0:T(1024)S(1)} %broadcast_multiply_fusion.7, f32[1024]{0:T(1024)S(1)} %bitcast.913, ...), kind=kOutput, calls=%fused_computation.305 | convolution fusion | flops 6450311168 | bytes 24141824 | tf_op jit(solution)/shard_map/...j,ij->...i/dot_general | solution.py:414
  464.7 43.2 %shard_map.222 = (bf16[2,3,128,1024]{3,2,1,0:T(8,128)(2,1)S(1)}, bf16[8,2,128,1024]{3,2,1,0:T(8,128)(2,1)S(1)}, bf16[8,2,128,1024]{3,2,1,0:T(8,128)(2,1)S(1)}) custom-call(s32[2,3]{1,0:T(2,128)S(1)} %get-tuple-element.777.refs_0_, bf16[2,3,128,1024]{3,2,1,0:T(8,128)(2,1)S(1)} %bitcast.862, bf16[8,2,128,1024]{3,2,1,0:T(8,128)(2,1)S(1)} %copy-done.31, ...), custom_call_target="tpu_custom_call" | custom-call | flops 32212254720 | bytes 40000000 | tf_op jit(solution)/shard_map/pallas_call | solution.py:308
  508.0 7.1 fusion.44
  515.1 9.1 add_convert_fusion.2
  566.3 17.2 %collective-permute-done.36 = bf16[4,1,128,1024]{3,2,0,1:T(8,128)(2,1)} collective-permute-done((bf16[4,1,128,1024]{3,2,0,1:T(8,128)(2,1)S(1)}, bf16[4,1,128,1024]{3,2,0,1:T(8,128)(2,1)}, u32[]{:S(2)}, u32[]{:S(2)}) %collective-permute-start.36) | collective-permute-done | bytes 1048608 | tf_op jit(solution)/shard_map/ppermute | solution.py:429
  585.9 8.2 collective-permute-start.67
  594.1 7.3 collective-permute-done.67
  602.1 9.5 collective-permute-start.65
  623.4 27.1 %collective-permute-done.37 = bf16[4,1,32,4096]{3,2,0,1:T(8,128)(2,1)} collective-permute-done((bf16[4,1,32,4096]{3,2,0,1:T(8,128)(2,1)}, bf16[4,1,32,4096]{3,2,0,1:T(8,128)(2,1)}, u32[]{:S(2)}, u32[]{:S(2)}) %collective-permute-start.37) | collective-permute-done | bytes 1048608 | tf_op jit(solution)/shard_map/ppermute | solution.py:429
  653.8 7.7 collective-permute-start.64
  665.9 9.7 add_convert_fusion
  683.2 33.6 %shard_map.223 = (bf16[2,3,128,1024]{3,2,1,0:T(8,128)(2,1)S(1)}, bf16[8,2,128,1024]{3,2,1,0:T(8,128)(2,1)S(1)}, bf16[8,2,128,1024]{3,2,1,0:T(8,128)(2,1)S(1)}, b...) custom-call(s32[2,3]{1,0:T(2,128)S(1)} %copy-done.4, ...), custom_call_target="tpu_custom_call" | custom-call | flops 32212254720 | bytes 40000000 | tf_op jit(solution)/shard_map/pallas_call | solution.py:308
  732.5 7.1 fusion.35
  739.6 9.0 add_convert_fusion.1
  778.4 20.3 %collective-permute-start.46 = (bf16[2,128,1024]{2,1,0:T(8,128)(2,1)S(1)}, bf16[2,128,1024]{2,1,0:T(8,128)(2,1)S(1)}, u32[]{:S(2)}, u32[]{:S(2)}) collective-permute-start(bf16[2,128,1024]{2,1,0:T(8,128)(2,1)S(1)} %get-tuple-element.734), channel_id=1, source_target_pairs={{0,6},{1,7},{2,4},{3,5},{4,2},{5,3},{6,0},{7,1},{8,14},{9,15},{10,... | collective-permute-start | bytes 1572872 | tf_op jit(solution)/shard_map/ppermute | solution.py:429
  803.9 7.8 collective-permute-done.46
  811.6 26.0 %collective-permute-done.45 = bf16[2,128,1024]{2,1,0:T(8,128)(2,1)S(1)} collective-permute-done((bf16[2,128,1024]{2,1,0:T(8,128)(2,1)S(1)}, bf16[2,128,1024]{2,1,0:T(8,128)(2,1)S(1)}, u32[]{:S(2)}, u32[]{:S(2)}) %collective-permute-start.45) | collective-permute-done | bytes 524320 | tf_op jit(solution)/shard_map/ppermute | solution.py:429
  865.5 32.1 %collective-permute-done.39 = bf16[4,2,128,1024]{3,2,1,0:T(8,128)(2,1)} collective-permute-done((bf16[4,2,128,1024]{3,2,1,0:T(8,128)(2,1)}, bf16[4,2,128,1024]{3,2,1,0:T(8,128)(2,1)}, u32[]{:S(2)}, u32[]{:S(2)}) %collective-permute-start.39) | collective-permute-done | bytes 2097184 | tf_op jit(solution)/shard_map/ppermute | solution.py:429
  897.5 25.8 %collective-permute-done.52 = bf16[4,5,32,1024]{3,2,1,0:T(8,128)(2,1)} collective-permute-done((bf16[4,5,32,1024]{3,2,1,0:T(8,128)(2,1)}, bf16[4,5,32,1024]{3,2,1,0:T(8,128)(2,1)}, u32[]{:S(2)}, u32[]{:S(2)}) %collective-permute-start.52) | collective-permute-done | bytes 1310752 | tf_op jit(solution)/shard_map/ppermute | solution.py:429
  937.6 34.2 %collective-permute-start.41 = (bf16[2,128,1024]{2,1,0:T(8,128)(2,1)S(1)}, bf16[2,128,1024]{2,1,0:T(8,128)(2,1)S(1)}, u32[]{:S(2)}, u32[]{:S(2)}) collective-permute-start(bf16[2,128,1024]{2,1,0:T(8,128)(2,1)S(1)} %get-tuple-element.736), channel_id=1, source_target_pairs={{0,2},{1,3},{2,0},{3,1},{4,6},{5,7},{6,4},{7,5},{8,10},{9,11},{10,... | collective-permute-start | bytes 1572872 | tf_op jit(solution)/shard_map/ppermute | solution.py:429
  971.9 26.9 %collective-permute-done.54 = bf16[5,32,1024]{2,1,0:T(8,128)(2,1)S(1)} collective-permute-done((bf16[5,32,1024]{2,1,0:T(8,128)(2,1)S(1)}, bf16[5,32,1024]{2,1,0:T(8,128)(2,1)S(1)}, u32[]{:S(2)}, u32[]{:S(2)}) %collective-permute-start.54) | collective-permute-done | bytes 327712 | tf_op jit(solution)/shard_map/ppermute | solution.py:429
  1001.4 15.0 %collective-permute-done.48 = bf16[4,3,32,1024]{3,2,1,0:T(8,128)(2,1)S(1)} collective-permute-done((bf16[4,3,32,1024]{3,2,1,0:T(8,128)(2,1)S(1)}, bf16[4,3,32,1024]{3,2,1,0:T(8,128)(2,1)S(1)}, u32[]{:S(2)}, u32[]{:S(2)}) %collective-permute-start.48) | collective-permute-done | bytes 786464 | tf_op jit(solution)/shard_map/ppermute | solution.py:429
  1026.4 6.6 collective-permute-done.50
  (606 shorter events, 363.4 us)
Async XLA Ops:
  2.5 40.2 %collective-permute-start.3 = (bf16[2,128,1024]{2,1,0:T(8,128)(2,1)}, bf16[2,128,1024]{2,1,0:T(8,128)(2,1)}, u32[]{:S(2)}, u32[]{:S(2)}) collective-permute-start(bf16[2,128,1024]{2,1,0:T(8,128)(2,1)} %slice_bitcast_fusion.128), channel_id=1, source_target_pairs={{0,2},{1,3},{2,0},{3,1},{4,6},{5,7},{6,4},{7,5},{8,10},{9,11},{10,... | collective-permute-start | bytes 1572872 | tf_op jit(solution)/shard_map/ppermute | solution.py:429
  5.6 44.9 %collective-permute-start.4 = (bf16[2,128,1024]{2,1,0:T(8,128)(2,1)}, bf16[2,128,1024]{2,1,0:T(8,128)(2,1)}, u32[]{:S(2)}, u32[]{:S(2)}) collective-permute-start(bf16[2,128,1024]{2,1,0:T(8,128)(2,1)} %slice_bitcast_fusion.128), channel_id=1, source_target_pairs={{0,4},{1,5},{2,6},{3,7},{4,0},{5,1},{6,2},{7,3},{8,12},{9,13},{10,... | collective-permute-start | bytes 1572872 | tf_op jit(solution)/shard_map/ppermute | solution.py:429
  8.1 44.7 %collective-permute-start.5 = (bf16[2,128,1024]{2,1,0:T(8,128)(2,1)}, bf16[2,128,1024]{2,1,0:T(8,128)(2,1)}, u32[]{:S(2)}, u32[]{:S(2)}) collective-permute-start(bf16[2,128,1024]{2,1,0:T(8,128)(2,1)} %slice_bitcast_fusion.128), channel_id=1, source_target_pairs={{0,6},{1,7},{2,4},{3,5},{4,2},{5,3},{6,0},{7,1},{8,14},{9,15},{10,... | collective-permute-start | bytes 1572872 | tf_op jit(solution)/shard_map/ppermute | solution.py:429
  8.1 48.1 %collective-permute-start.6 = (bf16[2,128,1024]{2,1,0:T(8,128)(2,1)}, bf16[2,128,1024]{2,1,0:T(8,128)(2,1)}, u32[]{:S(2)}, u32[]{:S(2)}) collective-permute-start(bf16[2,128,1024]{2,1,0:T(8,128)(2,1)} %slice_bitcast_fusion.128), channel_id=1, source_target_pairs={{0,1},{1,0},{2,3},{3,2},{4,5},{5,4},{6,7},{7,6},{8,9},{9,8},{10,11... | collective-permute-start | bytes 1572872 | tf_op jit(solution)/shard_map/ppermute | solution.py:429
  13.2 35.4 %collective-permute-start.1 = (bf16[3,256,1024]{2,1,0:T(8,128)(2,1)}, bf16[3,256,1024]{2,1,0:T(8,128)(2,1)}, u32[]{:S(2)}, u32[]{:S(2)}) collective-permute-start(bf16[3,256,1024]{2,1,0:T(8,128)(2,1)} %convert_element_type.664), channel_id=1, source_target_pairs={{0,16},{8,24},{16,0},{24,8},{1,17},{9,25},{17,1},{25,9},{2,18},{10... | collective-permute-start | bytes 4718600 | tf_op jit(solution)/shard_map/ppermute | solution.py:424
  42.7 47.1 %collective-permute-start = (bf16[3,256,1024]{2,1,0:T(8,128)(2,1)}, bf16[3,256,1024]{2,1,0:T(8,128)(2,1)S(1)}, u32[]{:S(2)}, u32[]{:S(2)}) collective-permute-start(bf16[3,256,1024]{2,1,0:T(8,128)(2,1)} %convert_element_type.664), channel_id=1, source_target_pairs={{0,8},{8,0},{16,24},{24,16},{1,9},{9,1},{17,25},{25,17},{2,10},{10... | collective-permute-start | bytes 4718600 | tf_op jit(solution)/shard_map/ppermute | solution.py:419
  48.6 41.2 %collective-permute-start.2 = (bf16[3,256,1024]{2,1,0:T(8,128)(2,1)}, bf16[3,256,1024]{2,1,0:T(8,128)(2,1)S(1)}, u32[]{:S(2)}, u32[]{:S(2)}) collective-permute-start(bf16[3,256,1024]{2,1,0:T(8,128)(2,1)} %collective-permute-done.1), channel_id=1, source_target_pairs={{0,8},{8,0},{16,24},{24,16},{1,9},{9,1},{17,25},{25,17},{2,10},{10... | collective-permute-start | bytes 4718600 | tf_op jit(solution)/shard_map/ppermute | solution.py:419
  56.3 31.2 %collective-permute-start.9 = (bf16[2,128,1024]{2,1,0:T(8,128)(2,1)}, bf16[2,128,1024]{2,1,0:T(8,128)(2,1)S(1)}, u32[]{:S(2)}, u32[]{:S(2)}) collective-permute-start(bf16[2,128,1024]{2,1,0:T(8,128)(2,1)} %collective-permute-done.5), channel_id=1, source_target_pairs={{0,1},{1,0},{2,3},{3,2},{4,5},{5,4},{6,7},{7,6},{8,9},{9,8},{10,11... | collective-permute-start | bytes 1572872 | tf_op jit(solution)/shard_map/ppermute | solution.py:429
  65.4 160.2 %collective-permute-start.10 = (bf16[5,256,1024]{2,1,0:T(8,128)(2,1)}, bf16[5,256,1024]{2,1,0:T(8,128)(2,1)}, u32[]{:S(2)}, u32[]{:S(2)}) collective-permute-start(bf16[5,256,1024]{2,1,0:T(8,128)(2,1)} %pad_maximum_fusion.33), channel_id=1, source_target_pairs={{0,8},{8,0},{16,24},{24,16},{1,9},{9,1},{17,25},{25,17},{2,10},{10... | collective-permute-start | bytes 7864328 | tf_op jit(solution)/shard_map/ppermute | solution.py:419
  88.3 58.8 %collective-permute-start.11 = (bf16[5,256,1024]{2,1,0:T(8,128)(2,1)}, bf16[5,256,1024]{2,1,0:T(8,128)(2,1)}, u32[]{:S(2)}, u32[]{:S(2)}) collective-permute-start(bf16[5,256,1024]{2,1,0:T(8,128)(2,1)} %pad_maximum_fusion.33), channel_id=1, source_target_pairs={{0,16},{8,24},{16,0},{24,8},{1,17},{9,25},{17,1},{25,9},{2,18},{10... | collective-permute-start | bytes 7864328 | tf_op jit(solution)/shard_map/ppermute | solution.py:424
  147.2 78.4 %collective-permute-start.12 = (bf16[5,256,1024]{2,1,0:T(8,128)(2,1)}, bf16[5,256,1024]{2,1,0:T(8,128)(2,1)}, u32[]{:S(2)}, u32[]{:S(2)}) collective-permute-start(bf16[5,256,1024]{2,1,0:T(8,128)(2,1)} %collective-permute-done.11), channel_id=1, source_target_pairs={{0,8},{8,0},{16,24},{24,16},{1,9},{9,1},{17,25},{25,17},{2,10},{10... | collective-permute-start | bytes 7864328 | tf_op jit(solution)/shard_map/ppermute | solution.py:419
  150.0 25.3 %collective-permute-start.13 = (bf16[2,128,1024]{2,1,0:T(8,128)(2,1)}, bf16[2,128,1024]{2,1,0:T(8,128)(2,1)}, u32[]{:S(2)}, u32[]{:S(2)}) collective-permute-start(bf16[2,128,1024]{2,1,0:T(8,128)(2,1)} %param.38), channel_id=1, source_target_pairs={{0,2},{1,3},{2,0},{3,1},{4,6},{5,7},{6,4},{7,5},{8,10},{9,11},{10,... | collective-permute-start | bytes 1572872 | tf_op jit(solution)/shard_map/ppermute | solution.py:429
  150.6 45.3 %collective-permute-start.14 = (bf16[2,128,1024]{2,1,0:T(8,128)(2,1)}, bf16[2,128,1024]{2,1,0:T(8,128)(2,1)}, u32[]{:S(2)}, u32[]{:S(2)}) collective-permute-start(bf16[2,128,1024]{2,1,0:T(8,128)(2,1)} %param.38), channel_id=1, source_target_pairs={{0,4},{1,5},{2,6},{3,7},{4,0},{5,1},{6,2},{7,3},{8,12},{9,13},{10,... | collective-permute-start | bytes 1572872 | tf_op jit(solution)/shard_map/ppermute | solution.py:429
  166.0 32.6 %collective-permute-start.15 = (bf16[2,128,1024]{2,1,0:T(8,128)(2,1)}, bf16[2,128,1024]{2,1,0:T(8,128)(2,1)S(1)}, u32[]{:S(2)}, u32[]{:S(2)}) collective-permute-start(bf16[2,128,1024]{2,1,0:T(8,128)(2,1)} %param.38), channel_id=1, source_target_pairs={{0,6},{1,7},{2,4},{3,5},{4,2},{5,3},{6,0},{7,1},{8,14},{9,15},{10,... | collective-permute-start | bytes 1572872 | tf_op jit(solution)/shard_map/ppermute | solution.py:429
  175.3 24.9 %collective-permute-start.16 = (bf16[2,128,1024]{2,1,0:T(8,128)(2,1)}, bf16[2,128,1024]{2,1,0:T(8,128)(2,1)S(1)}, u32[]{:S(2)}, u32[]{:S(2)}) collective-permute-start(bf16[2,128,1024]{2,1,0:T(8,128)(2,1)} %param.38), channel_id=1, source_target_pairs={{0,1},{1,0},{2,3},{3,2},{4,5},{5,4},{6,7},{7,6},{8,9},{9,8},{10,11... | collective-permute-start | bytes 1572872 | tf_op jit(solution)/shard_map/ppermute | solution.py:429
  200.2 24.8 %collective-permute-start.21 = (bf16[1,128,4096]{2,1,0:T(8,128)(2,1)S(1)}, bf16[1,128,4096]{2,1,0:T(8,128)(2,1)}, u32[]{:S(2)}, u32[]{:S(2)}) collective-permute-start(bf16[1,128,4096]{2,1,0:T(8,128)(2,1)S(1)} %copy-done.107), channel_id=1, source_target_pairs={{0,16},{8,24},{16,0},{24,8},{1,17},{9,25},{17,1},{25,9},{2,18},{10... | collective-permute-start | bytes 3145736 | tf_op jit(solution)/shard_map/ppermute | solution.py:424
  219.3 103.7 %collective-permute-start.20 = (bf16[1,256,4096]{2,1,0:T(8,128)(2,1)}, bf16[1,256,4096]{2,1,0:T(8,128)(2,1)}, u32[]{:S(2)}, u32[]{:S(2)}) collective-permute-start(bf16[1,256,4096]{2,1,0:T(8,128)(2,1)} %convert_bitcast_fusion.3), channel_id=1, source_target_pairs={{0,8},{8,0},{16,24},{24,16},{1,9},{9,1},{17,25},{25,17},{2,10},{10... | collective-permute-start | bytes 6291464 | tf_op jit(solution)/shard_map/ppermute | solution.py:419
  225.0 126.5 %collective-permute-start.25 = (bf16[1,1024,1024]{2,1,0:T(8,128)(2,1)}, bf16[1,1024,1024]{2,1,0:T(8,128)(2,1)}, u32[]{:S(2)}, u32[]{:S(2)}) collective-permute-start(bf16[1,1024,1024]{2,1,0:T(8,128)(2,1)} %convert_bitcast_fusion), channel_id=1, source_target_pairs={{0,8},{8,0},{16,24},{24,16},{1,9},{9,1},{17,25},{25,17},{2,10},{10... | collective-permute-start | bytes 6291464 | tf_op jit(solution)/shard_map/ppermute | solution.py:419
  225.0 72.1 %collective-permute-start.22 = (bf16[1,128,4096]{2,1,0:T(8,128)(2,1)}, bf16[1,128,4096]{2,1,0:T(8,128)(2,1)}, u32[]{:S(2)}, u32[]{:S(2)}) collective-permute-start(bf16[1,128,4096]{2,1,0:T(8,128)(2,1)} %collective-permute-done.21), channel_id=1, source_target_pairs={{0,1},{1,0},{2,3},{3,2},{4,5},{5,4},{6,7},{7,6},{8,9},{9,8},{10,11... | collective-permute-start | bytes 3145736 | tf_op jit(solution)/shard_map/ppermute | solution.py:429
  225.6 72.2 %collective-permute-start.26 = (bf16[1,512,1024]{2,1,0:T(8,128)(2,1)}, bf16[1,512,1024]{2,1,0:T(8,128)(2,1)S(1)}, u32[]{:S(2)}, u32[]{:S(2)}) collective-permute-start(bf16[1,512,1024]{2,1,0:T(8,128)(2,1)} %dynamic-slice_bitcast_fusion.15), channel_id=1, source_target_pairs={{0,16},{8,24},{16,0},{24,8},{1,17},{9,25},{17,1},{25,9},{2,18},{10... | collective-permute-start | bytes 3145736 | tf_op jit(solution)/shard_map/ppermute | solution.py:424
  225.6 97.9 %collective-permute-start.23 = (bf16[1,128,4096]{2,1,0:T(8,128)(2,1)}, bf16[1,128,4096]{2,1,0:T(8,128)(2,1)}, u32[]{:S(2)}, u32[]{:S(2)}) collective-permute-start(bf16[1,128,4096]{2,1,0:T(8,128)(2,1)} %collective-permute-done.21), channel_id=1, source_target_pairs={{0,8},{8,0},{16,24},{24,16},{1,9},{9,1},{17,25},{25,17},{2,10},{10... | collective-permute-start | bytes 3145736 | tf_op jit(solution)/shard_map/ppermute | solution.py:419
  297.2 26.3 %collective-permute-start.24 = (bf16[1,128,4096]{2,1,0:T(8,128)(2,1)}, bf16[1,128,4096]{2,1,0:T(8,128)(2,1)S(1)}, u32[]{:S(2)}, u32[]{:S(2)}) collective-permute-start(bf16[1,128,4096]{2,1,0:T(8,128)(2,1)} %collective-permute-done.22), channel_id=1, source_target_pairs={{0,8},{8,0},{16,24},{24,16},{1,9},{9,1},{17,25},{25,17},{2,10},{10... | collective-permute-start | bytes 3145736 | tf_op jit(solution)/shard_map/ppermute | solution.py:419
  297.7 25.3 %collective-permute-start.27 = (bf16[1,512,1024]{2,1,0:T(8,128)(2,1)S(1)}, bf16[1,512,1024]{2,1,0:T(8,128)(2,1)}, u32[]{:S(2)}, u32[]{:S(2)}) collective-permute-start(bf16[1,512,1024]{2,1,0:T(8,128)(2,1)S(1)} %collective-permute-done.26), channel_id=1, source_target_pairs={{0,1},{1,0},{2,3},{3,2},{4,5},{5,4},{6,7},{7,6},{8,9},{9,8},{10,11... | collective-permute-start | bytes 3145736 | tf_op jit(solution)/shard_map/ppermute | solution.py:429
  323.0 28.4 %collective-permute-start.28 = (bf16[1,512,1024]{2,1,0:T(8,128)(2,1)S(1)}, bf16[1,512,1024]{2,1,0:T(8,128)(2,1)}, u32[]{:S(2)}, u32[]{:S(2)}) collective-permute-start(bf16[1,512,1024]{2,1,0:T(8,128)(2,1)S(1)} %collective-permute-done.26), channel_id=1, source_target_pairs={{0,8},{8,0},{16,24},{24,16},{1,9},{9,1},{17,25},{25,17},{2,10},{10... | collective-permute-start | bytes 3145736 | tf_op jit(solution)/shard_map/ppermute | solution.py:419
  323.0 28.4 %collective-permute-start.29 = (bf16[1,512,1024]{2,1,0:T(8,128)(2,1)}, bf16[1,512,1024]{2,1,0:T(8,128)(2,1)}, u32[]{:S(2)}, u32[]{:S(2)}) collective-permute-start(bf16[1,512,1024]{2,1,0:T(8,128)(2,1)} %collective-permute-done.27), channel_id=1, source_target_pairs={{0,8},{8,0},{16,24},{24,16},{1,9},{9,1},{17,25},{25,17},{2,10},{10... | collective-permute-start | bytes 3145736 | tf_op jit(solution)/shard_map/ppermute | solution.py:419
  431.5 92.7 %collective-permute-start.33 = (bf16[8,1,128,1024]{3,2,0,1:T(8,128)(2,1)}, bf16[8,1,128,1024]{3,2,0,1:T(8,128)(2,1)S(1)}, u32[]{:S(2)}, u32[]{:S(2)}) collective-permute-start(bf16[8,1,128,1024]{3,2,0,1:T(8,128)(2,1)} %dynamic-slice_bitcast_fusion.4), channel_id=1, source_target_pairs={{0,16},{8,24},{16,0},{24,8},{1,17},{9,25},{17,1},{25,9},{2,18},{10... | collective-permute-start | bytes 6291464 | tf_op jit(solution)/shard_map/ppermute | solution.py:424
  459.5 76.6 %collective-permute-start.32 = (bf16[8,1,32,4096]{3,2,0,1:T(8,128)(2,1)}, bf16[8,1,32,4096]{3,2,0,1:T(8,128)(2,1)}, u32[]{:S(2)}, u32[]{:S(2)}) collective-permute-start(bf16[8,1,32,4096]{3,2,0,1:T(8,128)(2,1)} %dynamic-slice_bitcast_fusion.3), channel_id=1, source_target_pairs={{0,16},{8,24},{16,0},{24,8},{1,17},{9,25},{17,1},{25,9},{2,18},{10... | collective-permute-start | bytes 6291464 | tf_op jit(solution)/shard_map/ppermute | solution.py:424
  557.4 108.5 %collective-permute-start.34 = (bf16[2,8,5,32,1024]{4,3,2,1,0:T(8,128)(2,1)}, bf16[2,8,5,32,1024]{4,3,2,1,0:T(8,128)(2,1)}, u32[]{:S(2)}, u32[]{:S(2)}) collective-permute-start(bf16[2,8,5,32,1024]{4,3,2,1,0:T(8,128)(2,1)} %get-tuple-element.746), channel_id=1, source_target_pairs={{0,8},{8,0},{16,24},{24,16},{1,9},{9,1},{17,25},{25,17},{2,10},{10... | collective-permute-start | bytes 15728648 | tf_op jit(solution)/shard_map/ppermute | solution.py:419
  557.5 26.1 %collective-permute-start.36 = (bf16[4,1,128,1024]{3,2,0,1:T(8,128)(2,1)S(1)}, bf16[4,1,128,1024]{3,2,0,1:T(8,128)(2,1)}, u32[]{:S(2)}, u32[]{:S(2)}) collective-permute-start(bf16[4,1,128,1024]{3,2,0,1:T(8,128)(2,1)S(1)} %dynamic-slice_bitcast_fusion.14), channel_id=1, source_target_pairs={{0,1},{1,0},{2,3},{3,2},{4,5},{5,4},{6,7},{7,6},{8,9},{9,8},{10,11... | collective-permute-start | bytes 3145736 | tf_op jit(solution)/shard_map/ppermute | solution.py:429
  561.3 90.7 %collective-permute-start.35 = (bf16[4,2,128,1024]{3,2,1,0:T(8,128)(2,1)}, bf16[4,2,128,1024]{3,2,1,0:T(8,128)(2,1)}, u32[]{:S(2)}, u32[]{:S(2)}) collective-permute-start(bf16[4,2,128,1024]{3,2,1,0:T(8,128)(2,1)} %slice.531), channel_id=1, source_target_pairs={{0,1},{1,0},{2,3},{3,2},{4,5},{5,4},{6,7},{7,6},{8,9},{9,8},{10,11... | collective-permute-start | bytes 6291464 | tf_op jit(solution)/shard_map/ppermute | solution.py:429
  562.8 87.7 %collective-permute-start.37 = (bf16[4,1,32,4096]{3,2,0,1:T(8,128)(2,1)}, bf16[4,1,32,4096]{3,2,0,1:T(8,128)(2,1)}, u32[]{:S(2)}, u32[]{:S(2)}) collective-permute-start(bf16[4,1,32,4096]{3,2,0,1:T(8,128)(2,1)} %dynamic-slice_bitcast_fusion.13), channel_id=1, source_target_pairs={{0,1},{1,0},{2,3},{3,2},{4,5},{5,4},{6,7},{7,6},{8,9},{9,8},{10,11... | collective-permute-start | bytes 3145736 | tf_op jit(solution)/shard_map/ppermute | solution.py:429
  653.8 145.0 %collective-permute-start.64 = (bf16[1,32,4096]{2,1,0:T(8,128)(2,1)}, bf16[1,32,4096]{2,1,0:T(8,128)(2,1)}, u32[]{:S(2)}, u32[]{:S(2)}) collective-permute-start(bf16[1,32,4096]{2,1,0:T(8,128)(2,1)} %get-tuple-element.762), channel_id=1, source_target_pairs={{0,6},{1,7},{2,4},{3,5},{4,2},{5,3},{6,0},{7,1},{8,14},{9,15},{10,... | collective-permute-start | bytes 786440 | tf_op jit(solution)/shard_map/ppermute | solution.py:429
  661.5 137.4 %collective-permute-start.63 = (bf16[1,32,4096]{2,1,0:T(8,128)(2,1)}, bf16[1,32,4096]{2,1,0:T(8,128)(2,1)}, u32[]{:S(2)}, u32[]{:S(2)}) collective-permute-start(bf16[1,32,4096]{2,1,0:T(8,128)(2,1)} %get-tuple-element.763), channel_id=1, source_target_pairs={{0,4},{1,5},{2,6},{3,7},{4,0},{5,1},{6,2},{7,3},{8,12},{9,13},{10,... | collective-permute-start | bytes 786440 | tf_op jit(solution)/shard_map/ppermute | solution.py:429
  661.5 137.9 %collective-permute-start.62 = (bf16[1,32,4096]{2,1,0:T(8,128)(2,1)S(1)}, bf16[1,32,4096]{2,1,0:T(8,128)(2,1)}, u32[]{:S(2)}, u32[]{:S(2)}) collective-permute-start(bf16[1,32,4096]{2,1,0:T(8,128)(2,1)S(1)} %get-tuple-element.761), channel_id=1, source_target_pairs={{0,2},{1,3},{2,0},{3,1},{4,6},{5,7},{6,4},{7,5},{8,10},{9,11},{10,... | collective-permute-start | bytes 786440 | tf_op jit(solution)/shard_map/ppermute | solution.py:429
  679.5 69.1 %collective-permute-start.38 = (bf16[8,5,32,1024]{3,2,1,0:T(8,128)(2,1)}, bf16[8,5,32,1024]{3,2,1,0:T(8,128)(2,1)}, u32[]{:S(2)}, u32[]{:S(2)}) collective-permute-start(bf16[8,5,32,1024]{3,2,1,0:T(8,128)(2,1)} %dynamic-slice_bitcast_fusion.2), channel_id=1, source_target_pairs={{0,16},{8,24},{16,0},{24,8},{1,17},{9,25},{17,1},{25,9},{2,18},{10... | collective-permute-start | bytes 7864328 | tf_op jit(solution)/shard_map/ppermute | solution.py:424
  773.1 81.8 %collective-permute-start.40 = (bf16[2,8,3,32,1024]{4,3,2,1,0:T(8,128)(2,1)}, bf16[2,8,3,32,1024]{4,3,2,1,0:T(8,128)(2,1)}, u32[]{:S(2)}, u32[]{:S(2)}) collective-permute-start(bf16[2,8,3,32,1024]{4,3,2,1,0:T(8,128)(2,1)} %pad_maximum_fusion.32), channel_id=1, source_target_pairs={{0,8},{8,0},{16,24},{24,16},{1,9},{9,1},{17,25},{25,17},{2,10},{10... | collective-permute-start | bytes 9437192 | tf_op jit(solution)/shard_map/ppermute | solution.py:419
  778.4 33.2 %collective-permute-start.46 = (bf16[2,128,1024]{2,1,0:T(8,128)(2,1)S(1)}, bf16[2,128,1024]{2,1,0:T(8,128)(2,1)S(1)}, u32[]{:S(2)}, u32[]{:S(2)}) collective-permute-start(bf16[2,128,1024]{2,1,0:T(8,128)(2,1)S(1)} %get-tuple-element.734), channel_id=1, source_target_pairs={{0,6},{1,7},{2,4},{3,5},{4,2},{5,3},{6,0},{7,1},{8,14},{9,15},{10,... | collective-permute-start | bytes 1572872 | tf_op jit(solution)/shard_map/ppermute | solution.py:429
  798.8 38.9 %collective-permute-start.45 = (bf16[2,128,1024]{2,1,0:T(8,128)(2,1)S(1)}, bf16[2,128,1024]{2,1,0:T(8,128)(2,1)S(1)}, u32[]{:S(2)}, u32[]{:S(2)}) collective-permute-start(bf16[2,128,1024]{2,1,0:T(8,128)(2,1)S(1)} %get-tuple-element.735), channel_id=1, source_target_pairs={{0,4},{1,5},{2,6},{3,7},{4,0},{5,1},{6,2},{7,3},{8,12},{9,13},{10,... | collective-permute-start | bytes 1572872 | tf_op jit(solution)/shard_map/ppermute | solution.py:429
  798.9 38.8 %collective-permute-start.44 = (bf16[2,128,1024]{2,1,0:T(8,128)(2,1)S(1)}, bf16[2,128,1024]{2,1,0:T(8,128)(2,1)S(1)}, u32[]{:S(2)}, u32[]{:S(2)}) collective-permute-start(bf16[2,128,1024]{2,1,0:T(8,128)(2,1)S(1)} %get-tuple-element.733), channel_id=1, source_target_pairs={{0,2},{1,3},{2,0},{3,1},{4,6},{5,7},{6,4},{7,5},{8,10},{9,11},{10,... | collective-permute-start | bytes 1572872 | tf_op jit(solution)/shard_map/ppermute | solution.py:429
  803.3 36.7 %collective-permute-start.58 = (f32[7,1024]{1,0:T(8,128)S(1)}, f32[7,1024]{1,0:T(8,128)S(1)}, u32[]{:S(2)}, u32[]{:S(2)}) collective-permute-start(f32[7,1024]{1,0:T(8,128)S(1)} %add.713), channel_id=1, source_target_pairs={{0,1},{1,0},{2,3},{3,2},{4,5},{5,4},{6,7},{7,6},{8,9},{9,8},{10,11... | collective-permute-start | bytes 86024 | tf_op jit(solution)/shard_map/ppermute | solution.py:429
  848.7 48.9 %collective-permute-start.39 = (bf16[4,2,128,1024]{3,2,1,0:T(8,128)(2,1)}, bf16[4,2,128,1024]{3,2,1,0:T(8,128)(2,1)}, u32[]{:S(2)}, u32[]{:S(2)}) collective-permute-start(bf16[4,2,128,1024]{3,2,1,0:T(8,128)(2,1)} %slice.533), channel_id=1, source_target_pairs={{0,1},{1,0},{2,3},{3,2},{4,5},{5,4},{6,7},{7,6},{8,9},{9,8},{10,11... | collective-permute-start | bytes 6291464 | tf_op jit(solution)/shard_map/ppermute | solution.py:429
  849.9 73.4 %collective-permute-start.52 = (bf16[4,5,32,1024]{3,2,1,0:T(8,128)(2,1)}, bf16[4,5,32,1024]{3,2,1,0:T(8,128)(2,1)}, u32[]{:S(2)}, u32[]{:S(2)}) collective-permute-start(bf16[4,5,32,1024]{3,2,1,0:T(8,128)(2,1)} %dynamic-slice_bitcast_fusion.6), channel_id=1, source_target_pairs={{0,1},{1,0},{2,3},{3,2},{4,5},{5,4},{6,7},{7,6},{8,9},{9,8},{10,11... | collective-permute-start | bytes 3932168 | tf_op jit(solution)/shard_map/ppermute | solution.py:429
  861.0 73.9 %collective-permute-start.47 = (bf16[8,3,32,1024]{3,2,1,0:T(8,128)(2,1)}, bf16[8,3,32,1024]{3,2,1,0:T(8,128)(2,1)S(1)}, u32[]{:S(2)}, u32[]{:S(2)}) collective-permute-start(bf16[8,3,32,1024]{3,2,1,0:T(8,128)(2,1)} %dynamic-slice_bitcast_fusion.5), channel_id=1, source_target_pairs={{0,16},{8,24},{16,0},{24,8},{1,17},{9,25},{17,1},{25,9},{2,18},{10... | collective-permute-start | bytes 4718600 | tf_op jit(solution)/shard_map/ppermute | solution.py:424
  929.5 71.5 %collective-permute-start.43 = (bf16[2,128,1024]{2,1,0:T(8,128)(2,1)S(1)}, bf16[2,128,1024]{2,1,0:T(8,128)(2,1)S(1)}, u32[]{:S(2)}, u32[]{:S(2)}) collective-permute-start(bf16[2,128,1024]{2,1,0:T(8,128)(2,1)S(1)} %get-tuple-element.737), channel_id=1, source_target_pairs={{0,6},{1,7},{2,4},{3,5},{4,2},{5,3},{6,0},{7,1},{8,14},{9,15},{10,... | collective-permute-start | bytes 1572872 | tf_op jit(solution)/shard_map/ppermute | solution.py:429
  932.0 69.0 %collective-permute-start.42 = (bf16[2,128,1024]{2,1,0:T(8,128)(2,1)S(1)}, bf16[2,128,1024]{2,1,0:T(8,128)(2,1)S(1)}, u32[]{:S(2)}, u32[]{:S(2)}) collective-permute-start(bf16[2,128,1024]{2,1,0:T(8,128)(2,1)S(1)} %get-tuple-element.738), channel_id=1, source_target_pairs={{0,4},{1,5},{2,6},{3,7},{4,0},{5,1},{6,2},{7,3},{8,12},{9,13},{10,... | collective-permute-start | bytes 1572872 | tf_op jit(solution)/shard_map/ppermute | solution.py:429
  932.0 66.7 %collective-permute-start.54 = (bf16[5,32,1024]{2,1,0:T(8,128)(2,1)S(1)}, bf16[5,32,1024]{2,1,0:T(8,128)(2,1)S(1)}, u32[]{:S(2)}, u32[]{:S(2)}) collective-permute-start(bf16[5,32,1024]{2,1,0:T(8,128)(2,1)S(1)} %get-tuple-element.757), channel_id=1, source_target_pairs={{0,4},{1,5},{2,6},{3,7},{4,0},{5,1},{6,2},{7,3},{8,12},{9,13},{10,... | collective-permute-start | bytes 983048 | tf_op jit(solution)/shard_map/ppermute | solution.py:429
  935.0 64.3 %collective-permute-start.53 = (bf16[5,32,1024]{2,1,0:T(8,128)(2,1)S(1)}, bf16[5,32,1024]{2,1,0:T(8,128)(2,1)S(1)}, u32[]{:S(2)}, u32[]{:S(2)}) collective-permute-start(bf16[5,32,1024]{2,1,0:T(8,128)(2,1)S(1)} %get-tuple-element.755), channel_id=1, source_target_pairs={{0,2},{1,3},{2,0},{3,1},{4,6},{5,7},{6,4},{7,5},{8,10},{9,11},{10,... | collective-permute-start | bytes 983048 | tf_op jit(solution)/shard_map/ppermute | solution.py:429
  937.6 63.4 %collective-permute-start.41 = (bf16[2,128,1024]{2,1,0:T(8,128)(2,1)S(1)}, bf16[2,128,1024]{2,1,0:T(8,128)(2,1)S(1)}, u32[]{:S(2)}, u32[]{:S(2)}) collective-permute-start(bf16[2,128,1024]{2,1,0:T(8,128)(2,1)S(1)} %get-tuple-element.736), channel_id=1, source_target_pairs={{0,2},{1,3},{2,0},{3,1},{4,6},{5,7},{6,4},{7,5},{8,10},{9,11},{10,... | collective-permute-start | bytes 1572872 | tf_op jit(solution)/shard_map/ppermute | solution.py:429
  (164 other events, 2503.9 us)

commit v2 on v1

--- a/solution.py
+++ b/solution.py
@@ -258,7 +258,6 @@
             pl.BlockSpec((1, 1, 2 * rows), lambda p, n, s: (p, 0, 0)),
         ]
         args += [own_keys, own_values, tiles, own_bias]
-    flops = 2 * 2 * streams * 3 * rows * length * width
     return pl.pallas_call(
         partial(forward_kernel, is_self, rows, near_tiles),
         grid_spec=pltpu.PrefetchScalarGridSpec(
@@ -276,7 +275,7 @@
             jax.ShapeDtypeStruct((pairs, streams, 1, 6 * rows), jnp.float32),
         ],
         compiler_params=pltpu.CompilerParams(vmem_limit_bytes=20 * 1024 * 1024),
-        cost_estimate=pl.CostEstimate(flops=4 * flops, bytes_accessed=20_000_000, transcendentals=0),
+        cost_estimate=pl.CostEstimate(flops=0, bytes_accessed=0, transcendentals=0),
     )(bounds, *args)
 
 
@@ -304,7 +303,6 @@
         out_specs += [own_spec, own_spec, tile_spec, own_bias_spec]
         out_shape += [jax.ShapeDtypeStruct(own_keys.shape, jnp.bfloat16)] * 2
         out_shape += [jax.ShapeDtypeStruct(tiles.shape, jnp.float32), jax.ShapeDtypeStruct(own_bias.shape, jnp.float32)]
-    flops = 5 * 2 * streams * 3 * rows * length * width
     return pl.pallas_call(
         partial(backward_kernel, is_self, rows, near_tiles),
         grid_spec=pltpu.PrefetchScalarGridSpec(
@@ -320,7 +318,7 @@
         ),
         out_shape=out_shape,
         compiler_params=pltpu.CompilerParams(vmem_limit_bytes=20 * 1024 * 1024),
-        cost_estimate=pl.CostEstimate(flops=4 * flops, bytes_accessed=40_000_000, transcendentals=0),
+        cost_estimate=pl.CostEstimate(flops=0, bytes_accessed=0, transcendentals=0),
     )(bounds, *args)
 
 
@@ -435,33 +433,14 @@
 
 def assemble(pieces):
     count = pieces[0].shape[0]
-    place = lax.axis_index("dp")
-    split_rows = len(pieces) > 4
-
-    def ordered(at, row):
+
+    def ordered(at):
         def joined(*parts):
-            shards = [[parts[0]], [parts[1]]]
-            if split_rows:
-                halves = (parts[2:4], parts[4:6])
-                shards += [[half[row], half[1 - row]] for half in halves]
-            else:
-                shards += [[parts[2]], [parts[3]]]
-            return [
-                jnp.concatenate([part[k] for index in range(4) for part in shards[at ^ index]], axis=0)
-                for k in range(count)
-            ]
+            return [jnp.concatenate([parts[at ^ index][k] for index in range(4)], axis=0) for k in range(count)]
 
         return joined
 
-    if split_rows:
-        row = lax.axis_index("blk") % 2
-        return lax.switch(2 * place + row, [ordered(at, r) for at in range(4) for r in range(2)], *pieces)
-    return lax.switch(place, [ordered(at, 0) for at in range(4)], *pieces)
-
-
-def half_rows(shard):
-    rows = shard.shape[1] // 2
-    return lax.dynamic_slice_in_dim(shard, (lax.axis_index("blk") % 2) * rows, rows, 1)
+    return lax.switch(lax.axis_index("dp"), [ordered(at) for at in range(4)], *pieces)
 
 
 def outer_low(left_side, right_side):
@@ -500,12 +479,23 @@
     return pick(values_in, 1 - mine, axis + 1), pick(values_in, mine, axis + 1)
 
 
-def start_rows(values_in):
-    return [values_in] + [swap_block(values_in, gap) for gap in range(2, lax.axis_size("blk"), 2)]
-
-
-def finish_rows(pieces):
-    return jnp.stack(pieces + [swap_block(piece, 1) for piece in pieces])
+def gather_far_first(values_in):
+    even = [values_in]
+    odd = [swap_block(values_in, 1)]
+    before = values_in
+    for gap in range(2, lax.axis_size("blk"), 2):
+        piece = swap_block(values_in if gap <= 4 else tie(values_in, before), gap)
+        before = piece
+        even.append(piece)
+        odd.append(swap_block(piece, 1))
+    return jnp.stack(even + odd), before
+
+
+def gather_near_first(values_in, *earlier):
+    both = jnp.stack([values_in, swap_block(values_in, 1)])
+    sent = tie(both, *earlier)
+    pieces = [both] + [swap_block(sent, gap) for gap in range(2, lax.axis_size("blk"), 2)]
+    return jnp.stack(pieces, axis=1).reshape((lax.axis_size("blk"),) + values_in.shape)
 
 
 def fold_odd(terms):
@@ -520,14 +510,20 @@
     )
 
 
-def exchange_blocks(values_in):
-    count = values_in.shape[0]
+def fold_far_first(terms):
+    half = terms.shape[0] // 2
+    split = terms.reshape((2, half) + terms.shape[1:])
+    return split[:, 0], [swap_block(split[:, index], 2 * index) for index in range(1, half)]
+
+
+def sum_all(kept, come):
+    return sum([piece.astype(jnp.float32) for piece in come], kept.astype(jnp.float32))
+
+
+def start_exchange(values_in):
     mine = lax.axis_index("blk") // 2
-    come = [swap_block(pick(values_in, mine ^ gap, 0), 2 * gap) for gap in range(1, count)]
-    total = pick(values_in, mine, 0).astype(jnp.float32)
-    for piece in come:
-        total = total + piece.astype(jnp.float32)
-    return total
+    come = [swap_block(pick(values_in, mine ^ gap, 0), 2 * gap) for gap in range(1, values_in.shape[0])]
+    return pick(values_in, mine, 0), come
 
 
 def split_shares(share):
@@ -564,13 +560,13 @@
     heads, buckets = rel_table.shape
     head_size = width // heads
     place = lax.axis_index("blk")
-    main_rows = start_rows(hidden[:, 0])
+    main_all, main_last = gather_far_first(hidden[:, 0])
+    enc_all = gather_near_first(encoder, main_last)
     low = partial(lax.convert_element_type, new_dtype=jnp.bfloat16)
     qkv_low = low(qkv_self)
     middle_low = jnp.concatenate([low(out_self)[None], low(qkv_cross), low(out_cross)[None]])
     first_low_w, second_low_w = low(ffn_in)[None], low(ffn_out)[None]
     qkv_far = swap_chip(qkv_low)
-    main_all = finish_rows(main_rows)
     w_qkv = assemble([qkv_low, swap_core(qkv_low), qkv_far, swap_core(qkv_far)])
     doc_ends = jnp.cumsum(lengths, axis=-1)
     begin = place * rows
@@ -595,20 +591,15 @@
     own_keys = matmul(hidden_own, w_qkv[1]).astype(jnp.bfloat16)
     own_values = matmul(hidden_own, w_qkv[2]).astype(jnp.bfloat16)
     middle_far = swap_chip(tie(middle_low, qkv_far))
-    enc_all = finish_rows(start_rows(tie(encoder, main_all)))
     main_keys = matmul(main_all, w_qkv[1]).astype(jnp.bfloat16)
     main_values = matmul(main_all, w_qkv[2]).astype(jnp.bfloat16)
     own = (own_keys, own_values, tiles, own_bias)
 
-    first_half_sent = half_rows(first_low_w)
-    first_far = swap_chip(tie(first_half_sent, main_values, query))
-    query = tie(query, first_half_sent)
+    first_far = swap_chip(tie(first_low_w, main_values, query))
     attended, self_lse = attend_forward(
         self_bounds, query, main_keys, main_values, own, near_tiles, head_size
     )
-    second_half_sent = half_rows(second_low_w)
-    second_far = swap_chip(tie(second_half_sent, attended, first_far))
-    first_other = swap_block(tie(first_far, attended), 1)
+    second_far = swap_chip(tie(second_low_w, first_far))
     middle_pieces = [middle_low, swap_core(middle_low), middle_far, swap_core(tie(middle_far, attended))]
     w_out, *c_qkv, c_out = assemble(middle_pieces)
     first_norm, first_scale = norm_parts(
@@ -622,15 +613,9 @@
     cross_att, cross_lse = attend_forward(
         cross_bounds, tall(cross_query), enc_keys, enc_values, None, 0, head_size
     )
-    second_other = swap_block(tie(second_far, cross_query), 1)
     w_first, w_second = (
-        assemble(
-            [shard, swap_core(shard), far, other, swap_core(far), swap_core(tie(other, cross_att))]
-        )[0]
-        for shard, far, other in (
-            (first_low_w, first_far, first_other),
-            (second_low_w, second_far, second_other),
-        )
+        assemble([shard, swap_core(shard), far, swap_core(far)])[0]
+        for shard, far in ((first_low_w, tie(first_far, cross_query)), (second_low_w, tie(second_far, cross_query)))
     )
     second_norm, second_scale = norm_parts(first_out + matmul(flat(cross_att), c_out))
     second_out = second_norm * norm_gain[1] + norm_bias[1]
@@ -654,9 +639,9 @@
     inner_grad = (
         matmul_t(tie(third_low, second_sent), w_second) * act_slope.astype(jnp.float32)
     ).astype(jnp.bfloat16)
-    chip_sent, chip_kept = open_chip(add_low(second_kept, second_come))
-    chip_come = swap_chip(chip_sent)
-    inner_grad = tie(inner_grad, chip_sent)
+    row_sent, row_kept = open_block(add_low(second_kept, second_come), 1, 1)
+    row_come = swap_block(row_sent, 1)
+    inner_grad = tie(inner_grad, row_sent)
     first_part = outer_low(second_low, inner_grad).astype(jnp.bfloat16)
     first_sent, first_kept = open_core([first_part])
     first_come = swap_core(first_sent)
@@ -672,11 +657,12 @@
         cross_bounds, tall(cross_query), enc_keys, enc_values, cross_att, cross_mix_grad, cross_lse,
         None, 0, head_size,
     )
+    chip_sent, chip_kept = open_chip(add_low(row_kept, tie(row_come, enc_key_grad)))
+    chip_come = swap_chip(chip_sent)
+    enc_key_grad = tie(enc_key_grad, chip_sent)
     encoder_terms = (matmul_t(enc_key_grad, c_qkv[1]) + matmul_t(enc_value_grad, c_qkv[2])).astype(jnp.bfloat16)
-    encoder_kept, encoder_come = fold_odd(encoder_terms)
-    second_row_sent, second_row_kept = open_block(add_low(chip_kept, tie(chip_come, encoder_terms)), 0, 1)
-    second_row_come = swap_block(second_row_sent, 1)
-    first_row_sent, first_row_kept = open_block(add_low(first_chip_kept, tie(first_chip_come, second_row_sent)), 0, 1)
+    encoder_kept, encoder_come = fold_far_first(encoder_terms)
+    first_row_sent, first_row_kept = open_block(add_low(first_chip_kept, tie(first_chip_come, encoder_terms)), 0, 1)
     first_row_come = swap_block(first_row_sent, 1)
     first_total = second_grad + matmul_t(flat(tie(cross_query_grad, first_row_sent)), c_qkv[0])
     gain_one = jnp.sum(first_total * first_norm, axis=0)
@@ -698,23 +684,23 @@
     mix_grad = tall(matmul_t(tie(out_low, cross_sent), w_out).astype(jnp.bfloat16))
     cross_chip_sent, cross_chip_kept = open_chip(add_low(cross_kept, tie(cross_come, mix_grad)))
     cross_chip_come = swap_chip(cross_chip_sent)
-    second_half = add_low(second_row_kept, tie(second_row_come, mix_grad))
-    first_half = add_low(first_row_kept, tie(first_row_come, mix_grad))
-    g_second = exchange_blocks(second_half)[0]
-    g_first = exchange_blocks(first_half)[0]
-    encoder_half = add_low(encoder_kept, tie(encoder_come, second_half, first_half))
-    d_encoder = fold_even(encoder_half)
-    mix_grad = tie(mix_grad, cross_chip_sent, encoder_half)
+    second_half = add_low(chip_kept, tie(chip_come, mix_grad))
+    g_second = sum_all(*start_exchange(second_half))[0]
+    mix_grad = tie(mix_grad, cross_chip_sent, second_half)
     query_grad, key_grad, value_grad, own_key_grad, own_value_grad, tile_grads, own_sums = attend_backward(
         self_bounds, query, main_keys, main_values, attended, mix_grad, self_lse, own, near_tiles, head_size
     )
+    first_half = add_low(first_row_kept, tie(first_row_come, query_grad))
+    g_first = sum_all(*start_exchange(first_half))[0]
+    key_grad = tie(key_grad, first_half)
     main_terms = (matmul_t(key_grad, w_qkv[1]) + matmul_t(value_grad, w_qkv[2])).astype(jnp.bfloat16)
     main_kept, main_come = fold_odd(main_terms)
-    cross_row_sent, cross_row_kept = open_block(add_low(cross_chip_kept, tie(cross_chip_come, main_terms)), 0, 1)
-    cross_row_come = swap_block(cross_row_sent, 1)
+    main_come_from = main_terms
+    encoder_half = sum_all(encoder_kept, [tie(piece, main_terms) for piece in encoder_come]).astype(jnp.bfloat16)
+    d_encoder = sum_all(encoder_half[0], [swap_block(encoder_half[1], 1)])
     own_flat = flat(hidden_own)
     main_flat = flat(main_all)
-    started = tie(query_grad, cross_row_sent)
+    started = tie(query_grad, main_come_from, encoder_half)
     self_parts = [outer_low(flat(hidden), flat(started)).astype(jnp.bfloat16)] + [
         (outer_low(main_flat, flat(tie(grad, started))) + outer_low(own_flat, flat(own_grad))).astype(jnp.bfloat16)
         for grad, own_grad in ((key_grad, own_key_grad), (value_grad, own_value_grad))
@@ -727,12 +713,15 @@
     own_back = matmul_t(tie(own_key_grad, self_chip_sent), w_qkv[1]) + matmul_t(own_value_grad, w_qkv[2])
     main_half = add_low(main_kept, tie(main_come, own_back))
     main_back = fold_even(main_half)
-    cross_share = exchange_blocks(add_low(cross_row_kept, tie(cross_row_come, own_back)))
-    g_cross_out, *g_cross, g_self_out = split_shares(cross_share)
+    cross_half = add_low(cross_chip_kept, tie(cross_chip_come, main_half))
+    late_sent, late_kept = open_block(
+        jnp.concatenate([cross_half, add_low(self_chip_kept, tie(self_chip_come, main_half))], axis=1), 0, 1
+    )
+    late_half = add_low(late_kept, swap_block(late_sent, 1))
+    late_share = sum_all(*start_exchange(late_half))
+    g_cross_out, *g_cross, g_self_out = split_shares(late_share[:5])
     g_cross = jnp.stack(g_cross)
-    self_row_sent, self_row_kept = open_block(add_low(self_chip_kept, self_chip_come), 0, 1)
-    self_row_come = swap_block(self_row_sent, 1)
-    g_qkv = exchange_blocks(add_low(self_row_kept, self_row_come))
+    g_qkv = late_share[5:]
     d_hidden = local_grad + jnp.concatenate([main_back[:, None], own_back], axis=1)
     rel_grad = table_grad(tile_grads, own_sums, onehot, buckets)
     small = jnp.concatenate(

time: 1050 us -> 885 us (0.84); the launches traced: 1030 us -> 884 us
  waiting for transfers between devices: 329 us -> 259 us
  starting transfers between devices: 136 us -> 94 us
  local copies, waits for them, and re-layouts: 133 us -> 95.4 us
  other arithmetic: 91.7 us -> 118 us
  matrix products: 202 us -> 185 us
    ppermute x44 -> x35, waiting for transfers between devices: 308 us -> 173 us  [swap_block(): return lax.ppermute(values_in, 'blk', [(i, i ^ bit) for i in range(size)])]
    ppermute x9, waiting for transfers between devices: 18.2 us -> 86 us  [swap_chip(): return lax.ppermute(values_in, 'dp', [(i, i ^ 2) for i in range(size)])]
    ppermute x44 -> x35, starting transfers between devices: 127 us -> 80 us  [swap_block(): return lax.ppermute(values_in, 'blk', [(i, i ^ bit) for i in range(size)])]
    cond x10 -> x0, local copies, waits for them, and re-layouts: 21.7 us -> none
    concatenate x6 -> x9, other arithmetic: 1.96 us -> 15 us  [the longest x8 14.6 us: joined(): jnp.concatenate([parts[at ^ index][k] for index in range(4)], axis=0)]
    unnamed x309 -> x264, local copies, waits for them, and re-layouts: 56.6 us -> 46.9 us
    convert_element_type x14 -> x12, other arithmetic: 42.2 us -> 42.3 us  [add_low(): (kept.astype(jnp.float32) + arrived.astype(jnp.float32)).astype(jnp.bfloa...]
  transfers between devices with their start and end apart: 68 -> 57, of which waited for: 27 -> 18; matrix products, arithmetic and copies ran while one was open for 30% -> 31% of each run, Pallas kernels for 12% -> 14%
where the time goes in v2:
time: 885 us; the launch traced here: 884 us
  waiting for transfers between devices  259 us (29%)
  matrix products  185 us (21%)
  Pallas kernels  120 us (14%)
  other arithmetic  118 us (13%)
  local copies, waits for them, and re-layouts  95.4 us (11%)
  starting transfers between devices  94 us (11%)
  loops' own time  9.31 us (1%)
    ppermute x35, waiting for transfers between devices, swap_block(): return lax.ppermute(values_in, 'blk', [(i, i ^ bit) for i in range(size)])  173 us
    ppermute x9, waiting for transfers between devices, swap_chip(): return lax.ppermute(values_in, 'dp', [(i, i ^ 2) for i in range(size)])  86 us
    ppermute x35, starting transfers between devices, swap_block(): return lax.ppermute(values_in, 'blk', [(i, i ^ bit) for i in range(size)])  80 us
    pallas_call x2, Pallas kernels, attend_backward(): pl.pallas_call(partial(backward_kernel, is_self, rows, near_tiles), grid_...  72.2 us
    dot_general x12, matrix products, matmul_t(): jnp.einsum('...j,ij->...i', left_side, right_side, preferred_element_type...  70.4 us
    dot_general x12, matrix products, matmul(): jnp.einsum('...i,ij->...j', left_side, right_side, preferred_element_type...  61.3 us
    pallas_call x2, Pallas kernels, attend_forward(): pl.pallas_call(partial(forward_kernel, is_self, rows, near_tiles), grid_s...  47.9 us
    unnamed x264, local copies, waits for them, and re-layouts  46.9 us
  transfers between devices with their start and end apart: 57, of which 18 were waited for; matrix products, arithmetic and copies ran while one was open for 31% of the time, Pallas kernels for 14%

profile of v2, /device:TPU:0, one launch (start us, length us, event | category | flops | bytes accessed | tf_op | source)
XLA Modules:
  0.0 884.0 jit_solution(2182581660017566919)
XLA Ops:
  36.8 10.4 %collective-permute-done.1 = bf16[3,256,1024]{2,1,0:T(8,128)(2,1)} collective-permute-done((bf16[3,256,1024]{2,1,0:T(8,128)(2,1)S(1)}, bf16[3,256,1024]{2,1,0:T(8,128)(2,1)}, u32[]{:S(2)}, u32[]{:S(2)}) %collective-permute-start.1) | collective-permute-done | bytes 1572896 | tf_op jit(solution)/shard_map/ppermute | solution.py:422
  57.0 7.0 collective-permute-done.7
  64.9 10.4 %collective-permute-done.8 = bf16[2,128,1024]{2,1,0:T(8,128)(2,1)S(1)} collective-permute-done((bf16[2,128,1024]{2,1,0:T(8,128)(2,1)}, bf16[2,128,1024]{2,1,0:T(8,128)(2,1)S(1)}, u32[]{:S(2)}, u32[]{:S(2)}) %collective-permute-start.8) | collective-permute-done | bytes 524320 | tf_op jit(solution)/shard_map/ppermute | solution.py:427
  76.4 9.8 %collective-permute-done.9 = bf16[2,128,1024]{2,1,0:T(8,128)(2,1)S(1)} collective-permute-done((bf16[2,128,1024]{2,1,0:T(8,128)(2,1)S(1)}, bf16[2,128,1024]{2,1,0:T(8,128)(2,1)S(1)}, u32[]{:S(2)}, u32[]{:S(2)}) %collective-permute-start.9) | collective-permute-done | bytes 524320 | tf_op jit(solution)/shard_map/ppermute | solution.py:427
  104.8 4.7 convolution_convert_fusion.4.refs_3_
  109.5 4.7 convolution_convert_fusion.5.refs_2_
  114.4 19.2 %shard_map.220 = (bf16[2,3,128,1024]{3,2,1,0:T(8,128)(2,1)S(1)}, f32[8,2,1,768]{3,2,1,0:T(1,128)S(1)}) custom-call(s32[2,3]{1,0:T(2,128)S(1)} %get-tuple-element.583.refs_0_, bf16[2,3,128,1024]{3,2,1,0:T(8,128)(2,1)S(1)} %fusion.69.refs_1_, bf16[8,2,128,1024]{3,2,1,0:T(8,128)(2,1)S(1)} %convolution_convert_fusion.5.refs_2_, ...), custom_call_target="tpu_custom_call" | custom-call | tf_op jit(solution)/shard_map/pallas_call | solution.py:261
  133.6 12.3 %collective-permute-done.11 = bf16[5,256,1024]{2,1,0:T(8,128)(2,1)} collective-permute-done((bf16[5,256,1024]{2,1,0:T(8,128)(2,1)}, bf16[5,256,1024]{2,1,0:T(8,128)(2,1)}, u32[]{:S(2)}, u32[]{:S(2)}) %collective-permute-start.11) | collective-permute-done | bytes 2621472 | tf_op jit(solution)/shard_map/ppermute | solution.py:422
  167.2 39.0 %collective-permute-done.15 = bf16[2,2,128,1024]{3,2,1,0:T(8,128)(2,1)} collective-permute-done((bf16[2,2,128,1024]{3,2,1,0:T(8,128)(2,1)}, bf16[2,2,128,1024]{3,2,1,0:T(8,128)(2,1)}, u32[]{:S(2)}, u32[]{:S(2)}) %collective-permute-start.15) | collective-permute-done | bytes 1048608 | tf_op jit(solution)/shard_map/ppermute | solution.py:427
  211.9 15.9 %conditional.5 = (bf16[1024,1024]{1,0:T(8,128)(2,1)S(1)}, bf16[1024,1024]{1,0:T(8,128)(2,1)S(1)}, bf16[1024,1024]{1,0:T(8,128)(2,1)S(1)}, bf16[1024,1024]{1,0:T(8,128)(2,1)S(1)}, bf16[1024,1024]{1,0:T(8,128)(2,1)S(1)}) conditional(s32[]{:T(128)} %clamp.2, (bf16[5,256,1024]{2,1,0:T(8,128)(2,1)}, ...), branch_computations={%region_6.7_spmd, %region_7.8_spmd, %region_8.9_spmd, %region_9.10... | conditional | flops 41943040 | bytes 39845928 | solution.py:443
  240.0 4.7 convolution_convert_fusion.3.refs_2_
  244.7 4.7 convolution_convert_fusion.2.refs_3_
  249.5 28.8 %shard_map.221 = (bf16[2,3,128,1024]{3,2,1,0:T(8,128)(2,1)S(1)}, f32[8,2,1,768]{3,2,1,0:T(1,128)S(1)}) custom-call(s32[2,3]{1,0:T(2,128)S(1)} %get-tuple-element.582.refs_0_, bf16[2,3,128,1024]{3,2,1,0:T(8,128)(2,1)S(1)} %bitcast.710, bf16[8,2,128,1024]{3,2,1,0:T(8,128)(2,1)S(1)} %convolution_convert_fusion.3.refs_2_, ...), custom_call_target="tpu_custom_call" | custom-call | tf_op jit(solution)/shard_map/pallas_call | solution.py:261
  282.0 6.6 conditional.6
  282.0 6.1 pad_maximum_fusion.32
  288.6 13.8 %multiply_convert_fusion.1 = (bf16[768,4096]{1,0:T(8,128)(2,1)}, f32[768,4096]{1,0:T(8,128)}) fusion(bf16[1024,4096]{1,0:T(8,128)(2,1)} %get-tuple-element.630, f32[768,1024]{1,0:T(8,128)S(1)} %get-tuple-element.587, f32[1024]{0:T(1024)S(1)} %bitcast.785, f32[1024]{0:T(1024)S(1)} %bitcast.774, f32[768]{0:T(1024)S(1)} %add_rsqrt_fusion.1, ...), kind=kOutput, calls=%fused_computation.167 | convolution fusion | flops 6462111744 | bytes 30423040 | tf_op jit(solution)/shard_map/...i,ij->...j/dot_general | solution.py:408
  302.4 6.6 conditional.7
  302.4 6.5 pad_maximum_fusion.36
  309.0 11.3 %fusion.144 = (f32[768]{0:T(1024)S(1)}, f32[768,1024]{1,0:T(8,128)S(1)}) fusion(bf16[768,4096]{1,0:T(8,128)(2,1)} %get-tuple-element.588, bf16[4096,1024]{1,0:T(8,128)(2,1)} %get-tuple-element.631, f32[1024]{0:T(1024)S(1)} %bitcast.786, f32[1024]{0:T(1024)S(1)} %bitcast.775, f32[768]{0:T(1024)S(1)} %add_rsqrt_fusion.1, ...), kind=kOutput, calls=%fused_computation.459 | convolution fusion | flops 6447168512 | bytes 20988928 | tf_op jit(solution)/shard_map/...i,ij->...j/dot_general | solution.py:408
  326.4 7.1 convolution_convert_fusion.1
  338.3 13.8 %multiply_convert_fusion = bf16[768,4096]{1,0:T(8,128)(2,1)S(1)} fusion(bf16[768,1024]{1,0:T(8,128)(2,1)} %copy-done.93, bf16[4096,1024]{1,0:T(8,128)(2,1)} %get-tuple-element.631, f32[768,4096]{1,0:T(8,128)} %get-tuple-element.589), kind=kOutput, calls=%fused_computation.166 | convolution fusion | flops 6480199680 | bytes 28835840 | tf_op jit(solution)/shard_map/...j,ij->...i/dot_general | solution.py:412
  352.1 6.6 fusion.6
  360.4 7.9 convolution_convert_fusion
  373.2 7.0 collective-permute-start.26
  380.2 12.5 %multiply_reduce_fusion = (f32[1024]{0:T(1024)S(1)}, f32[768]{0:T(1024)S(1)}, f32[768]{0:T(1024)S(1)}, f32[1024]{0:T(1024)S(1)}, f32[768,1024]{1,0:T(8,128)S(1)}) fusion(f32[768,1024]{1,0:T(8,128)S(1)} %get-tuple-element.587, f32[768]{0:T(1024)S(1)} %add_rsqrt_fusion.1, f32[768]{0:T(1024)S(1)} %broadcast_multiply_fusion.7, f32[1024]{0:T(1024)S(1)} %bitcast.777, ...), kind=kOutput, calls=%fused_computation.218 | convolution fusion | flops 6450311168 | bytes 24141824 | tf_op jit(solution)/shard_map/...j,ij->...i/dot_general | solution.py:412
  398.6 5.0 fusion.5
  409.2 38.4 %shard_map.222 = (bf16[2,3,128,1024]{3,2,1,0:T(8,128)(2,1)S(1)}, bf16[8,2,128,1024]{3,2,1,0:T(8,128)(2,1)S(1)}, bf16[8,2,128,1024]{3,2,1,0:T(8,128)(2,1)S(1)}) custom-call(s32[2,3]{1,0:T(2,128)S(1)} %get-tuple-element.582.refs_0_, bf16[2,3,128,1024]{3,2,1,0:T(8,128)(2,1)S(1)} %bitcast.711, bf16[8,2,128,1024]{3,2,1,0:T(8,128)(2,1)S(1)} %copy-done.2, ...), custom_call_target="tpu_custom_call" | custom-call | tf_op jit(solution)/shard_map/pallas_call | solution.py:306
  455.0 5.8 convolution_convert_fusion.6
  463.1 7.5 fusion.47
  470.6 8.5 add_convert_fusion.2
  490.1 4.9 convolution_convert_fusion.7
  507.9 7.4 collective-permute-start.31
  517.3 10.3 %collective-permute-done.28 = bf16[4,1,128,1024]{3,2,0,1:T(8,128)(2,1)S(1)} collective-permute-done((bf16[4,1,128,1024]{3,2,0,1:T(8,128)(2,1)}, bf16[4,1,128,1024]{3,2,0,1:T(8,128)(2,1)S(1)}, u32[]{:S(2)}, u32[]{:S(2)}) %collective-permute-start.28) | collective-permute-done | bytes 1048608 | tf_op jit(solution)/shard_map/ppermute | solution.py:422
  527.6 7.2 collective-permute-start.29
  538.5 9.7 %add_convert_fusion = bf16[2,8,5,32,1024]{4,3,2,1,0:T(8,128)(2,1)} fusion(bf16[2,8,5,32,1024]{4,3,2,1,0:T(8,128)(2,1)} %copy-done.51, bf16[2,8,5,32,1024]{4,3,2,1,0:T(8,128)(2,1)} %get-tuple-element.552), kind=kLoop, calls=%fused_computation.169 | loop fusion | flops 10485760 | bytes 15728640 | tf_op jit(solution)/shard_map/convert_element_type | solution.py:455
  552.1 33.8 %shard_map.223 = (bf16[2,3,128,1024]{3,2,1,0:T(8,128)(2,1)S(1)}, bf16[8,2,128,1024]{3,2,1,0:T(8,128)(2,1)S(1)}, bf16[8,2,128,1024]{3,2,1,0:T(8,128)(2,1)S(1)}, b...) custom-call(s32[2,3]{1,0:T(2,128)S(1)} %copy-done.25, ...), custom_call_target="tpu_custom_call" | custom-call | tf_op jit(solution)/shard_map/pallas_call | solution.py:306
  594.3 6.5 add_convert_fusion.1
  608.9 5.2 fusion.9
  615.7 4.8 fusion.10
  626.9 18.0 %collective-permute-start.56 = (bf16[1,128,1024]{2,1,0:T(8,128)(2,1)}, bf16[1,128,1024]{2,1,0:T(8,128)(2,1)}, u32[]{:S(2)}, u32[]{:S(2)}) collective-permute-start(bf16[1,128,1024]{2,1,0:T(8,128)(2,1)} %get-tuple-element.563), channel_id=1, source_target_pairs={{0,6},{1,7},{2,4},{3,5},{4,2},{5,3},{6,0},{7,1},{8,14},{9,15},{10,... | collective-permute-start | bytes 786440 | tf_op jit(solution)/shard_map/ppermute | solution.py:427
  652.3 16.6 %collective-permute-done.55 = bf16[1,128,1024]{2,1,0:T(8,128)(2,1)} collective-permute-done((bf16[1,128,1024]{2,1,0:T(8,128)(2,1)}, bf16[1,128,1024]{2,1,0:T(8,128)(2,1)}, u32[]{:S(2)}, u32[]{:S(2)}) %collective-permute-start.55) | collective-permute-done | bytes 262176 | tf_op jit(solution)/shard_map/ppermute | solution.py:427
  682.8 6.6 fusion.60
  698.3 36.6 %collective-permute-done.46 = f32[7,1024]{1,0:T(8,128)S(1)} collective-permute-done((f32[7,1024]{1,0:T(8,128)S(1)}, f32[7,1024]{1,0:T(8,128)S(1)}, u32[]{:S(2)}, u32[]{:S(2)}) %collective-permute-start.46) | collective-permute-done | bytes 28704 | tf_op jit(solution)/shard_map/ppermute | solution.py:422
  751.5 16.3 %collective-permute-done.40 = bf16[8,3,32,1024]{3,2,1,0:T(8,128)(2,1)S(1)} collective-permute-done((bf16[8,3,32,1024]{3,2,1,0:T(8,128)(2,1)S(1)}, bf16[8,3,32,1024]{3,2,1,0:T(8,128)(2,1)S(1)}, u32[]{:S(2)}, u32[]{:S(2)}) %collective-permute-start.40) | collective-permute-done | bytes 1572896 | tf_op jit(solution)/shard_map/ppermute | solution.py:422
  777.9 9.9 %collective-permute-done.52 = bf16[1,32,4096]{2,1,0:T(8,128)(2,1)} collective-permute-done((bf16[1,32,4096]{2,1,0:T(8,128)(2,1)}, bf16[1,32,4096]{2,1,0:T(8,128)(2,1)}, u32[]{:S(2)}, u32[]{:S(2)}) %collective-permute-start.52) | collective-permute-done | bytes 262176 | tf_op jit(solution)/shard_map/ppermute | solution.py:427
  797.7 25.2 %collective-permute-done.41 = bf16[4,8,32,1024]{3,2,1,0:T(8,128)(2,1)} collective-permute-done((bf16[4,8,32,1024]{3,2,1,0:T(8,128)(2,1)}, bf16[4,8,32,1024]{3,2,1,0:T(8,128)(2,1)}, u32[]{:S(2)}, u32[]{:S(2)}) %collective-permute-start.41) | collective-permute-done | bytes 2097184 | tf_op jit(solution)/shard_map/ppermute | solution.py:427
  830.2 31.8 %collective-permute-done.36 = bf16[2,128,1024]{2,1,0:T(8,128)(2,1)S(1)} collective-permute-done((bf16[2,128,1024]{2,1,0:T(8,128)(2,1)S(1)}, bf16[2,128,1024]{2,1,0:T(8,128)(2,1)S(1)}, u32[]{:S(2)}, u32[]{:S(2)}) %collective-permute-start.36) | collective-permute-done | bytes 524320 | tf_op jit(solution)/shard_map/ppermute | solution.py:427
  864.8 17.0 %collective-permute-done.43 = bf16[8,32,1024]{2,1,0:T(8,128)(2,1)S(1)} collective-permute-done((bf16[8,32,1024]{2,1,0:T(8,128)(2,1)S(1)}, bf16[8,32,1024]{2,1,0:T(8,128)(2,1)S(1)}, u32[]{:S(2)}, u32[]{:S(2)}) %collective-permute-start.43) | collective-permute-done | bytes 524320 | tf_op jit(solution)/shard_map/ppermute | solution.py:427
  (525 shorter events, 293.5 us)
Async XLA Ops:
  2.5 32.1 %collective-permute-start.3 = (bf16[2,128,1024]{2,1,0:T(8,128)(2,1)}, bf16[2,128,1024]{2,1,0:T(8,128)(2,1)}, u32[]{:S(2)}, u32[]{:S(2)}) collective-permute-start(bf16[2,128,1024]{2,1,0:T(8,128)(2,1)} %slice_bitcast_fusion.130), channel_id=1, source_target_pairs={{0,2},{1,3},{2,0},{3,1},{4,6},{5,7},{6,4},{7,5},{8,10},{9,11},{10,... | collective-permute-start | bytes 1572872 | tf_op jit(solution)/shard_map/ppermute | solution.py:427
  5.6 29.0 %collective-permute-start.4 = (bf16[2,128,1024]{2,1,0:T(8,128)(2,1)}, bf16[2,128,1024]{2,1,0:T(8,128)(2,1)}, u32[]{:S(2)}, u32[]{:S(2)}) collective-permute-start(bf16[2,128,1024]{2,1,0:T(8,128)(2,1)} %slice_bitcast_fusion.130), channel_id=1, source_target_pairs={{0,4},{1,5},{2,6},{3,7},{4,0},{5,1},{6,2},{7,3},{8,12},{9,13},{10,... | collective-permute-start | bytes 1572872 | tf_op jit(solution)/shard_map/ppermute | solution.py:427
  8.1 46.5 %collective-permute-start.6 = (bf16[2,128,1024]{2,1,0:T(8,128)(2,1)}, bf16[2,128,1024]{2,1,0:T(8,128)(2,1)}, u32[]{:S(2)}, u32[]{:S(2)}) collective-permute-start(bf16[2,128,1024]{2,1,0:T(8,128)(2,1)} %slice_bitcast_fusion.130), channel_id=1, source_target_pairs={{0,1},{1,0},{2,3},{3,2},{4,5},{5,4},{6,7},{7,6},{8,9},{9,8},{10,11... | collective-permute-start | bytes 1572872 | tf_op jit(solution)/shard_map/ppermute | solution.py:427
  11.8 35.5 %collective-permute-start.1 = (bf16[3,256,1024]{2,1,0:T(8,128)(2,1)S(1)}, bf16[3,256,1024]{2,1,0:T(8,128)(2,1)}, u32[]{:S(2)}, u32[]{:S(2)}) collective-permute-start(bf16[3,256,1024]{2,1,0:T(8,128)(2,1)S(1)} %convert_element_type.639), channel_id=1, source_target_pairs={{0,16},{8,24},{16,0},{24,8},{1,17},{9,25},{17,1},{25,9},{2,18},{10... | collective-permute-start | bytes 4718600 | tf_op jit(solution)/shard_map/ppermute | solution.py:422
  13.3 35.8 %collective-permute-start.13 = (bf16[2,128,1024]{2,1,0:T(8,128)(2,1)}, bf16[2,128,1024]{2,1,0:T(8,128)(2,1)}, u32[]{:S(2)}, u32[]{:S(2)}) collective-permute-start(bf16[2,128,1024]{2,1,0:T(8,128)(2,1)} %param.30), channel_id=1, source_target_pairs={{0,1},{1,0},{2,3},{3,2},{4,5},{5,4},{6,7},{7,6},{8,9},{9,8},{10,11... | collective-permute-start | bytes 1572872 | tf_op jit(solution)/shard_map/ppermute | solution.py:427
  34.6 53.9 %collective-permute-start = (bf16[3,256,1024]{2,1,0:T(8,128)(2,1)S(1)}, bf16[3,256,1024]{2,1,0:T(8,128)(2,1)S(1)}, u32[]{:S(2)}, u32[]{:S(2)}) collective-permute-start(bf16[3,256,1024]{2,1,0:T(8,128)(2,1)S(1)} %convert_element_type.639), channel_id=1, source_target_pairs={{0,8},{8,0},{16,24},{24,16},{1,9},{9,1},{17,25},{25,17},{2,10},{10... | collective-permute-start | bytes 4718600 | tf_op jit(solution)/shard_map/ppermute | solution.py:417
  47.3 41.3 %collective-permute-start.2 = (bf16[3,256,1024]{2,1,0:T(8,128)(2,1)}, bf16[3,256,1024]{2,1,0:T(8,128)(2,1)S(1)}, u32[]{:S(2)}, u32[]{:S(2)}) collective-permute-start(bf16[3,256,1024]{2,1,0:T(8,128)(2,1)} %collective-permute-done.1), channel_id=1, source_target_pairs={{0,8},{8,0},{16,24},{24,16},{1,9},{9,1},{17,25},{25,17},{2,10},{10... | collective-permute-start | bytes 4718600 | tf_op jit(solution)/shard_map/ppermute | solution.py:417
  52.3 23.0 %collective-permute-start.8 = (bf16[2,128,1024]{2,1,0:T(8,128)(2,1)}, bf16[2,128,1024]{2,1,0:T(8,128)(2,1)S(1)}, u32[]{:S(2)}, u32[]{:S(2)}) collective-permute-start(bf16[2,128,1024]{2,1,0:T(8,128)(2,1)} %collective-permute-done.4), channel_id=1, source_target_pairs={{0,1},{1,0},{2,3},{3,2},{4,5},{5,4},{6,7},{7,6},{8,9},{9,8},{10,11... | collective-permute-start | bytes 1572872 | tf_op jit(solution)/shard_map/ppermute | solution.py:427
  54.6 31.5 %collective-permute-start.9 = (bf16[2,128,1024]{2,1,0:T(8,128)(2,1)S(1)}, bf16[2,128,1024]{2,1,0:T(8,128)(2,1)S(1)}, u32[]{:S(2)}, u32[]{:S(2)}) collective-permute-start(bf16[2,128,1024]{2,1,0:T(8,128)(2,1)S(1)} %collective-permute-done.5), channel_id=1, source_target_pairs={{0,1},{1,0},{2,3},{3,2},{4,5},{5,4},{6,7},{7,6},{8,9},{9,8},{10,11... | collective-permute-start | bytes 1572872 | tf_op jit(solution)/shard_map/ppermute | solution.py:427
  64.1 147.9 %collective-permute-start.10 = (bf16[5,256,1024]{2,1,0:T(8,128)(2,1)}, bf16[5,256,1024]{2,1,0:T(8,128)(2,1)}, u32[]{:S(2)}, u32[]{:S(2)}) collective-permute-start(bf16[5,256,1024]{2,1,0:T(8,128)(2,1)} %pad_maximum_fusion.43), channel_id=1, source_target_pairs={{0,8},{8,0},{16,24},{24,16},{1,9},{9,1},{17,25},{25,17},{2,10},{10... | collective-permute-start | bytes 7864328 | tf_op jit(solution)/shard_map/ppermute | solution.py:417
  75.3 84.4 %collective-permute-start.16 = (bf16[2,2,128,1024]{3,2,1,0:T(8,128)(2,1)}, bf16[2,2,128,1024]{3,2,1,0:T(8,128)(2,1)}, u32[]{:S(2)}, u32[]{:S(2)}) collective-permute-start(bf16[2,2,128,1024]{3,2,1,0:T(8,128)(2,1)} %get-tuple-element.304), channel_id=1, source_target_pairs={{0,6},{1,7},{2,4},{3,5},{4,2},{5,3},{6,0},{7,1},{8,14},{9,15},{10,... | collective-permute-start | bytes 3145736 | tf_op jit(solution)/shard_map/ppermute | solution.py:427
  87.0 58.9 %collective-permute-start.11 = (bf16[5,256,1024]{2,1,0:T(8,128)(2,1)}, bf16[5,256,1024]{2,1,0:T(8,128)(2,1)}, u32[]{:S(2)}, u32[]{:S(2)}) collective-permute-start(bf16[5,256,1024]{2,1,0:T(8,128)(2,1)} %pad_maximum_fusion.43), channel_id=1, source_target_pairs={{0,16},{8,24},{16,0},{24,8},{1,17},{9,25},{17,1},{25,9},{2,18},{10... | collective-permute-start | bytes 7864328 | tf_op jit(solution)/shard_map/ppermute | solution.py:422
  145.9 66.0 %collective-permute-start.12 = (bf16[5,256,1024]{2,1,0:T(8,128)(2,1)}, bf16[5,256,1024]{2,1,0:T(8,128)(2,1)}, u32[]{:S(2)}, u32[]{:S(2)}) collective-permute-start(bf16[5,256,1024]{2,1,0:T(8,128)(2,1)} %collective-permute-done.11), channel_id=1, source_target_pairs={{0,8},{8,0},{16,24},{24,16},{1,9},{9,1},{17,25},{25,17},{2,10},{10... | collective-permute-start | bytes 7864328 | tf_op jit(solution)/shard_map/ppermute | solution.py:417
  147.6 63.0 %collective-permute-start.18 = (bf16[1,256,4096]{2,1,0:T(8,128)(2,1)}, bf16[1,256,4096]{2,1,0:T(8,128)(2,1)}, u32[]{:S(2)}, u32[]{:S(2)}) collective-permute-start(bf16[1,256,4096]{2,1,0:T(8,128)(2,1)} %convert_bitcast_fusion.3), channel_id=1, source_target_pairs={{0,16},{8,24},{16,0},{24,8},{1,17},{9,25},{17,1},{25,9},{2,18},{10... | collective-permute-start | bytes 6291464 | tf_op jit(solution)/shard_map/ppermute | solution.py:422
  156.4 49.8 %collective-permute-start.15 = (bf16[2,2,128,1024]{3,2,1,0:T(8,128)(2,1)}, bf16[2,2,128,1024]{3,2,1,0:T(8,128)(2,1)}, u32[]{:S(2)}, u32[]{:S(2)}) collective-permute-start(bf16[2,2,128,1024]{3,2,1,0:T(8,128)(2,1)} %get-tuple-element.304), channel_id=1, source_target_pairs={{0,4},{1,5},{2,6},{3,7},{4,0},{5,1},{6,2},{7,3},{8,12},{9,13},{10,... | collective-permute-start | bytes 3145736 | tf_op jit(solution)/shard_map/ppermute | solution.py:427
  159.7 47.2 %collective-permute-start.14 = (bf16[2,2,128,1024]{3,2,1,0:T(8,128)(2,1)}, bf16[2,2,128,1024]{3,2,1,0:T(8,128)(2,1)}, u32[]{:S(2)}, u32[]{:S(2)}) collective-permute-start(bf16[2,2,128,1024]{3,2,1,0:T(8,128)(2,1)} %get-tuple-element.304), channel_id=1, source_target_pairs={{0,2},{1,3},{2,0},{3,1},{4,6},{5,7},{6,4},{7,5},{8,10},{9,11},{10,... | collective-permute-start | bytes 3145736 | tf_op jit(solution)/shard_map/ppermute | solution.py:427
  206.2 75.0 %collective-permute-start.17 = (bf16[1,256,4096]{2,1,0:T(8,128)(2,1)}, bf16[1,256,4096]{2,1,0:T(8,128)(2,1)}, u32[]{:S(2)}, u32[]{:S(2)}) collective-permute-start(bf16[1,256,4096]{2,1,0:T(8,128)(2,1)} %convert_bitcast_fusion.3), channel_id=1, source_target_pairs={{0,8},{8,0},{16,24},{24,16},{1,9},{9,1},{17,25},{25,17},{2,10},{10... | collective-permute-start | bytes 6291464 | tf_op jit(solution)/shard_map/ppermute | solution.py:417
  206.9 95.5 %collective-permute-start.20 = (bf16[1,1024,1024]{2,1,0:T(8,128)(2,1)}, bf16[1,1024,1024]{2,1,0:T(8,128)(2,1)}, u32[]{:S(2)}, u32[]{:S(2)}) collective-permute-start(bf16[1,1024,1024]{2,1,0:T(8,128)(2,1)} %convert_bitcast_fusion), channel_id=1, source_target_pairs={{0,8},{8,0},{16,24},{24,16},{1,9},{9,1},{17,25},{25,17},{2,10},{10... | collective-permute-start | bytes 6291464 | tf_op jit(solution)/shard_map/ppermute | solution.py:417
  210.6 69.8 %collective-permute-start.21 = (bf16[1,1024,1024]{2,1,0:T(8,128)(2,1)}, bf16[1,1024,1024]{2,1,0:T(8,128)(2,1)}, u32[]{:S(2)}, u32[]{:S(2)}) collective-permute-start(bf16[1,1024,1024]{2,1,0:T(8,128)(2,1)} %convert_bitcast_fusion), channel_id=1, source_target_pairs={{0,16},{8,24},{16,0},{24,8},{1,17},{9,25},{17,1},{25,9},{2,18},{10... | collective-permute-start | bytes 6291464 | tf_op jit(solution)/shard_map/ppermute | solution.py:422
  239.0 42.2 %collective-permute-start.19 = (bf16[1,256,4096]{2,1,0:T(8,128)(2,1)}, bf16[1,256,4096]{2,1,0:T(8,128)(2,1)S(1)}, u32[]{:S(2)}, u32[]{:S(2)}) collective-permute-start(bf16[1,256,4096]{2,1,0:T(8,128)(2,1)} %collective-permute-done.18), channel_id=1, source_target_pairs={{0,8},{8,0},{16,24},{24,16},{1,9},{9,1},{17,25},{25,17},{2,10},{10... | collective-permute-start | bytes 6291464 | tf_op jit(solution)/shard_map/ppermute | solution.py:417
  280.4 22.0 %collective-permute-start.22 = (bf16[1,1024,1024]{2,1,0:T(8,128)(2,1)}, bf16[1,1024,1024]{2,1,0:T(8,128)(2,1)}, u32[]{:S(2)}, u32[]{:S(2)}) collective-permute-start(bf16[1,1024,1024]{2,1,0:T(8,128)(2,1)} %collective-permute-done.21), channel_id=1, source_target_pairs={{0,8},{8,0},{16,24},{24,16},{1,9},{9,1},{17,25},{25,17},{2,10},{10... | collective-permute-start | bytes 6291464 | tf_op jit(solution)/shard_map/ppermute | solution.py:417
  372.9 25.7 %collective-permute-start.24 = (bf16[2,8,1,32,4096]{4,3,1,2,0:T(8,128)(2,1)}, bf16[2,8,1,32,4096]{4,3,1,2,0:T(8,128)(2,1)}, u32[]{:S(2)}, u32[]{:S(2)}) collective-permute-start(bf16[2,8,1,32,4096]{4,3,1,2,0:T(8,128)(2,1)} %dynamic-slice_bitcast_fusion), channel_id=1, source_target_pairs={{0,8},{8,0},{16,24},{24,16},{1,9},{9,1},{17,25},{25,17},{2,10},{10... | collective-permute-start | bytes 12582920 | tf_op jit(solution)/shard_map/ppermute | solution.py:417
  373.2 74.4 %collective-permute-start.26 = (bf16[2,4,1,128,1024]{4,3,1,0,2:T(8,128)(2,1)}, bf16[2,4,1,128,1024]{4,3,1,0,2:T(8,128)(2,1)S(1)}, u32[]{:S(2)}, u32[]{:S(2)}) collective-permute-start(bf16[2,4,1,128,1024]{4,3,1,0,2:T(8,128)(2,1)} %dynamic-slice_bitcast_fusion.5), channel_id=1, source_target_pairs={{0,1},{1,0},{2,3},{3,2},{4,5},{5,4},{6,7},{7,6},{8,9},{9,8},{10,11... | collective-permute-start | bytes 6291464 | tf_op jit(solution)/shard_map/ppermute | solution.py:427
  405.2 74.0 %collective-permute-start.25 = (bf16[8,1,32,4096]{3,2,0,1:T(8,128)(2,1)}, bf16[8,1,32,4096]{3,2,0,1:T(8,128)(2,1)}, u32[]{:S(2)}, u32[]{:S(2)}) collective-permute-start(bf16[8,1,32,4096]{3,2,0,1:T(8,128)(2,1)} %dynamic-slice_bitcast_fusion.4), channel_id=1, source_target_pairs={{0,16},{8,24},{16,0},{24,8},{1,17},{9,25},{17,1},{25,9},{2,18},{10... | collective-permute-start | bytes 6291464 | tf_op jit(solution)/shard_map/ppermute | solution.py:422
  499.3 36.9 %collective-permute-start.27 = (bf16[2,8,5,32,1024]{4,3,2,1,0:T(8,128)(2,1)S(1)}, bf16[2,8,5,32,1024]{4,3,2,1,0:T(8,128)(2,1)S(1)}, u32[]{:S(2)}, u32[]{:S(2)}) collective-permute-start(bf16[2,8,5,32,1024]{4,3,2,1,0:T(8,128)(2,1)S(1)} %get-tuple-element.553), channel_id=1, source_target_pairs={{0,8},{8,0},{16,24},{24,16},{1,9},{9,1},{17,25},{25,17},{2,10},{10... | collective-permute-start | bytes 15728648 | tf_op jit(solution)/shard_map/ppermute | solution.py:417
  499.5 28.0 %collective-permute-start.28 = (bf16[4,1,128,1024]{3,2,0,1:T(8,128)(2,1)}, bf16[4,1,128,1024]{3,2,0,1:T(8,128)(2,1)S(1)}, u32[]{:S(2)}, u32[]{:S(2)}) collective-permute-start(bf16[4,1,128,1024]{3,2,0,1:T(8,128)(2,1)} %dynamic-slice_bitcast_fusion.14), channel_id=1, source_target_pairs={{0,16},{8,24},{16,0},{24,8},{1,17},{9,25},{17,1},{25,9},{2,18},{10... | collective-permute-start | bytes 3145736 | tf_op jit(solution)/shard_map/ppermute | solution.py:422
  505.8 95.0 %collective-permute-start.32 = (bf16[2,2,128,1024]{3,2,1,0:T(8,128)(2,1)}, bf16[2,2,128,1024]{3,2,1,0:T(8,128)(2,1)S(1)}, u32[]{:S(2)}, u32[]{:S(2)}) collective-permute-start(bf16[2,2,128,1024]{3,2,1,0:T(8,128)(2,1)} %get-tuple-element.538), channel_id=1, source_target_pairs={{0,6},{1,7},{2,4},{3,5},{4,2},{5,3},{6,0},{7,1},{8,14},{9,15},{10,... | collective-permute-start | bytes 3145736 | tf_op jit(solution)/shard_map/ppermute | solution.py:427
  507.9 92.9 %collective-permute-start.31 = (bf16[2,2,128,1024]{3,2,1,0:T(8,128)(2,1)}, bf16[2,2,128,1024]{3,2,1,0:T(8,128)(2,1)}, u32[]{:S(2)}, u32[]{:S(2)}) collective-permute-start(bf16[2,2,128,1024]{3,2,1,0:T(8,128)(2,1)} %get-tuple-element.537), channel_id=1, source_target_pairs={{0,4},{1,5},{2,6},{3,7},{4,0},{5,1},{6,2},{7,3},{8,12},{9,13},{10,... | collective-permute-start | bytes 3145736 | tf_op jit(solution)/shard_map/ppermute | solution.py:427
  515.4 85.5 %collective-permute-start.30 = (bf16[2,2,128,1024]{3,2,1,0:T(8,128)(2,1)}, bf16[2,2,128,1024]{3,2,1,0:T(8,128)(2,1)}, u32[]{:S(2)}, u32[]{:S(2)}) collective-permute-start(bf16[2,2,128,1024]{3,2,1,0:T(8,128)(2,1)} %get-tuple-element.536), channel_id=1, source_target_pairs={{0,2},{1,3},{2,0},{3,1},{4,6},{5,7},{6,4},{7,5},{8,10},{9,11},{10,... | collective-permute-start | bytes 3145736 | tf_op jit(solution)/shard_map/ppermute | solution.py:427
  527.6 64.1 %collective-permute-start.29 = (bf16[4,1,32,4096]{3,2,0,1:T(8,128)(2,1)}, bf16[4,1,32,4096]{3,2,0,1:T(8,128)(2,1)}, u32[]{:S(2)}, u32[]{:S(2)}) collective-permute-start(bf16[4,1,32,4096]{3,2,0,1:T(8,128)(2,1)} %dynamic-slice_bitcast_fusion.13), channel_id=1, source_target_pairs={{0,1},{1,0},{2,3},{3,2},{4,5},{5,4},{6,7},{7,6},{8,9},{9,8},{10,11... | collective-permute-start | bytes 3145736 | tf_op jit(solution)/shard_map/ppermute | solution.py:427
  624.9 67.4 %collective-permute-start.34 = (bf16[2,8,3,32,1024]{4,3,2,1,0:T(8,128)(2,1)}, bf16[2,8,3,32,1024]{4,3,2,1,0:T(8,128)(2,1)}, u32[]{:S(2)}, u32[]{:S(2)}) collective-permute-start(bf16[2,8,3,32,1024]{4,3,2,1,0:T(8,128)(2,1)} %pad_maximum_fusion.42), channel_id=1, source_target_pairs={{0,8},{8,0},{16,24},{24,16},{1,9},{9,1},{17,25},{25,17},{2,10},{10... | collective-permute-start | bytes 9437192 | tf_op jit(solution)/shard_map/ppermute | solution.py:417
  626.9 25.5 %collective-permute-start.56 = (bf16[1,128,1024]{2,1,0:T(8,128)(2,1)}, bf16[1,128,1024]{2,1,0:T(8,128)(2,1)}, u32[]{:S(2)}, u32[]{:S(2)}) collective-permute-start(bf16[1,128,1024]{2,1,0:T(8,128)(2,1)} %get-tuple-element.563), channel_id=1, source_target_pairs={{0,6},{1,7},{2,4},{3,5},{4,2},{5,3},{6,0},{7,1},{8,14},{9,15},{10,... | collective-permute-start | bytes 786440 | tf_op jit(solution)/shard_map/ppermute | solution.py:427
  644.8 24.1 %collective-permute-start.55 = (bf16[1,128,1024]{2,1,0:T(8,128)(2,1)}, bf16[1,128,1024]{2,1,0:T(8,128)(2,1)}, u32[]{:S(2)}, u32[]{:S(2)}) collective-permute-start(bf16[1,128,1024]{2,1,0:T(8,128)(2,1)} %get-tuple-element.564), channel_id=1, source_target_pairs={{0,4},{1,5},{2,6},{3,7},{4,0},{5,1},{6,2},{7,3},{8,12},{9,13},{10,... | collective-permute-start | bytes 786440 | tf_op jit(solution)/shard_map/ppermute | solution.py:427
  674.3 74.1 %collective-permute-start.39 = (bf16[8,5,32,1024]{3,2,1,0:T(8,128)(2,1)}, bf16[8,5,32,1024]{3,2,1,0:T(8,128)(2,1)}, u32[]{:S(2)}, u32[]{:S(2)}) collective-permute-start(bf16[8,5,32,1024]{3,2,1,0:T(8,128)(2,1)} %dynamic-slice_bitcast_fusion.2), channel_id=1, source_target_pairs={{0,16},{8,24},{16,0},{24,8},{1,17},{9,25},{17,1},{25,9},{2,18},{10... | collective-permute-start | bytes 7864328 | tf_op jit(solution)/shard_map/ppermute | solution.py:422
  674.3 71.2 %collective-permute-start.33 = (bf16[4,2,128,1024]{3,2,1,0:T(8,128)(2,1)}, bf16[4,2,128,1024]{3,2,1,0:T(8,128)(2,1)}, u32[]{:S(2)}, u32[]{:S(2)}) collective-permute-start(bf16[4,2,128,1024]{3,2,1,0:T(8,128)(2,1)} %slice.545), channel_id=1, source_target_pairs={{0,1},{1,0},{2,3},{3,2},{4,5},{5,4},{6,7},{7,6},{8,9},{9,8},{10,11... | collective-permute-start | bytes 6291464 | tf_op jit(solution)/shard_map/ppermute | solution.py:427
  690.3 44.6 %collective-permute-start.46 = (f32[7,1024]{1,0:T(8,128)S(1)}, f32[7,1024]{1,0:T(8,128)S(1)}, u32[]{:S(2)}, u32[]{:S(2)}) collective-permute-start(f32[7,1024]{1,0:T(8,128)S(1)} %add.670), channel_id=1, source_target_pairs={{0,16},{8,24},{16,0},{24,8},{1,17},{9,25},{17,1},{25,9},{2,18},{10... | collective-permute-start | bytes 86024 | tf_op jit(solution)/shard_map/ppermute | solution.py:422
  695.6 72.1 %collective-permute-start.40 = (bf16[8,3,32,1024]{3,2,1,0:T(8,128)(2,1)S(1)}, bf16[8,3,32,1024]{3,2,1,0:T(8,128)(2,1)S(1)}, u32[]{:S(2)}, u32[]{:S(2)}) collective-permute-start(bf16[8,3,32,1024]{3,2,1,0:T(8,128)(2,1)S(1)} %dynamic-slice_bitcast_fusion.6), channel_id=1, source_target_pairs={{0,16},{8,24},{16,0},{24,8},{1,17},{9,25},{17,1},{25,9},{2,18},{10... | collective-permute-start | bytes 4718600 | tf_op jit(solution)/shard_map/ppermute | solution.py:422
  735.8 59.8 %collective-permute-start.38 = (bf16[2,128,1024]{2,1,0:T(8,128)(2,1)}, bf16[2,128,1024]{2,1,0:T(8,128)(2,1)}, u32[]{:S(2)}, u32[]{:S(2)}) collective-permute-start(bf16[2,128,1024]{2,1,0:T(8,128)(2,1)} %slice_bitcast_fusion.124), channel_id=1, source_target_pairs={{0,1},{1,0},{2,3},{3,2},{4,5},{5,4},{6,7},{7,6},{8,9},{9,8},{10,11... | collective-permute-start | bytes 1572872 | tf_op jit(solution)/shard_map/ppermute | solution.py:427
  739.2 38.7 %collective-permute-start.53 = (bf16[1,32,4096]{2,1,0:T(8,128)(2,1)}, bf16[1,32,4096]{2,1,0:T(8,128)(2,1)}, u32[]{:S(2)}, u32[]{:S(2)}) collective-permute-start(bf16[1,32,4096]{2,1,0:T(8,128)(2,1)} %get-tuple-element.566), channel_id=1, source_target_pairs={{0,6},{1,7},{2,4},{3,5},{4,2},{5,3},{6,0},{7,1},{8,14},{9,15},{10,... | collective-permute-start | bytes 786440 | tf_op jit(solution)/shard_map/ppermute | solution.py:427
  745.5 27.6 %collective-permute-start.50 = (f32[7,1024]{1,0:T(8,128)S(1)}, f32[7,1024]{1,0:T(8,128)S(1)}, u32[]{:S(2)}, u32[]{:S(2)}) collective-permute-start(f32[7,1024]{1,0:T(8,128)S(1)} %add.672), channel_id=1, source_target_pairs={{0,6},{1,7},{2,4},{3,5},{4,2},{5,3},{6,0},{7,1},{8,14},{9,15},{10,... | collective-permute-start | bytes 86024 | tf_op jit(solution)/shard_map/ppermute | solution.py:427
  748.3 28.1 %collective-permute-start.49 = (f32[7,1024]{1,0:T(8,128)S(1)}, f32[7,1024]{1,0:T(8,128)S(1)}, u32[]{:S(2)}, u32[]{:S(2)}) collective-permute-start(f32[7,1024]{1,0:T(8,128)S(1)} %add.672), channel_id=1, source_target_pairs={{0,4},{1,5},{2,6},{3,7},{4,0},{5,1},{6,2},{7,3},{8,12},{9,13},{10,... | collective-permute-start | bytes 86024 | tf_op jit(solution)/shard_map/ppermute | solution.py:427
  776.4 46.5 %collective-permute-start.41 = (bf16[4,8,32,1024]{3,2,1,0:T(8,128)(2,1)}, bf16[4,8,32,1024]{3,2,1,0:T(8,128)(2,1)}, u32[]{:S(2)}, u32[]{:S(2)}) collective-permute-start(bf16[4,8,32,1024]{3,2,1,0:T(8,128)(2,1)} %dynamic-slice_bitcast_fusion.3), channel_id=1, source_target_pairs={{0,1},{1,0},{2,3},{3,2},{4,5},{5,4},{6,7},{7,6},{8,9},{9,8},{10,11... | collective-permute-start | bytes 6291464 | tf_op jit(solution)/shard_map/ppermute | solution.py:427
  791.1 37.9 %collective-permute-start.37 = (bf16[2,128,1024]{2,1,0:T(8,128)(2,1)S(1)}, bf16[2,128,1024]{2,1,0:T(8,128)(2,1)S(1)}, u32[]{:S(2)}, u32[]{:S(2)}) collective-permute-start(bf16[2,128,1024]{2,1,0:T(8,128)(2,1)S(1)} %get-tuple-element.544), channel_id=1, source_target_pairs={{0,6},{1,7},{2,4},{3,5},{4,2},{5,3},{6,0},{7,1},{8,14},{9,15},{10,... | collective-permute-start | bytes 1572872 | tf_op jit(solution)/shard_map/ppermute | solution.py:427
  792.5 69.6 %collective-permute-start.36 = (bf16[2,128,1024]{2,1,0:T(8,128)(2,1)S(1)}, bf16[2,128,1024]{2,1,0:T(8,128)(2,1)S(1)}, u32[]{:S(2)}, u32[]{:S(2)}) collective-permute-start(bf16[2,128,1024]{2,1,0:T(8,128)(2,1)S(1)} %get-tuple-element.545), channel_id=1, source_target_pairs={{0,4},{1,5},{2,6},{3,7},{4,0},{5,1},{6,2},{7,3},{8,12},{9,13},{10,... | collective-permute-start | bytes 1572872 | tf_op jit(solution)/shard_map/ppermute | solution.py:427
  793.3 68.7 %collective-permute-start.35 = (bf16[2,128,1024]{2,1,0:T(8,128)(2,1)S(1)}, bf16[2,128,1024]{2,1,0:T(8,128)(2,1)S(1)}, u32[]{:S(2)}, u32[]{:S(2)}) collective-permute-start(bf16[2,128,1024]{2,1,0:T(8,128)(2,1)S(1)} %get-tuple-element.543), channel_id=1, source_target_pairs={{0,2},{1,3},{2,0},{3,1},{4,6},{5,7},{6,4},{7,5},{8,10},{9,11},{10,... | collective-permute-start | bytes 1572872 | tf_op jit(solution)/shard_map/ppermute | solution.py:427
  825.7 39.0 %collective-permute-start.44 = (bf16[8,32,1024]{2,1,0:T(8,128)(2,1)S(1)}, bf16[8,32,1024]{2,1,0:T(8,128)(2,1)S(1)}, u32[]{:S(2)}, u32[]{:S(2)}) collective-permute-start(bf16[8,32,1024]{2,1,0:T(8,128)(2,1)S(1)} %get-tuple-element.541), channel_id=1, source_target_pairs={{0,6},{1,7},{2,4},{3,5},{4,2},{5,3},{6,0},{7,1},{8,14},{9,15},{10,... | collective-permute-start | bytes 1572872 | tf_op jit(solution)/shard_map/ppermute | solution.py:427
  827.3 54.5 %collective-permute-start.43 = (bf16[8,32,1024]{2,1,0:T(8,128)(2,1)S(1)}, bf16[8,32,1024]{2,1,0:T(8,128)(2,1)S(1)}, u32[]{:S(2)}, u32[]{:S(2)}) collective-permute-start(bf16[8,32,1024]{2,1,0:T(8,128)(2,1)S(1)} %get-tuple-element.542), channel_id=1, source_target_pairs={{0,4},{1,5},{2,6},{3,7},{4,0},{5,1},{6,2},{7,3},{8,12},{9,13},{10,... | collective-permute-start | bytes 1572872 | tf_op jit(solution)/shard_map/ppermute | solution.py:427
  828.9 52.8 %collective-permute-start.42 = (bf16[8,32,1024]{2,1,0:T(8,128)(2,1)S(1)}, bf16[8,32,1024]{2,1,0:T(8,128)(2,1)S(1)}, u32[]{:S(2)}, u32[]{:S(2)}) collective-permute-start(bf16[8,32,1024]{2,1,0:T(8,128)(2,1)S(1)} %get-tuple-element.540), channel_id=1, source_target_pairs={{0,2},{1,3},{2,0},{3,1},{4,6},{5,7},{6,4},{7,5},{8,10},{9,11},{10,... | collective-permute-start | bytes 1572872 | tf_op jit(solution)/shard_map/ppermute | solution.py:427
  (134 other events, 1659.1 us)

commit v3 on v2

--- a/solution.py
+++ b/solution.py
@@ -532,13 +532,13 @@
 
 
 def sum_everywhere(values_in):
-    total = values_in + swap_core(values_in)
-    total = total + swap_chip(total)
-    total = total + swap_block(total, 1)
     blocks = lax.axis_size("blk")
     mine = lax.axis_index("blk") // 2
-    come = jnp.stack([total] + [swap_block(total, 2 * gap) for gap in range(1, blocks // 2)])
-    return sum(pick(come, mine ^ index, 0) for index in range(blocks // 2))
+    come = jnp.stack([values_in] + [swap_block(values_in, 2 * gap) for gap in range(1, blocks // 2)])
+    total = sum(pick(come, mine ^ index, 0) for index in range(blocks // 2))
+    total = total + swap_core(total)
+    total = total + swap_block(total, 1)
+    return total + swap_chip(total)
 
 
 def shards(
@@ -685,14 +685,11 @@
     cross_chip_sent, cross_chip_kept = open_chip(add_low(cross_kept, tie(cross_come, mix_grad)))
     cross_chip_come = swap_chip(cross_chip_sent)
     second_half = add_low(chip_kept, tie(chip_come, mix_grad))
-    g_second = sum_all(*start_exchange(second_half))[0]
     mix_grad = tie(mix_grad, cross_chip_sent, second_half)
     query_grad, key_grad, value_grad, own_key_grad, own_value_grad, tile_grads, own_sums = attend_backward(
         self_bounds, query, main_keys, main_values, attended, mix_grad, self_lse, own, near_tiles, head_size
     )
     first_half = add_low(first_row_kept, tie(first_row_come, query_grad))
-    g_first = sum_all(*start_exchange(first_half))[0]
-    key_grad = tie(key_grad, first_half)
     main_terms = (matmul_t(key_grad, w_qkv[1]) + matmul_t(value_grad, w_qkv[2])).astype(jnp.bfloat16)
     main_kept, main_come = fold_odd(main_terms)
     main_come_from = main_terms
@@ -707,12 +704,18 @@
     ]
     self_sent, self_kept = open_core(self_parts)
     self_come = swap_core(self_sent)
+    main_half = add_low(main_kept, tie(main_come, self_sent))
+    main_back = fold_even(main_half)
+    ffn_half = jnp.concatenate(
+        [half.reshape(half.shape[0], -1, width) for half in (second_half, tie(first_half, main_half))], axis=1
+    )
+    ffn_share = sum_all(*start_exchange(ffn_half))
+    g_second = ffn_share[: second_part.shape[0] // (4 * lax.axis_size("blk"))]
+    g_first = ffn_share[g_second.shape[0] :].reshape(-1, first_part.shape[1])
     local_grad = tall(first_grad) + matmul_t(tie(query_grad, self_sent), w_qkv[0])
     self_chip_sent, self_chip_kept = open_chip(add_low(self_kept, tie(self_come, local_grad)))
     self_chip_come = swap_chip(self_chip_sent)
     own_back = matmul_t(tie(own_key_grad, self_chip_sent), w_qkv[1]) + matmul_t(own_value_grad, w_qkv[2])
-    main_half = add_low(main_kept, tie(main_come, own_back))
-    main_back = fold_even(main_half)
     cross_half = add_low(cross_chip_kept, tie(cross_chip_come, main_half))
     late_sent, late_kept = open_block(
         jnp.concatenate([cross_half, add_low(self_chip_kept, tie(self_chip_come, main_half))], axis=1), 0, 1

time: 885 us -> 900 us (1.017); the launches traced: 884 us -> 889 us
  waiting for transfers between devices: 259 us -> 277 us
  Pallas kernels: 120 us -> 130 us
    ppermute x35 -> x32, waiting for transfers between devices: 173 us -> 211 us  [swap_block(): return lax.ppermute(values_in, 'blk', [(i, i ^ bit) for i in range(size)])]
    ppermute x9, waiting for transfers between devices: 86 us -> 66.7 us  [swap_chip(): return lax.ppermute(values_in, 'dp', [(i, i ^ 2) for i in range(size)])]
    ppermute x35 -> x32, starting transfers between devices: 80 us -> 76.8 us  [swap_block(): return lax.ppermute(values_in, 'blk', [(i, i ^ bit) for i in range(size)])]
    unnamed x264 -> x272, local copies, waits for them, and re-layouts: 46.9 us -> 48.6 us
  transfers between devices with their start and end apart: 57 -> 54, of which waited for: 18 -> 17; matrix products, arithmetic and copies ran while one was open for 31% -> 29% of each run, Pallas kernels for 14% -> 15%
where the time goes in v3:
time: 900 us; the launch traced here: 889 us
  waiting for transfers between devices  277 us (31%)
  matrix products  184 us (20%)
  Pallas kernels  130 us (14%)
  other arithmetic  111 us (12%)
  local copies, waits for them, and re-layouts  96.6 us (11%)
  starting transfers between devices  86.6 us (10%)
    ppermute x32, waiting for transfers between devices, swap_block(): return lax.ppermute(values_in, 'blk', [(i, i ^ bit) for i in range(size)])  211 us
    pallas_call x2, Pallas kernels, attend_backward(): pl.pallas_call(partial(backward_kernel, is_self, rows, near_tiles), grid_...  77.4 us
    ppermute x32, starting transfers between devices, swap_block(): return lax.ppermute(values_in, 'blk', [(i, i ^ bit) for i in range(size)])  76.8 us
    dot_general x12, matrix products, matmul_t(): jnp.einsum('...j,ij->...i', left_side, right_side, preferred_element_type...  69.7 us
    ppermute x9, waiting for transfers between devices, swap_chip(): return lax.ppermute(values_in, 'dp', [(i, i ^ 2) for i in range(size)])  66.7 us
    dot_general x12, matrix products, matmul(): jnp.einsum('...i,ij->...j', left_side, right_side, preferred_element_type...  61.2 us
    pallas_call x2, Pallas kernels, attend_forward(): pl.pallas_call(partial(forward_kernel, is_self, rows, near_tiles), grid_s...  52.3 us
    unnamed x272, local copies, waits for them, and re-layouts  48.6 us
  transfers between devices with their start and end apart: 54, of which 17 were waited for; matrix products, arithmetic and copies ran while one was open for 29% of the time, Pallas kernels for 15%

profile of v3, /device:TPU:0, one launch (start us, length us, event | category | flops | bytes accessed | tf_op | source)
XLA Modules:
  0.0 888.9 jit_solution(7498817984518359256)
XLA Ops:
  36.8 10.4 %collective-permute-done.1 = bf16[3,256,1024]{2,1,0:T(8,128)(2,1)} collective-permute-done((bf16[3,256,1024]{2,1,0:T(8,128)(2,1)S(1)}, bf16[3,256,1024]{2,1,0:T(8,128)(2,1)}, u32[]{:S(2)}, u32[]{:S(2)}) %collective-permute-start.1) | collective-permute-done | bytes 1572896 | tf_op jit(solution)/shard_map/ppermute | solution.py:422
  57.1 7.0 collective-permute-done.7
  64.9 10.4 %collective-permute-done.8 = bf16[2,128,1024]{2,1,0:T(8,128)(2,1)S(1)} collective-permute-done((bf16[2,128,1024]{2,1,0:T(8,128)(2,1)}, bf16[2,128,1024]{2,1,0:T(8,128)(2,1)S(1)}, u32[]{:S(2)}, u32[]{:S(2)}) %collective-permute-start.8) | collective-permute-done | bytes 524320 | tf_op jit(solution)/shard_map/ppermute | solution.py:427
  76.4 9.8 %collective-permute-done.9 = bf16[2,128,1024]{2,1,0:T(8,128)(2,1)S(1)} collective-permute-done((bf16[2,128,1024]{2,1,0:T(8,128)(2,1)S(1)}, bf16[2,128,1024]{2,1,0:T(8,128)(2,1)S(1)}, u32[]{:S(2)}, u32[]{:S(2)}) %collective-permute-start.9) | collective-permute-done | bytes 524320 | tf_op jit(solution)/shard_map/ppermute | solution.py:427
  105.0 4.7 convolution_convert_fusion.4.refs_3_
  109.7 4.7 convolution_convert_fusion.5.refs_2_
  114.5 19.2 %shard_map.220 = (bf16[2,3,128,1024]{3,2,1,0:T(8,128)(2,1)S(1)}, f32[8,2,1,768]{3,2,1,0:T(1,128)S(1)}) custom-call(s32[2,3]{1,0:T(2,128)S(1)} %get-tuple-element.582.refs_0_, bf16[2,3,128,1024]{3,2,1,0:T(8,128)(2,1)S(1)} %fusion.69.refs_1_, bf16[8,2,128,1024]{3,2,1,0:T(8,128)(2,1)S(1)} %convolution_convert_fusion.5.refs_2_, ...), custom_call_target="tpu_custom_call" | custom-call | tf_op jit(solution)/shard_map/pallas_call | solution.py:261
  133.8 12.2 %collective-permute-done.11 = bf16[5,256,1024]{2,1,0:T(8,128)(2,1)} collective-permute-done((bf16[5,256,1024]{2,1,0:T(8,128)(2,1)}, bf16[5,256,1024]{2,1,0:T(8,128)(2,1)}, u32[]{:S(2)}, u32[]{:S(2)}) %collective-permute-start.11) | collective-permute-done | bytes 2621472 | tf_op jit(solution)/shard_map/ppermute | solution.py:422
  166.7 38.9 %collective-permute-done.15 = bf16[2,2,128,1024]{3,2,1,0:T(8,128)(2,1)} collective-permute-done((bf16[2,2,128,1024]{3,2,1,0:T(8,128)(2,1)}, bf16[2,2,128,1024]{3,2,1,0:T(8,128)(2,1)}, u32[]{:S(2)}, u32[]{:S(2)}) %collective-permute-start.15) | collective-permute-done | bytes 1048608 | tf_op jit(solution)/shard_map/ppermute | solution.py:427
  210.3 7.8 conditional.5
  230.3 4.7 convolution_convert_fusion.3.refs_2_
  235.0 4.7 convolution_convert_fusion.2.refs_3_
  239.8 33.2 %shard_map.221 = (bf16[2,3,128,1024]{3,2,1,0:T(8,128)(2,1)S(1)}, f32[8,2,1,768]{3,2,1,0:T(1,128)S(1)}) custom-call(s32[2,3]{1,0:T(2,128)S(1)} %get-tuple-element.581.refs_0_, bf16[2,3,128,1024]{3,2,1,0:T(8,128)(2,1)S(1)} %bitcast.702, bf16[8,2,128,1024]{3,2,1,0:T(8,128)(2,1)S(1)} %convolution_convert_fusion.3.refs_2_, ...), custom_call_target="tpu_custom_call" | custom-call | tf_op jit(solution)/shard_map/pallas_call | solution.py:261
  276.6 6.5 conditional.6
  276.6 6.3 pad_maximum_fusion.32
  283.1 13.9 %multiply_convert_fusion.1 = (bf16[768,4096]{1,0:T(8,128)(2,1)}, f32[768,4096]{1,0:T(8,128)}) fusion(bf16[1024,4096]{1,0:T(8,128)(2,1)} %get-tuple-element.629, f32[768,1024]{1,0:T(8,128)S(1)} %get-tuple-element.586, f32[1024]{0:T(1024)S(1)} %bitcast.779, f32[1024]{0:T(1024)S(1)} %bitcast.768, f32[768]{0:T(1024)S(1)} %add_rsqrt_fusion.1, ...), kind=kOutput, calls=%fused_computation.167 | convolution fusion | flops 6462111744 | bytes 30423040 | tf_op jit(solution)/shard_map/...i,ij->...j/dot_general | solution.py:408
  297.0 6.6 conditional.7
  297.0 6.6 pad_maximum_fusion.36
  303.6 11.3 %fusion.150 = (f32[768]{0:T(1024)S(1)}, f32[768,1024]{1,0:T(8,128)S(1)}) fusion(bf16[768,4096]{1,0:T(8,128)(2,1)} %get-tuple-element.587, bf16[4096,1024]{1,0:T(8,128)(2,1)} %get-tuple-element.630, f32[1024]{0:T(1024)S(1)} %bitcast.780, f32[1024]{0:T(1024)S(1)} %bitcast.769, f32[768]{0:T(1024)S(1)} %add_rsqrt_fusion.1, ...), kind=kOutput, calls=%fused_computation.464 | convolution fusion | flops 6447168512 | bytes 20988928 | tf_op jit(solution)/shard_map/...i,ij->...j/dot_general | solution.py:408
  321.0 7.1 convolution_convert_fusion.1
  332.7 14.0 %multiply_convert_fusion = bf16[768,4096]{1,0:T(8,128)(2,1)S(1)} fusion(bf16[768,1024]{1,0:T(8,128)(2,1)} %copy-done.94, bf16[4096,1024]{1,0:T(8,128)(2,1)} %get-tuple-element.630, f32[768,4096]{1,0:T(8,128)} %get-tuple-element.588), kind=kOutput, calls=%fused_computation.166 | convolution fusion | flops 6480199680 | bytes 28835840 | tf_op jit(solution)/shard_map/...j,ij->...i/dot_general | solution.py:412
  346.7 5.7 fusion.6
  354.2 7.7 convolution_convert_fusion
  367.6 12.5 %multiply_reduce_fusion = (f32[1024]{0:T(1024)S(1)}, f32[768]{0:T(1024)S(1)}, f32[768]{0:T(1024)S(1)}, f32[1024]{0:T(1024)S(1)}, f32[768,1024]{1,0:T(8,128)S(1)}) fusion(f32[768,1024]{1,0:T(8,128)S(1)} %get-tuple-element.586, f32[768]{0:T(1024)S(1)} %add_rsqrt_fusion.1, f32[768]{0:T(1024)S(1)} %broadcast_multiply_fusion.7, f32[1024]{0:T(1024)S(1)} %bitcast.771, ...), kind=kOutput, calls=%fused_computation.218 | convolution fusion | flops 6450311168 | bytes 24141824 | tf_op jit(solution)/shard_map/...j,ij->...i/dot_general | solution.py:412
  386.0 5.0 fusion.5
  396.6 43.4 %shard_map.222 = (bf16[2,3,128,1024]{3,2,1,0:T(8,128)(2,1)S(1)}, bf16[8,2,128,1024]{3,2,1,0:T(8,128)(2,1)S(1)}, bf16[8,2,128,1024]{3,2,1,0:T(8,128)(2,1)S(1)}) custom-call(s32[2,3]{1,0:T(2,128)S(1)} %get-tuple-element.581.refs_0_, bf16[2,3,128,1024]{3,2,1,0:T(8,128)(2,1)S(1)} %bitcast.703, bf16[8,2,128,1024]{3,2,1,0:T(8,128)(2,1)S(1)} %copy-done.2, ...), custom_call_target="tpu_custom_call" | custom-call | tf_op jit(solution)/shard_map/pallas_call | solution.py:306
  446.1 5.8 convolution_convert_fusion.6
  454.2 7.0 fusion.47
  461.2 8.3 add_convert_fusion.2
  480.8 5.2 convolution_convert_fusion.7
  499.8 16.2 %collective-permute-done.28 = bf16[4,1,128,1024]{3,2,0,1:T(8,128)(2,1)S(1)} collective-permute-done((bf16[4,1,128,1024]{3,2,0,1:T(8,128)(2,1)S(1)}, bf16[4,1,128,1024]{3,2,0,1:T(8,128)(2,1)S(1)}, u32[]{:S(2)}, u32[]{:S(2)}) %collective-permute-start.28) | collective-permute-done | bytes 1048608 | tf_op jit(solution)/shard_map/ppermute | solution.py:422
  518.7 9.7 %add_convert_fusion = bf16[2,8,5,32,1024]{4,3,2,1,0:T(8,128)(2,1)} fusion(bf16[2,8,5,32,1024]{4,3,2,1,0:T(8,128)(2,1)} %copy-done.51, bf16[2,8,5,32,1024]{4,3,2,1,0:T(8,128)(2,1)} %get-tuple-element.555), kind=kLoop, calls=%fused_computation.169 | loop fusion | flops 10485760 | bytes 15728640 | tf_op jit(solution)/shard_map/convert_element_type | solution.py:455
  532.2 34.0 %shard_map.223 = (bf16[2,3,128,1024]{3,2,1,0:T(8,128)(2,1)S(1)}, bf16[8,2,128,1024]{3,2,1,0:T(8,128)(2,1)S(1)}, bf16[8,2,128,1024]{3,2,1,0:T(8,128)(2,1)S(1)}, b...) custom-call(s32[2,3]{1,0:T(2,128)S(1)} %copy-done.25, ...), custom_call_target="tpu_custom_call" | custom-call | tf_op jit(solution)/shard_map/pallas_call | solution.py:306
  567.4 4.6 fusion.38
  572.0 6.1 add_convert_fusion.1
  578.2 7.7 collective-permute-done.30
  594.1 5.0 fusion.9
  601.7 4.8 fusion.10
  621.0 14.2 %collective-permute-start.46 = (f32[7,1024]{1,0:T(8,128)S(1)}, f32[7,1024]{1,0:T(8,128)S(1)}, u32[]{:S(2)}, u32[]{:S(2)}) collective-permute-start(f32[7,1024]{1,0:T(8,128)S(1)} %concatenate.146), channel_id=1, source_target_pairs={{0,6},{1,7},{2,4},{3,5},{4,2},{5,3},{6,0},{7,1},{8,14},{9,15},{10,... | collective-permute-start | bytes 86024 | tf_op jit(solution)/shard_map/ppermute | solution.py:427
  635.8 6.6 fusion.60
  654.1 47.5 %collective-permute-done.48 = f32[7,1024]{1,0:T(8,128)S(1)} collective-permute-done((f32[7,1024]{1,0:T(8,128)S(1)}, f32[7,1024]{1,0:T(8,128)S(1)}, u32[]{:S(2)}, u32[]{:S(2)}) %collective-permute-start.48) | collective-permute-done | bytes 28704 | tf_op jit(solution)/shard_map/ppermute | solution.py:427
  706.9 28.0 %collective-permute-done.39 = bf16[8,3,32,1024]{3,2,1,0:T(8,128)(2,1)S(1)} collective-permute-done((bf16[8,3,32,1024]{3,2,1,0:T(8,128)(2,1)S(1)}, bf16[8,3,32,1024]{3,2,1,0:T(8,128)(2,1)S(1)}, u32[]{:S(2)}, u32[]{:S(2)}) %collective-permute-start.39) | collective-permute-done | bytes 1572896 | tf_op jit(solution)/shard_map/ppermute | solution.py:422
  756.1 5.6 collective-permute-done.53
  761.7 25.0 %collective-permute-start.34 = (bf16[2,128,1024]{2,1,0:T(8,128)(2,1)}, bf16[2,128,1024]{2,1,0:T(8,128)(2,1)}, u32[]{:S(2)}, u32[]{:S(2)}) collective-permute-start(bf16[2,128,1024]{2,1,0:T(8,128)(2,1)} %get-tuple-element.548), channel_id=1, source_target_pairs={{0,4},{1,5},{2,6},{3,7},{4,0},{5,1},{6,2},{7,3},{8,12},{9,13},{10,... | collective-permute-start | bytes 1572872 | tf_op jit(solution)/shard_map/ppermute | solution.py:427
  786.7 28.1 %collective-permute-done.52 = bf16[256,1024]{1,0:T(8,128)(2,1)S(1)} collective-permute-done((bf16[256,1024]{1,0:T(8,128)(2,1)S(1)}, bf16[256,1024]{1,0:T(8,128)(2,1)S(1)}, u32[]{:S(2)}, u32[]{:S(2)}) %collective-permute-start.52) | collective-permute-done | bytes 524320 | tf_op jit(solution)/shard_map/ppermute | solution.py:427
  817.5 18.9 %collective-permute-done.34 = bf16[2,128,1024]{2,1,0:T(8,128)(2,1)} collective-permute-done((bf16[2,128,1024]{2,1,0:T(8,128)(2,1)}, bf16[2,128,1024]{2,1,0:T(8,128)(2,1)}, u32[]{:S(2)}, u32[]{:S(2)}) %collective-permute-start.34) | collective-permute-done | bytes 524320 | tf_op jit(solution)/shard_map/ppermute | solution.py:427
  851.7 8.6 collective-permute-done.43
  860.3 26.2 %collective-permute-done.42 = bf16[8,32,1024]{2,1,0:T(8,128)(2,1)S(1)} collective-permute-done((bf16[8,32,1024]{2,1,0:T(8,128)(2,1)S(1)}, bf16[8,32,1024]{2,1,0:T(8,128)(2,1)S(1)}, u32[]{:S(2)}, u32[]{:S(2)}) %collective-permute-start.42) | collective-permute-done | bytes 524320 | tf_op jit(solution)/shard_map/ppermute | solution.py:427
  (527 shorter events, 271.8 us)
Async XLA Ops:
  2.5 32.1 %collective-permute-start.3 = (bf16[2,128,1024]{2,1,0:T(8,128)(2,1)}, bf16[2,128,1024]{2,1,0:T(8,128)(2,1)}, u32[]{:S(2)}, u32[]{:S(2)}) collective-permute-start(bf16[2,128,1024]{2,1,0:T(8,128)(2,1)} %slice_bitcast_fusion.130), channel_id=1, source_target_pairs={{0,2},{1,3},{2,0},{3,1},{4,6},{5,7},{6,4},{7,5},{8,10},{9,11},{10,... | collective-permute-start | bytes 1572872 | tf_op jit(solution)/shard_map/ppermute | solution.py:427
  5.6 29.0 %collective-permute-start.4 = (bf16[2,128,1024]{2,1,0:T(8,128)(2,1)}, bf16[2,128,1024]{2,1,0:T(8,128)(2,1)}, u32[]{:S(2)}, u32[]{:S(2)}) collective-permute-start(bf16[2,128,1024]{2,1,0:T(8,128)(2,1)} %slice_bitcast_fusion.130), channel_id=1, source_target_pairs={{0,4},{1,5},{2,6},{3,7},{4,0},{5,1},{6,2},{7,3},{8,12},{9,13},{10,... | collective-permute-start | bytes 1572872 | tf_op jit(solution)/shard_map/ppermute | solution.py:427
  8.1 46.5 %collective-permute-start.6 = (bf16[2,128,1024]{2,1,0:T(8,128)(2,1)}, bf16[2,128,1024]{2,1,0:T(8,128)(2,1)}, u32[]{:S(2)}, u32[]{:S(2)}) collective-permute-start(bf16[2,128,1024]{2,1,0:T(8,128)(2,1)} %slice_bitcast_fusion.130), channel_id=1, source_target_pairs={{0,1},{1,0},{2,3},{3,2},{4,5},{5,4},{6,7},{7,6},{8,9},{9,8},{10,11... | collective-permute-start | bytes 1572872 | tf_op jit(solution)/shard_map/ppermute | solution.py:427
  11.8 35.5 %collective-permute-start.1 = (bf16[3,256,1024]{2,1,0:T(8,128)(2,1)S(1)}, bf16[3,256,1024]{2,1,0:T(8,128)(2,1)}, u32[]{:S(2)}, u32[]{:S(2)}) collective-permute-start(bf16[3,256,1024]{2,1,0:T(8,128)(2,1)S(1)} %convert_element_type.608), channel_id=1, source_target_pairs={{0,16},{8,24},{16,0},{24,8},{1,17},{9,25},{17,1},{25,9},{2,18},{10... | collective-permute-start | bytes 4718600 | tf_op jit(solution)/shard_map/ppermute | solution.py:422
  13.4 35.8 %collective-permute-start.13 = (bf16[2,128,1024]{2,1,0:T(8,128)(2,1)}, bf16[2,128,1024]{2,1,0:T(8,128)(2,1)}, u32[]{:S(2)}, u32[]{:S(2)}) collective-permute-start(bf16[2,128,1024]{2,1,0:T(8,128)(2,1)} %param.30), channel_id=1, source_target_pairs={{0,1},{1,0},{2,3},{3,2},{4,5},{5,4},{6,7},{7,6},{8,9},{9,8},{10,11... | collective-permute-start | bytes 1572872 | tf_op jit(solution)/shard_map/ppermute | solution.py:427
  34.6 53.9 %collective-permute-start = (bf16[3,256,1024]{2,1,0:T(8,128)(2,1)S(1)}, bf16[3,256,1024]{2,1,0:T(8,128)(2,1)S(1)}, u32[]{:S(2)}, u32[]{:S(2)}) collective-permute-start(bf16[3,256,1024]{2,1,0:T(8,128)(2,1)S(1)} %convert_element_type.608), channel_id=1, source_target_pairs={{0,8},{8,0},{16,24},{24,16},{1,9},{9,1},{17,25},{25,17},{2,10},{10... | collective-permute-start | bytes 4718600 | tf_op jit(solution)/shard_map/ppermute | solution.py:417
  34.6 17.7 %collective-permute-start.5 = (bf16[2,128,1024]{2,1,0:T(8,128)(2,1)}, bf16[2,128,1024]{2,1,0:T(8,128)(2,1)S(1)}, u32[]{:S(2)}, u32[]{:S(2)}) collective-permute-start(bf16[2,128,1024]{2,1,0:T(8,128)(2,1)} %slice_bitcast_fusion.130), channel_id=1, source_target_pairs={{0,6},{1,7},{2,4},{3,5},{4,2},{5,3},{6,0},{7,1},{8,14},{9,15},{10,... | collective-permute-start | bytes 1572872 | tf_op jit(solution)/shard_map/ppermute | solution.py:427
  47.3 41.3 %collective-permute-start.2 = (bf16[3,256,1024]{2,1,0:T(8,128)(2,1)}, bf16[3,256,1024]{2,1,0:T(8,128)(2,1)S(1)}, u32[]{:S(2)}, u32[]{:S(2)}) collective-permute-start(bf16[3,256,1024]{2,1,0:T(8,128)(2,1)} %collective-permute-done.1), channel_id=1, source_target_pairs={{0,8},{8,0},{16,24},{24,16},{1,9},{9,1},{17,25},{25,17},{2,10},{10... | collective-permute-start | bytes 4718600 | tf_op jit(solution)/shard_map/ppermute | solution.py:417
  52.3 23.0 %collective-permute-start.8 = (bf16[2,128,1024]{2,1,0:T(8,128)(2,1)}, bf16[2,128,1024]{2,1,0:T(8,128)(2,1)S(1)}, u32[]{:S(2)}, u32[]{:S(2)}) collective-permute-start(bf16[2,128,1024]{2,1,0:T(8,128)(2,1)} %collective-permute-done.4), channel_id=1, source_target_pairs={{0,1},{1,0},{2,3},{3,2},{4,5},{5,4},{6,7},{7,6},{8,9},{9,8},{10,11... | collective-permute-start | bytes 1572872 | tf_op jit(solution)/shard_map/ppermute | solution.py:427
  54.7 31.5 %collective-permute-start.9 = (bf16[2,128,1024]{2,1,0:T(8,128)(2,1)S(1)}, bf16[2,128,1024]{2,1,0:T(8,128)(2,1)S(1)}, u32[]{:S(2)}, u32[]{:S(2)}) collective-permute-start(bf16[2,128,1024]{2,1,0:T(8,128)(2,1)S(1)} %collective-permute-done.5), channel_id=1, source_target_pairs={{0,1},{1,0},{2,3},{3,2},{4,5},{5,4},{6,7},{7,6},{8,9},{9,8},{10,11... | collective-permute-start | bytes 1572872 | tf_op jit(solution)/shard_map/ppermute | solution.py:427
  64.1 146.2 %collective-permute-start.10 = (bf16[5,256,1024]{2,1,0:T(8,128)(2,1)}, bf16[5,256,1024]{2,1,0:T(8,128)(2,1)}, u32[]{:S(2)}, u32[]{:S(2)}) collective-permute-start(bf16[5,256,1024]{2,1,0:T(8,128)(2,1)} %pad_maximum_fusion.43), channel_id=1, source_target_pairs={{0,8},{8,0},{16,24},{24,16},{1,9},{9,1},{17,25},{25,17},{2,10},{10... | collective-permute-start | bytes 7864328 | tf_op jit(solution)/shard_map/ppermute | solution.py:417
  75.3 81.4 %collective-permute-start.16 = (bf16[2,2,128,1024]{3,2,1,0:T(8,128)(2,1)}, bf16[2,2,128,1024]{3,2,1,0:T(8,128)(2,1)}, u32[]{:S(2)}, u32[]{:S(2)}) collective-permute-start(bf16[2,2,128,1024]{3,2,1,0:T(8,128)(2,1)} %get-tuple-element.304), channel_id=1, source_target_pairs={{0,6},{1,7},{2,4},{3,5},{4,2},{5,3},{6,0},{7,1},{8,14},{9,15},{10,... | collective-permute-start | bytes 3145736 | tf_op jit(solution)/shard_map/ppermute | solution.py:427
  87.0 58.9 %collective-permute-start.11 = (bf16[5,256,1024]{2,1,0:T(8,128)(2,1)}, bf16[5,256,1024]{2,1,0:T(8,128)(2,1)}, u32[]{:S(2)}, u32[]{:S(2)}) collective-permute-start(bf16[5,256,1024]{2,1,0:T(8,128)(2,1)} %pad_maximum_fusion.43), channel_id=1, source_target_pairs={{0,16},{8,24},{16,0},{24,8},{1,17},{9,25},{17,1},{25,9},{2,18},{10... | collective-permute-start | bytes 7864328 | tf_op jit(solution)/shard_map/ppermute | solution.py:422
  145.9 64.4 %collective-permute-start.12 = (bf16[5,256,1024]{2,1,0:T(8,128)(2,1)}, bf16[5,256,1024]{2,1,0:T(8,128)(2,1)}, u32[]{:S(2)}, u32[]{:S(2)}) collective-permute-start(bf16[5,256,1024]{2,1,0:T(8,128)(2,1)} %collective-permute-done.11), channel_id=1, source_target_pairs={{0,8},{8,0},{16,24},{24,16},{1,9},{9,1},{17,25},{25,17},{2,10},{10... | collective-permute-start | bytes 7864328 | tf_op jit(solution)/shard_map/ppermute | solution.py:417
  147.6 62.1 %collective-permute-start.18 = (bf16[1,256,4096]{2,1,0:T(8,128)(2,1)}, bf16[1,256,4096]{2,1,0:T(8,128)(2,1)}, u32[]{:S(2)}, u32[]{:S(2)}) collective-permute-start(bf16[1,256,4096]{2,1,0:T(8,128)(2,1)} %convert_bitcast_fusion.3), channel_id=1, source_target_pairs={{0,16},{8,24},{16,0},{24,8},{1,17},{9,25},{17,1},{25,9},{2,18},{10... | collective-permute-start | bytes 6291464 | tf_op jit(solution)/shard_map/ppermute | solution.py:422
  156.4 49.1 %collective-permute-start.15 = (bf16[2,2,128,1024]{3,2,1,0:T(8,128)(2,1)}, bf16[2,2,128,1024]{3,2,1,0:T(8,128)(2,1)}, u32[]{:S(2)}, u32[]{:S(2)}) collective-permute-start(bf16[2,2,128,1024]{3,2,1,0:T(8,128)(2,1)} %get-tuple-element.304), channel_id=1, source_target_pairs={{0,4},{1,5},{2,6},{3,7},{4,0},{5,1},{6,2},{7,3},{8,12},{9,13},{10,... | collective-permute-start | bytes 3145736 | tf_op jit(solution)/shard_map/ppermute | solution.py:427
  156.7 48.9 %collective-permute-start.14 = (bf16[2,2,128,1024]{3,2,1,0:T(8,128)(2,1)}, bf16[2,2,128,1024]{3,2,1,0:T(8,128)(2,1)}, u32[]{:S(2)}, u32[]{:S(2)}) collective-permute-start(bf16[2,2,128,1024]{3,2,1,0:T(8,128)(2,1)} %get-tuple-element.304), channel_id=1, source_target_pairs={{0,2},{1,3},{2,0},{3,1},{4,6},{5,7},{6,4},{7,5},{8,10},{9,11},{10,... | collective-permute-start | bytes 3145736 | tf_op jit(solution)/shard_map/ppermute | solution.py:427
  205.6 70.0 %collective-permute-start.17 = (bf16[1,256,4096]{2,1,0:T(8,128)(2,1)}, bf16[1,256,4096]{2,1,0:T(8,128)(2,1)}, u32[]{:S(2)}, u32[]{:S(2)}) collective-permute-start(bf16[1,256,4096]{2,1,0:T(8,128)(2,1)} %convert_bitcast_fusion.3), channel_id=1, source_target_pairs={{0,8},{8,0},{16,24},{24,16},{1,9},{9,1},{17,25},{25,17},{2,10},{10... | collective-permute-start | bytes 6291464 | tf_op jit(solution)/shard_map/ppermute | solution.py:417
  205.7 91.3 %collective-permute-start.20 = (bf16[1,1024,1024]{2,1,0:T(8,128)(2,1)}, bf16[1,1024,1024]{2,1,0:T(8,128)(2,1)}, u32[]{:S(2)}, u32[]{:S(2)}) collective-permute-start(bf16[1,1024,1024]{2,1,0:T(8,128)(2,1)} %convert_bitcast_fusion), channel_id=1, source_target_pairs={{0,8},{8,0},{16,24},{24,16},{1,9},{9,1},{17,25},{25,17},{2,10},{10... | collective-permute-start | bytes 6291464 | tf_op jit(solution)/shard_map/ppermute | solution.py:417
  209.8 65.3 %collective-permute-start.21 = (bf16[1,1024,1024]{2,1,0:T(8,128)(2,1)}, bf16[1,1024,1024]{2,1,0:T(8,128)(2,1)}, u32[]{:S(2)}, u32[]{:S(2)}) collective-permute-start(bf16[1,1024,1024]{2,1,0:T(8,128)(2,1)} %convert_bitcast_fusion), channel_id=1, source_target_pairs={{0,16},{8,24},{16,0},{24,8},{1,17},{9,25},{17,1},{25,9},{2,18},{10... | collective-permute-start | bytes 6291464 | tf_op jit(solution)/shard_map/ppermute | solution.py:422
  229.3 46.3 %collective-permute-start.19 = (bf16[1,256,4096]{2,1,0:T(8,128)(2,1)}, bf16[1,256,4096]{2,1,0:T(8,128)(2,1)S(1)}, u32[]{:S(2)}, u32[]{:S(2)}) collective-permute-start(bf16[1,256,4096]{2,1,0:T(8,128)(2,1)} %collective-permute-done.18), channel_id=1, source_target_pairs={{0,8},{8,0},{16,24},{24,16},{1,9},{9,1},{17,25},{25,17},{2,10},{10... | collective-permute-start | bytes 6291464 | tf_op jit(solution)/shard_map/ppermute | solution.py:417
  275.1 21.9 %collective-permute-start.22 = (bf16[1,1024,1024]{2,1,0:T(8,128)(2,1)}, bf16[1,1024,1024]{2,1,0:T(8,128)(2,1)}, u32[]{:S(2)}, u32[]{:S(2)}) collective-permute-start(bf16[1,1024,1024]{2,1,0:T(8,128)(2,1)} %collective-permute-done.21), channel_id=1, source_target_pairs={{0,8},{8,0},{16,24},{24,16},{1,9},{9,1},{17,25},{25,17},{2,10},{10... | collective-permute-start | bytes 6291464 | tf_op jit(solution)/shard_map/ppermute | solution.py:417
  366.6 19.4 %collective-permute-start.24 = (bf16[2,8,1,32,4096]{4,3,1,0,2:T(8,128)(2,1)}, bf16[2,8,1,32,4096]{4,3,1,0,2:T(8,128)(2,1)}, u32[]{:S(2)}, u32[]{:S(2)}) collective-permute-start(bf16[2,8,1,32,4096]{4,3,1,0,2:T(8,128)(2,1)} %dynamic-slice_bitcast_fusion), channel_id=1, source_target_pairs={{0,8},{8,0},{16,24},{24,16},{1,9},{9,1},{17,25},{25,17},{2,10},{10... | collective-permute-start | bytes 12582920 | tf_op jit(solution)/shard_map/ppermute | solution.py:417
  367.1 72.9 %collective-permute-start.26 = (bf16[2,4,1,128,1024]{4,3,1,0,2:T(8,128)(2,1)}, bf16[2,4,1,128,1024]{4,3,1,0,2:T(8,128)(2,1)S(1)}, u32[]{:S(2)}, u32[]{:S(2)}) collective-permute-start(bf16[2,4,1,128,1024]{4,3,1,0,2:T(8,128)(2,1)} %dynamic-slice_bitcast_fusion.5), channel_id=1, source_target_pairs={{0,1},{1,0},{2,3},{3,2},{4,5},{5,4},{6,7},{7,6},{8,9},{9,8},{10,11... | collective-permute-start | bytes 6291464 | tf_op jit(solution)/shard_map/ppermute | solution.py:427
  392.6 77.0 %collective-permute-start.25 = (bf16[8,1,32,4096]{3,2,0,1:T(8,128)(2,1)}, bf16[8,1,32,4096]{3,2,0,1:T(8,128)(2,1)S(1)}, u32[]{:S(2)}, u32[]{:S(2)}) collective-permute-start(bf16[8,1,32,4096]{3,2,0,1:T(8,128)(2,1)} %dynamic-slice_bitcast_fusion.4), channel_id=1, source_target_pairs={{0,16},{8,24},{16,0},{24,8},{1,17},{9,25},{17,1},{25,9},{2,18},{10... | collective-permute-start | bytes 6291464 | tf_op jit(solution)/shard_map/ppermute | solution.py:422
  490.4 26.0 %collective-permute-start.27 = (bf16[2,8,5,32,1024]{4,3,2,1,0:T(8,128)(2,1)S(1)}, bf16[2,8,5,32,1024]{4,3,2,1,0:T(8,128)(2,1)S(1)}, u32[]{:S(2)}, u32[]{:S(2)}) collective-permute-start(bf16[2,8,5,32,1024]{4,3,2,1,0:T(8,128)(2,1)S(1)} %get-tuple-element.556), channel_id=1, source_target_pairs={{0,8},{8,0},{16,24},{24,16},{1,9},{9,1},{17,25},{25,17},{2,10},{10... | collective-permute-start | bytes 15728648 | tf_op jit(solution)/shard_map/ppermute | solution.py:417
  490.4 25.6 %collective-permute-start.28 = (bf16[4,1,128,1024]{3,2,0,1:T(8,128)(2,1)S(1)}, bf16[4,1,128,1024]{3,2,0,1:T(8,128)(2,1)S(1)}, u32[]{:S(2)}, u32[]{:S(2)}) collective-permute-start(bf16[4,1,128,1024]{3,2,0,1:T(8,128)(2,1)S(1)} %dynamic-slice_bitcast_fusion.14), channel_id=1, source_target_pairs={{0,16},{8,24},{16,0},{24,8},{1,17},{9,25},{17,1},{25,9},{2,18},{10... | collective-permute-start | bytes 3145736 | tf_op jit(solution)/shard_map/ppermute | solution.py:422
  493.5 84.6 %collective-permute-start.31 = (bf16[2,2,128,1024]{3,2,1,0:T(8,128)(2,1)}, bf16[2,2,128,1024]{3,2,1,0:T(8,128)(2,1)}, u32[]{:S(2)}, u32[]{:S(2)}) collective-permute-start(bf16[2,2,128,1024]{3,2,1,0:T(8,128)(2,1)} %get-tuple-element.538), channel_id=1, source_target_pairs={{0,6},{1,7},{2,4},{3,5},{4,2},{5,3},{6,0},{7,1},{8,14},{9,15},{10,... | collective-permute-start | bytes 3145736 | tf_op jit(solution)/shard_map/ppermute | solution.py:427
  494.7 91.2 %collective-permute-start.30 = (bf16[2,2,128,1024]{3,2,1,0:T(8,128)(2,1)}, bf16[2,2,128,1024]{3,2,1,0:T(8,128)(2,1)}, u32[]{:S(2)}, u32[]{:S(2)}) collective-permute-start(bf16[2,2,128,1024]{3,2,1,0:T(8,128)(2,1)} %get-tuple-element.537), channel_id=1, source_target_pairs={{0,4},{1,5},{2,6},{3,7},{4,0},{5,1},{6,2},{7,3},{8,12},{9,13},{10,... | collective-permute-start | bytes 3145736 | tf_op jit(solution)/shard_map/ppermute | solution.py:427
  494.7 91.2 %collective-permute-start.29 = (bf16[2,2,128,1024]{3,2,1,0:T(8,128)(2,1)}, bf16[2,2,128,1024]{3,2,1,0:T(8,128)(2,1)}, u32[]{:S(2)}, u32[]{:S(2)}) collective-permute-start(bf16[2,2,128,1024]{3,2,1,0:T(8,128)(2,1)} %get-tuple-element.536), channel_id=1, source_target_pairs={{0,2},{1,3},{2,0},{3,1},{4,6},{5,7},{6,4},{7,5},{8,10},{9,11},{10,... | collective-permute-start | bytes 3145736 | tf_op jit(solution)/shard_map/ppermute | solution.py:427
  611.0 35.7 %collective-permute-start.36 = (bf16[2,8,3,32,1024]{4,3,2,1,0:T(8,128)(2,1)}, bf16[2,8,3,32,1024]{4,3,2,1,0:T(8,128)(2,1)}, u32[]{:S(2)}, u32[]{:S(2)}) collective-permute-start(bf16[2,8,3,32,1024]{4,3,2,1,0:T(8,128)(2,1)} %pad_maximum_fusion.42), channel_id=1, source_target_pairs={{0,8},{8,0},{16,24},{24,16},{1,9},{9,1},{17,25},{25,17},{2,10},{10... | collective-permute-start | bytes 9437192 | tf_op jit(solution)/shard_map/ppermute | solution.py:417
  611.0 33.5 %collective-permute-start.50 = (bf16[4,1,32,4096]{3,2,0,1:T(8,128)(2,1)}, bf16[4,1,32,4096]{3,2,0,1:T(8,128)(2,1)}, u32[]{:S(2)}, u32[]{:S(2)}) collective-permute-start(bf16[4,1,32,4096]{3,2,0,1:T(8,128)(2,1)} %dynamic-slice_bitcast_fusion.13), channel_id=1, source_target_pairs={{0,1},{1,0},{2,3},{3,2},{4,5},{5,4},{6,7},{7,6},{8,9},{9,8},{10,11... | collective-permute-start | bytes 3145736 | tf_op jit(solution)/shard_map/ppermute | solution.py:427
  621.0 21.8 %collective-permute-start.46 = (f32[7,1024]{1,0:T(8,128)S(1)}, f32[7,1024]{1,0:T(8,128)S(1)}, u32[]{:S(2)}, u32[]{:S(2)}) collective-permute-start(f32[7,1024]{1,0:T(8,128)S(1)} %concatenate.146), channel_id=1, source_target_pairs={{0,6},{1,7},{2,4},{3,5},{4,2},{5,3},{6,0},{7,1},{8,14},{9,15},{10,... | collective-permute-start | bytes 86024 | tf_op jit(solution)/shard_map/ppermute | solution.py:427
  642.8 62.8 %collective-permute-start.38 = (bf16[8,5,32,1024]{3,2,1,0:T(8,128)(2,1)S(1)}, bf16[8,5,32,1024]{3,2,1,0:T(8,128)(2,1)S(1)}, u32[]{:S(2)}, u32[]{:S(2)}) collective-permute-start(bf16[8,5,32,1024]{3,2,1,0:T(8,128)(2,1)S(1)} %copy-done.67), channel_id=1, source_target_pairs={{0,16},{8,24},{16,0},{24,8},{1,17},{9,25},{17,1},{25,9},{2,18},{10... | collective-permute-start | bytes 7864328 | tf_op jit(solution)/shard_map/ppermute | solution.py:422
  642.9 60.4 %collective-permute-start.32 = (bf16[4,2,128,1024]{3,2,1,0:T(8,128)(2,1)S(1)}, bf16[4,2,128,1024]{3,2,1,0:T(8,128)(2,1)S(1)}, u32[]{:S(2)}, u32[]{:S(2)}) collective-permute-start(bf16[4,2,128,1024]{3,2,1,0:T(8,128)(2,1)S(1)} %slice.545), channel_id=1, source_target_pairs={{0,1},{1,0},{2,3},{3,2},{4,5},{5,4},{6,7},{7,6},{8,9},{9,8},{10,11... | collective-permute-start | bytes 6291464 | tf_op jit(solution)/shard_map/ppermute | solution.py:427
  644.5 104.8 %collective-permute-start.37 = (bf16[2,128,1024]{2,1,0:T(8,128)(2,1)}, bf16[2,128,1024]{2,1,0:T(8,128)(2,1)}, u32[]{:S(2)}, u32[]{:S(2)}) collective-permute-start(bf16[2,128,1024]{2,1,0:T(8,128)(2,1)} %slice_bitcast_fusion.124), channel_id=1, source_target_pairs={{0,1},{1,0},{2,3},{3,2},{4,5},{5,4},{6,7},{7,6},{8,9},{9,8},{10,11... | collective-permute-start | bytes 1572872 | tf_op jit(solution)/shard_map/ppermute | solution.py:427
  645.9 55.7 %collective-permute-start.48 = (f32[7,1024]{1,0:T(8,128)S(1)}, f32[7,1024]{1,0:T(8,128)S(1)}, u32[]{:S(2)}, u32[]{:S(2)}) collective-permute-start(f32[7,1024]{1,0:T(8,128)S(1)} %fusion.201), channel_id=1, source_target_pairs={{0,1},{1,0},{2,3},{3,2},{4,5},{5,4},{6,7},{7,6},{8,9},{9,8},{10,11... | collective-permute-start | bytes 86024 | tf_op jit(solution)/shard_map/ppermute | solution.py:427
  649.8 85.1 %collective-permute-start.39 = (bf16[8,3,32,1024]{3,2,1,0:T(8,128)(2,1)S(1)}, bf16[8,3,32,1024]{3,2,1,0:T(8,128)(2,1)S(1)}, u32[]{:S(2)}, u32[]{:S(2)}) collective-permute-start(bf16[8,3,32,1024]{3,2,1,0:T(8,128)(2,1)S(1)} %dynamic-slice_bitcast_fusion.6), channel_id=1, source_target_pairs={{0,16},{8,24},{16,0},{24,8},{1,17},{9,25},{17,1},{25,9},{2,18},{10... | collective-permute-start | bytes 4718600 | tf_op jit(solution)/shard_map/ppermute | solution.py:422
  701.6 40.0 %collective-permute-start.49 = (f32[7,1024]{1,0:T(8,128)S(1)}, f32[7,1024]{1,0:T(8,128)S(1)}, u32[]{:S(2)}, u32[]{:S(2)}) collective-permute-start(f32[7,1024]{1,0:T(8,128)S(1)} %add.660), channel_id=1, source_target_pairs={{0,16},{8,24},{16,0},{24,8},{1,17},{9,25},{17,1},{25,9},{2,18},{10... | collective-permute-start | bytes 86024 | tf_op jit(solution)/shard_map/ppermute | solution.py:422
  737.6 102.3 %collective-permute-start.40 = (bf16[4,8,32,1024]{3,2,1,0:T(8,128)(2,1)}, bf16[4,8,32,1024]{3,2,1,0:T(8,128)(2,1)}, u32[]{:S(2)}, u32[]{:S(2)}) collective-permute-start(bf16[4,8,32,1024]{3,2,1,0:T(8,128)(2,1)} %dynamic-slice_bitcast_fusion.3), channel_id=1, source_target_pairs={{0,1},{1,0},{2,3},{3,2},{4,5},{5,4},{6,7},{7,6},{8,9},{9,8},{10,11... | collective-permute-start | bytes 6291464 | tf_op jit(solution)/shard_map/ppermute | solution.py:427
  744.9 16.8 %collective-permute-start.53 = (bf16[256,1024]{1,0:T(8,128)(2,1)S(1)}, bf16[256,1024]{1,0:T(8,128)(2,1)S(1)}, u32[]{:S(2)}, u32[]{:S(2)}) collective-permute-start(bf16[256,1024]{1,0:T(8,128)(2,1)S(1)} %get-tuple-element.542), channel_id=1, source_target_pairs={{0,6},{1,7},{2,4},{3,5},{4,2},{5,3},{6,0},{7,1},{8,14},{9,15},{10,... | collective-permute-start | bytes 1572872 | tf_op jit(solution)/shard_map/ppermute | solution.py:427
  748.4 66.5 %collective-permute-start.52 = (bf16[256,1024]{1,0:T(8,128)(2,1)S(1)}, bf16[256,1024]{1,0:T(8,128)(2,1)S(1)}, u32[]{:S(2)}, u32[]{:S(2)}) collective-permute-start(bf16[256,1024]{1,0:T(8,128)(2,1)S(1)} %get-tuple-element.541), channel_id=1, source_target_pairs={{0,4},{1,5},{2,6},{3,7},{4,0},{5,1},{6,2},{7,3},{8,12},{9,13},{10,... | collective-permute-start | bytes 1572872 | tf_op jit(solution)/shard_map/ppermute | solution.py:427
  748.4 66.8 %collective-permute-start.51 = (bf16[256,1024]{1,0:T(8,128)(2,1)S(1)}, bf16[256,1024]{1,0:T(8,128)(2,1)S(1)}, u32[]{:S(2)}, u32[]{:S(2)}) collective-permute-start(bf16[256,1024]{1,0:T(8,128)(2,1)S(1)} %get-tuple-element.540), channel_id=1, source_target_pairs={{0,2},{1,3},{2,0},{3,1},{4,6},{5,7},{6,4},{7,5},{8,10},{9,11},{10,... | collective-permute-start | bytes 1572872 | tf_op jit(solution)/shard_map/ppermute | solution.py:427
  752.7 64.8 %collective-permute-start.35 = (bf16[2,128,1024]{2,1,0:T(8,128)(2,1)}, bf16[2,128,1024]{2,1,0:T(8,128)(2,1)}, u32[]{:S(2)}, u32[]{:S(2)}) collective-permute-start(bf16[2,128,1024]{2,1,0:T(8,128)(2,1)} %get-tuple-element.547), channel_id=1, source_target_pairs={{0,6},{1,7},{2,4},{3,5},{4,2},{5,3},{6,0},{7,1},{8,14},{9,15},{10,... | collective-permute-start | bytes 1572872 | tf_op jit(solution)/shard_map/ppermute | solution.py:427
  761.7 74.7 %collective-permute-start.34 = (bf16[2,128,1024]{2,1,0:T(8,128)(2,1)}, bf16[2,128,1024]{2,1,0:T(8,128)(2,1)}, u32[]{:S(2)}, u32[]{:S(2)}) collective-permute-start(bf16[2,128,1024]{2,1,0:T(8,128)(2,1)} %get-tuple-element.548), channel_id=1, source_target_pairs={{0,4},{1,5},{2,6},{3,7},{4,0},{5,1},{6,2},{7,3},{8,12},{9,13},{10,... | collective-permute-start | bytes 1572872 | tf_op jit(solution)/shard_map/ppermute | solution.py:427
  814.8 23.2 %collective-permute-start.33 = (bf16[2,128,1024]{2,1,0:T(8,128)(2,1)}, bf16[2,128,1024]{2,1,0:T(8,128)(2,1)}, u32[]{:S(2)}, u32[]{:S(2)}) collective-permute-start(bf16[2,128,1024]{2,1,0:T(8,128)(2,1)} %get-tuple-element.546), channel_id=1, source_target_pairs={{0,2},{1,3},{2,0},{3,1},{4,6},{5,7},{6,4},{7,5},{8,10},{9,11},{10,... | collective-permute-start | bytes 1572872 | tf_op jit(solution)/shard_map/ppermute | solution.py:427
  845.6 40.9 %collective-permute-start.42 = (bf16[8,32,1024]{2,1,0:T(8,128)(2,1)S(1)}, bf16[8,32,1024]{2,1,0:T(8,128)(2,1)S(1)}, u32[]{:S(2)}, u32[]{:S(2)}) collective-permute-start(bf16[8,32,1024]{2,1,0:T(8,128)(2,1)S(1)} %get-tuple-element.545), channel_id=1, source_target_pairs={{0,4},{1,5},{2,6},{3,7},{4,0},{5,1},{6,2},{7,3},{8,12},{9,13},{10,... | collective-permute-start | bytes 1572872 | tf_op jit(solution)/shard_map/ppermute | solution.py:427
  845.6 40.9 %collective-permute-start.41 = (bf16[8,32,1024]{2,1,0:T(8,128)(2,1)S(1)}, bf16[8,32,1024]{2,1,0:T(8,128)(2,1)S(1)}, u32[]{:S(2)}, u32[]{:S(2)}) collective-permute-start(bf16[8,32,1024]{2,1,0:T(8,128)(2,1)S(1)} %get-tuple-element.543), channel_id=1, source_target_pairs={{0,2},{1,3},{2,0},{3,1},{4,6},{5,7},{6,4},{7,5},{8,10},{9,11},{10,... | collective-permute-start | bytes 1572872 | tf_op jit(solution)/shard_map/ppermute | solution.py:427
  (135 other events, 1548.8 us)

commit v4 on v2

--- a/solution.py
+++ b/solution.py
@@ -532,13 +532,13 @@
 
 
 def sum_everywhere(values_in):
-    total = values_in + swap_core(values_in)
-    total = total + swap_chip(total)
-    total = total + swap_block(total, 1)
     blocks = lax.axis_size("blk")
     mine = lax.axis_index("blk") // 2
-    come = jnp.stack([total] + [swap_block(total, 2 * gap) for gap in range(1, blocks // 2)])
-    return sum(pick(come, mine ^ index, 0) for index in range(blocks // 2))
+    come = jnp.stack([values_in] + [swap_block(values_in, 2 * gap) for gap in range(1, blocks // 2)])
+    total = sum(pick(come, mine ^ index, 0) for index in range(blocks // 2))
+    total = total + swap_core(total)
+    total = total + swap_block(total, 1)
+    return total + swap_chip(total)
 
 
 def shards(

time: 885 us -> 887 us (level); the launches traced: 884 us -> 876 us
  waiting for transfers between devices: 259 us -> 282 us
  starting transfers between devices: 94 us -> 72.2 us
    ppermute x35, waiting for transfers between devices: 173 us -> 205 us  [swap_block(): return lax.ppermute(values_in, 'blk', [(i, i ^ bit) for i in range(size)])]
    ppermute x35, starting transfers between devices: 80 us -> 61 us  [swap_block(): return lax.ppermute(values_in, 'blk', [(i, i ^ bit) for i in range(size)])]
    ppermute x9, waiting for transfers between devices: 86 us -> 76.9 us  [swap_chip(): return lax.ppermute(values_in, 'dp', [(i, i ^ 2) for i in range(size)])]
    unnamed x264 -> x270, local copies, waits for them, and re-layouts: 46.9 us -> 47.6 us
  transfers between devices with their start and end apart: 57 -> 57, of which waited for: 18 -> 17; matrix products, arithmetic and copies ran while one was open for 31% -> 30% of each run, Pallas kernels for 14% -> 14%
where the time goes in v4:
time: 887 us; the launch traced here: 876 us
  waiting for transfers between devices  282 us (32%)
  matrix products  184 us (21%)
  Pallas kernels  120 us (14%)
  other arithmetic  112 us (13%)
  local copies, waits for them, and re-layouts  93.7 us (11%)
  starting transfers between devices  72.2 us (8%)
  loops' own time  9.01 us (1%)
    ppermute x35, waiting for transfers between devices, swap_block(): return lax.ppermute(values_in, 'blk', [(i, i ^ bit) for i in range(size)])  205 us
    ppermute x9, waiting for transfers between devices, swap_chip(): return lax.ppermute(values_in, 'dp', [(i, i ^ 2) for i in range(size)])  76.9 us
    pallas_call x2, Pallas kernels, attend_backward(): pl.pallas_call(partial(backward_kernel, is_self, rows, near_tiles), grid_...  72.2 us
    dot_general x12, matrix products, matmul_t(): jnp.einsum('...j,ij->...i', left_side, right_side, preferred_element_type...  70 us
    ppermute x35, starting transfers between devices, swap_block(): return lax.ppermute(values_in, 'blk', [(i, i ^ bit) for i in range(size)])  61 us
    dot_general x12, matrix products, matmul(): jnp.einsum('...i,ij->...j', left_side, right_side, preferred_element_type...  60.3 us
    pallas_call x2, Pallas kernels, attend_forward(): pl.pallas_call(partial(forward_kernel, is_self, rows, near_tiles), grid_s...  48 us
    unnamed x270, local copies, waits for them, and re-layouts  47.6 us
  transfers between devices with their start and end apart: 57, of which 17 were waited for; matrix products, arithmetic and copies ran while one was open for 30% of the time, Pallas kernels for 14%

profile of v4, /device:TPU:0, one launch (start us, length us, event | category | flops | bytes accessed | tf_op | source)
XLA Modules:
  0.0 875.6 jit_solution(1056440541388369726)
XLA Ops:
  37.2 10.1 %collective-permute-done.1 = bf16[3,256,1024]{2,1,0:T(8,128)(2,1)} collective-permute-done((bf16[3,256,1024]{2,1,0:T(8,128)(2,1)S(1)}, bf16[3,256,1024]{2,1,0:T(8,128)(2,1)}, u32[]{:S(2)}, u32[]{:S(2)}) %collective-permute-start.1) | collective-permute-done | bytes 1572896 | tf_op jit(solution)/shard_map/ppermute | solution.py:422
  57.1 7.0 collective-permute-done.7
  64.9 10.4 %collective-permute-done.8 = bf16[2,128,1024]{2,1,0:T(8,128)(2,1)S(1)} collective-permute-done((bf16[2,128,1024]{2,1,0:T(8,128)(2,1)}, bf16[2,128,1024]{2,1,0:T(8,128)(2,1)S(1)}, u32[]{:S(2)}, u32[]{:S(2)}) %collective-permute-start.8) | collective-permute-done | bytes 524320 | tf_op jit(solution)/shard_map/ppermute | solution.py:427
  76.4 9.8 %collective-permute-done.9 = bf16[2,128,1024]{2,1,0:T(8,128)(2,1)S(1)} collective-permute-done((bf16[2,128,1024]{2,1,0:T(8,128)(2,1)S(1)}, bf16[2,128,1024]{2,1,0:T(8,128)(2,1)S(1)}, u32[]{:S(2)}, u32[]{:S(2)}) %collective-permute-start.9) | collective-permute-done | bytes 524320 | tf_op jit(solution)/shard_map/ppermute | solution.py:427
  101.1 4.7 convolution_convert_fusion.4.refs_3_
  105.9 4.7 convolution_convert_fusion.5.refs_2_
  110.8 19.2 %shard_map.220 = (bf16[2,3,128,1024]{3,2,1,0:T(8,128)(2,1)S(1)}, f32[8,2,1,768]{3,2,1,0:T(1,128)S(1)}) custom-call(s32[2,3]{1,0:T(2,128)S(1)} %get-tuple-element.583.refs_0_, bf16[2,3,128,1024]{3,2,1,0:T(8,128)(2,1)S(1)} %fusion.69.refs_1_, bf16[8,2,128,1024]{3,2,1,0:T(8,128)(2,1)S(1)} %convolution_convert_fusion.5.refs_2_, ...), custom_call_target="tpu_custom_call" | custom-call | tf_op jit(solution)/shard_map/pallas_call | solution.py:261
  130.0 15.9 %collective-permute-done.11 = bf16[5,256,1024]{2,1,0:T(8,128)(2,1)} collective-permute-done((bf16[5,256,1024]{2,1,0:T(8,128)(2,1)}, bf16[5,256,1024]{2,1,0:T(8,128)(2,1)}, u32[]{:S(2)}, u32[]{:S(2)}) %collective-permute-start.11) | collective-permute-done | bytes 2621472 | tf_op jit(solution)/shard_map/ppermute | solution.py:422
  162.4 41.5 %collective-permute-done.15 = bf16[2,2,128,1024]{3,2,1,0:T(8,128)(2,1)} collective-permute-done((bf16[2,2,128,1024]{3,2,1,0:T(8,128)(2,1)}, bf16[2,2,128,1024]{3,2,1,0:T(8,128)(2,1)}, u32[]{:S(2)}, u32[]{:S(2)}) %collective-permute-start.15) | collective-permute-done | bytes 1048608 | tf_op jit(solution)/shard_map/ppermute | solution.py:427
  208.4 16.2 %conditional.5 = (bf16[1024,1024]{1,0:T(8,128)(2,1)S(1)}, bf16[1024,1024]{1,0:T(8,128)(2,1)S(1)}, bf16[1024,1024]{1,0:T(8,128)(2,1)S(1)}, bf16[1024,1024]{1,0:T(8,128)(2,1)S(1)}, bf16[1024,1024]{1,0:T(8,128)(2,1)S(1)}) conditional(s32[]{:T(128)} %clamp.2, (bf16[5,256,1024]{2,1,0:T(8,128)(2,1)}, ...), branch_computations={%region_6.7_spmd, %region_7.8_spmd, %region_8.9_spmd, %region_9.10... | conditional | flops 41943040 | bytes 39845928 | solution.py:443
  241.3 4.7 convolution_convert_fusion.2.refs_3_
  246.0 28.8 %shard_map.221 = (bf16[2,3,128,1024]{3,2,1,0:T(8,128)(2,1)S(1)}, f32[8,2,1,768]{3,2,1,0:T(1,128)S(1)}) custom-call(s32[2,3]{1,0:T(2,128)S(1)} %get-tuple-element.582.refs_0_, bf16[2,3,128,1024]{3,2,1,0:T(8,128)(2,1)S(1)} %bitcast.708, bf16[8,2,128,1024]{3,2,1,0:T(8,128)(2,1)S(1)} %convolution_convert_fusion.3.refs_2_, ...), custom_call_target="tpu_custom_call" | custom-call | tf_op jit(solution)/shard_map/pallas_call | solution.py:261
  279.7 6.3 conditional.6
  279.7 6.1 pad_maximum_fusion.32
  286.0 15.0 %multiply_convert_fusion.1 = (bf16[768,4096]{1,0:T(8,128)(2,1)}, f32[768,4096]{1,0:T(8,128)}) fusion(bf16[1024,4096]{1,0:T(8,128)(2,1)} %get-tuple-element.630, f32[768,1024]{1,0:T(8,128)} %copy-done.43, f32[1024]{0:T(1024)S(1)} %bitcast.783, f32[1024]{0:T(1024)S(1)} %bitcast.772, f32[768]{0:T(1024)S(1)} %add_rsqrt_fusion.1, ...), kind=kOutput, calls=%fused_computation.167 | convolution fusion | flops 6462111744 | bytes 30423040 | tf_op jit(solution)/shard_map/...i,ij->...j/dot_general | solution.py:408
  301.0 6.6 conditional.7
  301.0 6.6 pad_maximum_fusion.36
  307.6 11.7 %fusion.145 = (f32[768]{0:T(1024)S(1)}, f32[768,1024]{1,0:T(8,128)S(1)}) fusion(bf16[768,4096]{1,0:T(8,128)(2,1)} %get-tuple-element.588, bf16[4096,1024]{1,0:T(8,128)(2,1)} %get-tuple-element.631, f32[1024]{0:T(1024)S(1)} %bitcast.784, f32[1024]{0:T(1024)S(1)} %bitcast.773, f32[768]{0:T(1024)S(1)} %add_rsqrt_fusion.1, f32[768,1024]{1,0:T(8,128)} %copy-done.43, ...), kind=kOutput, calls=%fused_computation.458 | convolution fusion | flops 6447168512 | bytes 20988928 | tf_op jit(solution)/shard_map/...i,ij->...j/dot_general | solution.py:408
  325.4 7.1 convolution_convert_fusion.1
  337.1 14.0 %multiply_convert_fusion = bf16[768,4096]{1,0:T(8,128)(2,1)S(1)} fusion(bf16[768,1024]{1,0:T(8,128)(2,1)} %copy-done.96, bf16[4096,1024]{1,0:T(8,128)(2,1)} %get-tuple-element.631, f32[768,4096]{1,0:T(8,128)} %get-tuple-element.589), kind=kOutput, calls=%fused_computation.166 | convolution fusion | flops 6480199680 | bytes 28835840 | tf_op jit(solution)/shard_map/...j,ij->...i/dot_general | solution.py:412
  351.1 6.6 fusion.6
  361.8 7.7 convolution_convert_fusion
  374.8 13.7 %multiply_reduce_fusion = (f32[1024]{0:T(1024)S(1)}, f32[768]{0:T(1024)S(1)}, f32[768]{0:T(1024)S(1)}, f32[1024]{0:T(1024)S(1)}, f32[768,1024]{1,0:T(8,128)S(1)}) fusion(f32[768,1024]{1,0:T(8,128)} %copy-done.43, f32[768]{0:T(1024)S(1)} %add_rsqrt_fusion.1, f32[768]{0:T(1024)S(1)} %broadcast_multiply_fusion.7, f32[1024]{0:T(1024)S(1)} %bitcast.775, ...), kind=kOutput, calls=%fused_computation.218 | convolution fusion | flops 6450311168 | bytes 24141824 | tf_op jit(solution)/shard_map/...j,ij->...i/dot_general | solution.py:412
  394.5 5.0 fusion.5
  405.0 38.4 %shard_map.222 = (bf16[2,3,128,1024]{3,2,1,0:T(8,128)(2,1)S(1)}, bf16[8,2,128,1024]{3,2,1,0:T(8,128)(2,1)S(1)}, bf16[8,2,128,1024]{3,2,1,0:T(8,128)(2,1)S(1)}) custom-call(s32[2,3]{1,0:T(2,128)S(1)} %get-tuple-element.582.refs_0_, bf16[2,3,128,1024]{3,2,1,0:T(8,128)(2,1)S(1)} %bitcast.709, bf16[8,2,128,1024]{3,2,1,0:T(8,128)(2,1)S(1)} %copy-done.2, ...), custom_call_target="tpu_custom_call" | custom-call | tf_op jit(solution)/shard_map/pallas_call | solution.py:306
  447.5 5.8 convolution_convert_fusion.6
  455.7 7.1 fusion.47
  462.8 8.4 add_convert_fusion.2
  482.2 5.2 convolution_convert_fusion.7
  494.9 5.7 collective-permute-start.32
  505.6 11.8 %collective-permute-done.28 = bf16[4,1,128,1024]{3,2,0,1:T(8,128)(2,1)S(1)} collective-permute-done((bf16[4,1,128,1024]{3,2,0,1:T(8,128)(2,1)S(1)}, bf16[4,1,128,1024]{3,2,0,1:T(8,128)(2,1)S(1)}, u32[]{:S(2)}, u32[]{:S(2)}) %collective-permute-start.28) | collective-permute-done | bytes 1048608 | tf_op jit(solution)/shard_map/ppermute | solution.py:422
  522.8 9.7 %add_convert_fusion = bf16[2,8,5,32,1024]{4,3,2,1,0:T(8,128)(2,1)} fusion(bf16[2,8,5,32,1024]{4,3,2,1,0:T(8,128)(2,1)} %copy-done.54, bf16[2,8,5,32,1024]{4,3,2,1,0:T(8,128)(2,1)} %get-tuple-element.552), kind=kLoop, calls=%fused_computation.169 | loop fusion | flops 10485760 | bytes 15728640 | tf_op jit(solution)/shard_map/convert_element_type | solution.py:455
  536.4 33.8 %shard_map.223 = (bf16[2,3,128,1024]{3,2,1,0:T(8,128)(2,1)S(1)}, bf16[8,2,128,1024]{3,2,1,0:T(8,128)(2,1)S(1)}, bf16[8,2,128,1024]{3,2,1,0:T(8,128)(2,1)S(1)}, b...) custom-call(s32[2,3]{1,0:T(2,128)S(1)} %copy-done.25, ...), custom_call_target="tpu_custom_call" | custom-call | tf_op jit(solution)/shard_map/pallas_call | solution.py:306
  577.5 6.5 add_convert_fusion.1
  583.9 7.8 collective-permute-done.31
  599.7 5.0 fusion.9
  606.2 4.8 fusion.10
  617.6 12.4 %collective-permute-start.56 = (bf16[1,128,1024]{2,1,0:T(8,128)(2,1)}, bf16[1,128,1024]{2,1,0:T(8,128)(2,1)}, u32[]{:S(2)}, u32[]{:S(2)}) collective-permute-start(bf16[1,128,1024]{2,1,0:T(8,128)(2,1)} %get-tuple-element.563), channel_id=1, source_target_pairs={{0,6},{1,7},{2,4},{3,5},{4,2},{5,3},{6,0},{7,1},{8,14},{9,15},{10,... | collective-permute-start | bytes 786440 | tf_op jit(solution)/shard_map/ppermute | solution.py:427
  643.8 11.0 %collective-permute-done.55 = bf16[1,128,1024]{2,1,0:T(8,128)(2,1)} collective-permute-done((bf16[1,128,1024]{2,1,0:T(8,128)(2,1)}, bf16[1,128,1024]{2,1,0:T(8,128)(2,1)}, u32[]{:S(2)}, u32[]{:S(2)}) %collective-permute-start.55) | collective-permute-done | bytes 262176 | tf_op jit(solution)/shard_map/ppermute | solution.py:427
  665.3 5.3 fusion.60
  681.4 29.0 %collective-permute-done.33 = bf16[4,2,128,1024]{3,2,1,0:T(8,128)(2,1)S(1)} collective-permute-done((bf16[4,2,128,1024]{3,2,1,0:T(8,128)(2,1)S(1)}, bf16[4,2,128,1024]{3,2,1,0:T(8,128)(2,1)S(1)}, u32[]{:S(2)}, u32[]{:S(2)}) %collective-permute-start.33) | collective-permute-done | bytes 2097184 | tf_op jit(solution)/shard_map/ppermute | solution.py:427
  711.3 8.5 collective-permute-done.39
  721.2 30.7 %collective-permute-done.40 = bf16[8,3,32,1024]{3,2,1,0:T(8,128)(2,1)S(1)} collective-permute-done((bf16[8,3,32,1024]{3,2,1,0:T(8,128)(2,1)S(1)}, bf16[8,3,32,1024]{3,2,1,0:T(8,128)(2,1)S(1)}, u32[]{:S(2)}, u32[]{:S(2)}) %collective-permute-start.40) | collective-permute-done | bytes 1572896 | tf_op jit(solution)/shard_map/ppermute | solution.py:422
  765.8 5.6 collective-permute-done.53
  771.4 10.7 %collective-permute-done.52 = bf16[1,32,4096]{2,1,0:T(8,128)(2,1)} collective-permute-done((bf16[1,32,4096]{2,1,0:T(8,128)(2,1)}, bf16[1,32,4096]{2,1,0:T(8,128)(2,1)}, u32[]{:S(2)}, u32[]{:S(2)}) %collective-permute-start.52) | collective-permute-done | bytes 262176 | tf_op jit(solution)/shard_map/ppermute | solution.py:427
  788.8 23.3 %collective-permute-done.38 = bf16[2,128,1024]{2,1,0:T(8,128)(2,1)} collective-permute-done((bf16[2,128,1024]{2,1,0:T(8,128)(2,1)}, bf16[2,128,1024]{2,1,0:T(8,128)(2,1)}, u32[]{:S(2)}, u32[]{:S(2)}) %collective-permute-start.38) | collective-permute-done | bytes 524320 | tf_op jit(solution)/shard_map/ppermute | solution.py:427
  821.5 32.3 %collective-permute-done.36 = bf16[2,128,1024]{2,1,0:T(8,128)(2,1)S(1)} collective-permute-done((bf16[2,128,1024]{2,1,0:T(8,128)(2,1)S(1)}, bf16[2,128,1024]{2,1,0:T(8,128)(2,1)S(1)}, u32[]{:S(2)}, u32[]{:S(2)}) %collective-permute-start.36) | collective-permute-done | bytes 524320 | tf_op jit(solution)/shard_map/ppermute | solution.py:427
  856.6 16.6 %collective-permute-done.43 = bf16[8,32,1024]{2,1,0:T(8,128)(2,1)S(1)} collective-permute-done((bf16[8,32,1024]{2,1,0:T(8,128)(2,1)S(1)}, bf16[8,32,1024]{2,1,0:T(8,128)(2,1)S(1)}, u32[]{:S(2)}, u32[]{:S(2)}) %collective-permute-start.43) | collective-permute-done | bytes 524320 | tf_op jit(solution)/shard_map/ppermute | solution.py:427
  (530 shorter events, 281.2 us)
Async XLA Ops:
  2.5 32.5 %collective-permute-start.3 = (bf16[2,128,1024]{2,1,0:T(8,128)(2,1)}, bf16[2,128,1024]{2,1,0:T(8,128)(2,1)}, u32[]{:S(2)}, u32[]{:S(2)}) collective-permute-start(bf16[2,128,1024]{2,1,0:T(8,128)(2,1)} %slice_bitcast_fusion.130), channel_id=1, source_target_pairs={{0,2},{1,3},{2,0},{3,1},{4,6},{5,7},{6,4},{7,5},{8,10},{9,11},{10,... | collective-permute-start | bytes 1572872 | tf_op jit(solution)/shard_map/ppermute | solution.py:427
  5.6 29.4 %collective-permute-start.4 = (bf16[2,128,1024]{2,1,0:T(8,128)(2,1)}, bf16[2,128,1024]{2,1,0:T(8,128)(2,1)}, u32[]{:S(2)}, u32[]{:S(2)}) collective-permute-start(bf16[2,128,1024]{2,1,0:T(8,128)(2,1)} %slice_bitcast_fusion.130), channel_id=1, source_target_pairs={{0,4},{1,5},{2,6},{3,7},{4,0},{5,1},{6,2},{7,3},{8,12},{9,13},{10,... | collective-permute-start | bytes 1572872 | tf_op jit(solution)/shard_map/ppermute | solution.py:427
  8.1 46.5 %collective-permute-start.6 = (bf16[2,128,1024]{2,1,0:T(8,128)(2,1)}, bf16[2,128,1024]{2,1,0:T(8,128)(2,1)}, u32[]{:S(2)}, u32[]{:S(2)}) collective-permute-start(bf16[2,128,1024]{2,1,0:T(8,128)(2,1)} %slice_bitcast_fusion.130), channel_id=1, source_target_pairs={{0,1},{1,0},{2,3},{3,2},{4,5},{5,4},{6,7},{7,6},{8,9},{9,8},{10,11... | collective-permute-start | bytes 1572872 | tf_op jit(solution)/shard_map/ppermute | solution.py:427
  11.8 35.5 %collective-permute-start.1 = (bf16[3,256,1024]{2,1,0:T(8,128)(2,1)S(1)}, bf16[3,256,1024]{2,1,0:T(8,128)(2,1)}, u32[]{:S(2)}, u32[]{:S(2)}) collective-permute-start(bf16[3,256,1024]{2,1,0:T(8,128)(2,1)S(1)} %convert_element_type.639), channel_id=1, source_target_pairs={{0,16},{8,24},{16,0},{24,8},{1,17},{9,25},{17,1},{25,9},{2,18},{10... | collective-permute-start | bytes 4718600 | tf_op jit(solution)/shard_map/ppermute | solution.py:422
  13.3 35.8 %collective-permute-start.13 = (bf16[2,128,1024]{2,1,0:T(8,128)(2,1)}, bf16[2,128,1024]{2,1,0:T(8,128)(2,1)}, u32[]{:S(2)}, u32[]{:S(2)}) collective-permute-start(bf16[2,128,1024]{2,1,0:T(8,128)(2,1)} %param.30), channel_id=1, source_target_pairs={{0,1},{1,0},{2,3},{3,2},{4,5},{5,4},{6,7},{7,6},{8,9},{9,8},{10,11... | collective-permute-start | bytes 1572872 | tf_op jit(solution)/shard_map/ppermute | solution.py:427
  35.0 53.6 %collective-permute-start = (bf16[3,256,1024]{2,1,0:T(8,128)(2,1)S(1)}, bf16[3,256,1024]{2,1,0:T(8,128)(2,1)S(1)}, u32[]{:S(2)}, u32[]{:S(2)}) collective-permute-start(bf16[3,256,1024]{2,1,0:T(8,128)(2,1)S(1)} %convert_element_type.639), channel_id=1, source_target_pairs={{0,8},{8,0},{16,24},{24,16},{1,9},{9,1},{17,25},{25,17},{2,10},{10... | collective-permute-start | bytes 4718600 | tf_op jit(solution)/shard_map/ppermute | solution.py:417
  47.3 41.3 %collective-permute-start.2 = (bf16[3,256,1024]{2,1,0:T(8,128)(2,1)}, bf16[3,256,1024]{2,1,0:T(8,128)(2,1)S(1)}, u32[]{:S(2)}, u32[]{:S(2)}) collective-permute-start(bf16[3,256,1024]{2,1,0:T(8,128)(2,1)} %collective-permute-done.1), channel_id=1, source_target_pairs={{0,8},{8,0},{16,24},{24,16},{1,9},{9,1},{17,25},{25,17},{2,10},{10... | collective-permute-start | bytes 4718600 | tf_op jit(solution)/shard_map/ppermute | solution.py:417
  52.3 23.0 %collective-permute-start.8 = (bf16[2,128,1024]{2,1,0:T(8,128)(2,1)}, bf16[2,128,1024]{2,1,0:T(8,128)(2,1)S(1)}, u32[]{:S(2)}, u32[]{:S(2)}) collective-permute-start(bf16[2,128,1024]{2,1,0:T(8,128)(2,1)} %collective-permute-done.4), channel_id=1, source_target_pairs={{0,1},{1,0},{2,3},{3,2},{4,5},{5,4},{6,7},{7,6},{8,9},{9,8},{10,11... | collective-permute-start | bytes 1572872 | tf_op jit(solution)/shard_map/ppermute | solution.py:427
  54.7 31.5 %collective-permute-start.9 = (bf16[2,128,1024]{2,1,0:T(8,128)(2,1)S(1)}, bf16[2,128,1024]{2,1,0:T(8,128)(2,1)S(1)}, u32[]{:S(2)}, u32[]{:S(2)}) collective-permute-start(bf16[2,128,1024]{2,1,0:T(8,128)(2,1)S(1)} %collective-permute-done.5), channel_id=1, source_target_pairs={{0,1},{1,0},{2,3},{3,2},{4,5},{5,4},{6,7},{7,6},{8,9},{9,8},{10,11... | collective-permute-start | bytes 1572872 | tf_op jit(solution)/shard_map/ppermute | solution.py:427
  64.1 144.3 %collective-permute-start.10 = (bf16[5,256,1024]{2,1,0:T(8,128)(2,1)}, bf16[5,256,1024]{2,1,0:T(8,128)(2,1)}, u32[]{:S(2)}, u32[]{:S(2)}) collective-permute-start(bf16[5,256,1024]{2,1,0:T(8,128)(2,1)} %pad_maximum_fusion.43), channel_id=1, source_target_pairs={{0,8},{8,0},{16,24},{24,16},{1,9},{9,1},{17,25},{25,17},{2,10},{10... | collective-permute-start | bytes 7864328 | tf_op jit(solution)/shard_map/ppermute | solution.py:417
  75.3 79.9 %collective-permute-start.16 = (bf16[2,2,128,1024]{3,2,1,0:T(8,128)(2,1)}, bf16[2,2,128,1024]{3,2,1,0:T(8,128)(2,1)}, u32[]{:S(2)}, u32[]{:S(2)}) collective-permute-start(bf16[2,2,128,1024]{3,2,1,0:T(8,128)(2,1)} %get-tuple-element.304), channel_id=1, source_target_pairs={{0,6},{1,7},{2,4},{3,5},{4,2},{5,3},{6,0},{7,1},{8,14},{9,15},{10,... | collective-permute-start | bytes 3145736 | tf_op jit(solution)/shard_map/ppermute | solution.py:427
  87.0 58.9 %collective-permute-start.11 = (bf16[5,256,1024]{2,1,0:T(8,128)(2,1)}, bf16[5,256,1024]{2,1,0:T(8,128)(2,1)}, u32[]{:S(2)}, u32[]{:S(2)}) collective-permute-start(bf16[5,256,1024]{2,1,0:T(8,128)(2,1)} %pad_maximum_fusion.43), channel_id=1, source_target_pairs={{0,16},{8,24},{16,0},{24,8},{1,17},{9,25},{17,1},{25,9},{2,18},{10... | collective-permute-start | bytes 7864328 | tf_op jit(solution)/shard_map/ppermute | solution.py:422
  145.9 62.4 %collective-permute-start.12 = (bf16[5,256,1024]{2,1,0:T(8,128)(2,1)}, bf16[5,256,1024]{2,1,0:T(8,128)(2,1)}, u32[]{:S(2)}, u32[]{:S(2)}) collective-permute-start(bf16[5,256,1024]{2,1,0:T(8,128)(2,1)} %collective-permute-done.11), channel_id=1, source_target_pairs={{0,8},{8,0},{16,24},{24,16},{1,9},{9,1},{17,25},{25,17},{2,10},{10... | collective-permute-start | bytes 7864328 | tf_op jit(solution)/shard_map/ppermute | solution.py:417
  147.6 60.5 %collective-permute-start.18 = (bf16[1,256,4096]{2,1,0:T(8,128)(2,1)}, bf16[1,256,4096]{2,1,0:T(8,128)(2,1)}, u32[]{:S(2)}, u32[]{:S(2)}) collective-permute-start(bf16[1,256,4096]{2,1,0:T(8,128)(2,1)} %convert_bitcast_fusion.3), channel_id=1, source_target_pairs={{0,16},{8,24},{16,0},{24,8},{1,17},{9,25},{17,1},{25,9},{2,18},{10... | collective-permute-start | bytes 6291464 | tf_op jit(solution)/shard_map/ppermute | solution.py:422
  154.9 48.9 %collective-permute-start.15 = (bf16[2,2,128,1024]{3,2,1,0:T(8,128)(2,1)}, bf16[2,2,128,1024]{3,2,1,0:T(8,128)(2,1)}, u32[]{:S(2)}, u32[]{:S(2)}) collective-permute-start(bf16[2,2,128,1024]{3,2,1,0:T(8,128)(2,1)} %get-tuple-element.304), channel_id=1, source_target_pairs={{0,4},{1,5},{2,6},{3,7},{4,0},{5,1},{6,2},{7,3},{8,12},{9,13},{10,... | collective-permute-start | bytes 3145736 | tf_op jit(solution)/shard_map/ppermute | solution.py:427
  155.2 48.7 %collective-permute-start.14 = (bf16[2,2,128,1024]{3,2,1,0:T(8,128)(2,1)}, bf16[2,2,128,1024]{3,2,1,0:T(8,128)(2,1)}, u32[]{:S(2)}, u32[]{:S(2)}) collective-permute-start(bf16[2,2,128,1024]{3,2,1,0:T(8,128)(2,1)} %get-tuple-element.304), channel_id=1, source_target_pairs={{0,2},{1,3},{2,0},{3,1},{4,6},{5,7},{6,4},{7,5},{8,10},{9,11},{10,... | collective-permute-start | bytes 3145736 | tf_op jit(solution)/shard_map/ppermute | solution.py:427
  203.8 73.7 %collective-permute-start.17 = (bf16[1,256,4096]{2,1,0:T(8,128)(2,1)}, bf16[1,256,4096]{2,1,0:T(8,128)(2,1)}, u32[]{:S(2)}, u32[]{:S(2)}) collective-permute-start(bf16[1,256,4096]{2,1,0:T(8,128)(2,1)} %convert_bitcast_fusion.3), channel_id=1, source_target_pairs={{0,8},{8,0},{16,24},{24,16},{1,9},{9,1},{17,25},{25,17},{2,10},{10... | collective-permute-start | bytes 6291464 | tf_op jit(solution)/shard_map/ppermute | solution.py:417
  203.9 97.1 %collective-permute-start.20 = (bf16[1,1024,1024]{2,1,0:T(8,128)(2,1)}, bf16[1,1024,1024]{2,1,0:T(8,128)(2,1)}, u32[]{:S(2)}, u32[]{:S(2)}) collective-permute-start(bf16[1,1024,1024]{2,1,0:T(8,128)(2,1)} %convert_bitcast_fusion), channel_id=1, source_target_pairs={{0,8},{8,0},{16,24},{24,16},{1,9},{9,1},{17,25},{25,17},{2,10},{10... | collective-permute-start | bytes 6291464 | tf_op jit(solution)/shard_map/ppermute | solution.py:417
  208.1 68.9 %collective-permute-start.21 = (bf16[1,1024,1024]{2,1,0:T(8,128)(2,1)}, bf16[1,1024,1024]{2,1,0:T(8,128)(2,1)}, u32[]{:S(2)}, u32[]{:S(2)}) collective-permute-start(bf16[1,1024,1024]{2,1,0:T(8,128)(2,1)} %convert_bitcast_fusion), channel_id=1, source_target_pairs={{0,16},{8,24},{16,0},{24,8},{1,17},{9,25},{17,1},{25,9},{2,18},{10... | collective-permute-start | bytes 6291464 | tf_op jit(solution)/shard_map/ppermute | solution.py:422
  235.6 42.0 %collective-permute-start.19 = (bf16[1,256,4096]{2,1,0:T(8,128)(2,1)}, bf16[1,256,4096]{2,1,0:T(8,128)(2,1)S(1)}, u32[]{:S(2)}, u32[]{:S(2)}) collective-permute-start(bf16[1,256,4096]{2,1,0:T(8,128)(2,1)} %collective-permute-done.18), channel_id=1, source_target_pairs={{0,8},{8,0},{16,24},{24,16},{1,9},{9,1},{17,25},{25,17},{2,10},{10... | collective-permute-start | bytes 6291464 | tf_op jit(solution)/shard_map/ppermute | solution.py:417
  277.0 24.0 %collective-permute-start.22 = (bf16[1,1024,1024]{2,1,0:T(8,128)(2,1)}, bf16[1,1024,1024]{2,1,0:T(8,128)(2,1)}, u32[]{:S(2)}, u32[]{:S(2)}) collective-permute-start(bf16[1,1024,1024]{2,1,0:T(8,128)(2,1)} %collective-permute-done.21), channel_id=1, source_target_pairs={{0,8},{8,0},{16,24},{24,16},{1,9},{9,1},{17,25},{25,17},{2,10},{10... | collective-permute-start | bytes 6291464 | tf_op jit(solution)/shard_map/ppermute | solution.py:417
  374.1 20.4 %collective-permute-start.24 = (bf16[2,8,1,32,4096]{4,3,1,2,0:T(8,128)(2,1)}, bf16[2,8,1,32,4096]{4,3,1,2,0:T(8,128)(2,1)}, u32[]{:S(2)}, u32[]{:S(2)}) collective-permute-start(bf16[2,8,1,32,4096]{4,3,1,2,0:T(8,128)(2,1)} %dynamic-slice_bitcast_fusion), channel_id=1, source_target_pairs={{0,8},{8,0},{16,24},{24,16},{1,9},{9,1},{17,25},{25,17},{2,10},{10... | collective-permute-start | bytes 12582920 | tf_op jit(solution)/shard_map/ppermute | solution.py:417
  374.6 68.8 %collective-permute-start.26 = (bf16[2,4,1,128,1024]{4,3,1,0,2:T(8,128)(2,1)}, bf16[2,4,1,128,1024]{4,3,1,0,2:T(8,128)(2,1)S(1)}, u32[]{:S(2)}, u32[]{:S(2)}) collective-permute-start(bf16[2,4,1,128,1024]{4,3,1,0,2:T(8,128)(2,1)} %dynamic-slice_bitcast_fusion.5), channel_id=1, source_target_pairs={{0,1},{1,0},{2,3},{3,2},{4,5},{5,4},{6,7},{7,6},{8,9},{9,8},{10,11... | collective-permute-start | bytes 6291464 | tf_op jit(solution)/shard_map/ppermute | solution.py:427
  401.0 70.3 %collective-permute-start.25 = (bf16[8,1,32,4096]{3,2,0,1:T(8,128)(2,1)}, bf16[8,1,32,4096]{3,2,0,1:T(8,128)(2,1)}, u32[]{:S(2)}, u32[]{:S(2)}) collective-permute-start(bf16[8,1,32,4096]{3,2,0,1:T(8,128)(2,1)} %dynamic-slice_bitcast_fusion.4), channel_id=1, source_target_pairs={{0,16},{8,24},{16,0},{24,8},{1,17},{9,25},{17,1},{25,9},{2,18},{10... | collective-permute-start | bytes 6291464 | tf_op jit(solution)/shard_map/ppermute | solution.py:422
  491.7 28.8 %collective-permute-start.27 = (bf16[2,8,5,32,1024]{4,3,2,1,0:T(8,128)(2,1)S(1)}, bf16[2,8,5,32,1024]{4,3,2,1,0:T(8,128)(2,1)S(1)}, u32[]{:S(2)}, u32[]{:S(2)}) collective-permute-start(bf16[2,8,5,32,1024]{4,3,2,1,0:T(8,128)(2,1)S(1)} %get-tuple-element.553), channel_id=1, source_target_pairs={{0,8},{8,0},{16,24},{24,16},{1,9},{9,1},{17,25},{25,17},{2,10},{10... | collective-permute-start | bytes 15728648 | tf_op jit(solution)/shard_map/ppermute | solution.py:417
  491.7 25.6 %collective-permute-start.28 = (bf16[4,1,128,1024]{3,2,0,1:T(8,128)(2,1)S(1)}, bf16[4,1,128,1024]{3,2,0,1:T(8,128)(2,1)S(1)}, u32[]{:S(2)}, u32[]{:S(2)}) collective-permute-start(bf16[4,1,128,1024]{3,2,0,1:T(8,128)(2,1)S(1)} %dynamic-slice_bitcast_fusion.14), channel_id=1, source_target_pairs={{0,16},{8,24},{16,0},{24,8},{1,17},{9,25},{17,1},{25,9},{2,18},{10... | collective-permute-start | bytes 3145736 | tf_op jit(solution)/shard_map/ppermute | solution.py:422
  494.9 89.0 %collective-permute-start.32 = (bf16[2,2,128,1024]{3,2,1,0:T(8,128)(2,1)}, bf16[2,2,128,1024]{3,2,1,0:T(8,128)(2,1)S(1)}, u32[]{:S(2)}, u32[]{:S(2)}) collective-permute-start(bf16[2,2,128,1024]{3,2,1,0:T(8,128)(2,1)} %get-tuple-element.538), channel_id=1, source_target_pairs={{0,6},{1,7},{2,4},{3,5},{4,2},{5,3},{6,0},{7,1},{8,14},{9,15},{10,... | collective-permute-start | bytes 3145736 | tf_op jit(solution)/shard_map/ppermute | solution.py:427
  500.5 91.2 %collective-permute-start.31 = (bf16[2,2,128,1024]{3,2,1,0:T(8,128)(2,1)}, bf16[2,2,128,1024]{3,2,1,0:T(8,128)(2,1)}, u32[]{:S(2)}, u32[]{:S(2)}) collective-permute-start(bf16[2,2,128,1024]{3,2,1,0:T(8,128)(2,1)} %get-tuple-element.537), channel_id=1, source_target_pairs={{0,4},{1,5},{2,6},{3,7},{4,0},{5,1},{6,2},{7,3},{8,12},{9,13},{10,... | collective-permute-start | bytes 3145736 | tf_op jit(solution)/shard_map/ppermute | solution.py:427
  503.7 88.1 %collective-permute-start.30 = (bf16[2,2,128,1024]{3,2,1,0:T(8,128)(2,1)}, bf16[2,2,128,1024]{3,2,1,0:T(8,128)(2,1)}, u32[]{:S(2)}, u32[]{:S(2)}) collective-permute-start(bf16[2,2,128,1024]{3,2,1,0:T(8,128)(2,1)} %get-tuple-element.536), channel_id=1, source_target_pairs={{0,2},{1,3},{2,0},{3,1},{4,6},{5,7},{6,4},{7,5},{8,10},{9,11},{10,... | collective-permute-start | bytes 3145736 | tf_op jit(solution)/shard_map/ppermute | solution.py:427
  517.3 57.5 %collective-permute-start.29 = (bf16[4,1,32,4096]{3,2,0,1:T(8,128)(2,1)}, bf16[4,1,32,4096]{3,2,0,1:T(8,128)(2,1)}, u32[]{:S(2)}, u32[]{:S(2)}) collective-permute-start(bf16[4,1,32,4096]{3,2,0,1:T(8,128)(2,1)} %dynamic-slice_bitcast_fusion.13), channel_id=1, source_target_pairs={{0,1},{1,0},{2,3},{3,2},{4,5},{5,4},{6,7},{7,6},{8,9},{9,8},{10,11... | collective-permute-start | bytes 3145736 | tf_op jit(solution)/shard_map/ppermute | solution.py:427
  615.5 55.3 %collective-permute-start.34 = (bf16[2,8,3,32,1024]{4,3,2,1,0:T(8,128)(2,1)}, bf16[2,8,3,32,1024]{4,3,2,1,0:T(8,128)(2,1)}, u32[]{:S(2)}, u32[]{:S(2)}) collective-permute-start(bf16[2,8,3,32,1024]{4,3,2,1,0:T(8,128)(2,1)} %pad_maximum_fusion.42), channel_id=1, source_target_pairs={{0,8},{8,0},{16,24},{24,16},{1,9},{9,1},{17,25},{25,17},{2,10},{10... | collective-permute-start | bytes 9437192 | tf_op jit(solution)/shard_map/ppermute | solution.py:417
  617.6 26.3 %collective-permute-start.56 = (bf16[1,128,1024]{2,1,0:T(8,128)(2,1)}, bf16[1,128,1024]{2,1,0:T(8,128)(2,1)}, u32[]{:S(2)}, u32[]{:S(2)}) collective-permute-start(bf16[1,128,1024]{2,1,0:T(8,128)(2,1)} %get-tuple-element.563), channel_id=1, source_target_pairs={{0,6},{1,7},{2,4},{3,5},{4,2},{5,3},{6,0},{7,1},{8,14},{9,15},{10,... | collective-permute-start | bytes 786440 | tf_op jit(solution)/shard_map/ppermute | solution.py:427
  629.9 24.9 %collective-permute-start.55 = (bf16[1,128,1024]{2,1,0:T(8,128)(2,1)}, bf16[1,128,1024]{2,1,0:T(8,128)(2,1)}, u32[]{:S(2)}, u32[]{:S(2)}) collective-permute-start(bf16[1,128,1024]{2,1,0:T(8,128)(2,1)} %get-tuple-element.564), channel_id=1, source_target_pairs={{0,4},{1,5},{2,6},{3,7},{4,0},{5,1},{6,2},{7,3},{8,12},{9,13},{10,... | collective-permute-start | bytes 786440 | tf_op jit(solution)/shard_map/ppermute | solution.py:427
  632.5 22.4 %collective-permute-start.54 = (bf16[1,128,1024]{2,1,0:T(8,128)(2,1)S(1)}, bf16[1,128,1024]{2,1,0:T(8,128)(2,1)}, u32[]{:S(2)}, u32[]{:S(2)}) collective-permute-start(bf16[1,128,1024]{2,1,0:T(8,128)(2,1)S(1)} %get-tuple-element.562), channel_id=1, source_target_pairs={{0,2},{1,3},{2,0},{3,1},{4,6},{5,7},{6,4},{7,5},{8,10},{9,11},{10,... | collective-permute-start | bytes 786440 | tf_op jit(solution)/shard_map/ppermute | solution.py:427
  641.4 23.7 %collective-permute-start.47 = (f32[7,1024]{1,0:T(8,128)S(1)}, f32[7,1024]{1,0:T(8,128)S(1)}, u32[]{:S(2)}, u32[]{:S(2)}) collective-permute-start(f32[7,1024]{1,0:T(8,128)S(1)} %concatenate.143), channel_id=1, source_target_pairs={{0,6},{1,7},{2,4},{3,5},{4,2},{5,3},{6,0},{7,1},{8,14},{9,15},{10,... | collective-permute-start | bytes 86024 | tf_op jit(solution)/shard_map/ppermute | solution.py:427
  658.8 61.0 %collective-permute-start.39 = (bf16[8,5,32,1024]{3,2,1,0:T(8,128)(2,1)}, bf16[8,5,32,1024]{3,2,1,0:T(8,128)(2,1)S(1)}, u32[]{:S(2)}, u32[]{:S(2)}) collective-permute-start(bf16[8,5,32,1024]{3,2,1,0:T(8,128)(2,1)} %dynamic-slice_bitcast_fusion.2), channel_id=1, source_target_pairs={{0,16},{8,24},{16,0},{24,8},{1,17},{9,25},{17,1},{25,9},{2,18},{10... | collective-permute-start | bytes 7864328 | tf_op jit(solution)/shard_map/ppermute | solution.py:422
  665.1 45.3 %collective-permute-start.33 = (bf16[4,2,128,1024]{3,2,1,0:T(8,128)(2,1)S(1)}, bf16[4,2,128,1024]{3,2,1,0:T(8,128)(2,1)S(1)}, u32[]{:S(2)}, u32[]{:S(2)}) collective-permute-start(bf16[4,2,128,1024]{3,2,1,0:T(8,128)(2,1)S(1)} %slice.537), channel_id=1, source_target_pairs={{0,1},{1,0},{2,3},{3,2},{4,5},{5,4},{6,7},{7,6},{8,9},{9,8},{10,11... | collective-permute-start | bytes 6291464 | tf_op jit(solution)/shard_map/ppermute | solution.py:427
  674.1 77.7 %collective-permute-start.40 = (bf16[8,3,32,1024]{3,2,1,0:T(8,128)(2,1)S(1)}, bf16[8,3,32,1024]{3,2,1,0:T(8,128)(2,1)S(1)}, u32[]{:S(2)}, u32[]{:S(2)}) collective-permute-start(bf16[8,3,32,1024]{3,2,1,0:T(8,128)(2,1)S(1)} %dynamic-slice_bitcast_fusion.6), channel_id=1, source_target_pairs={{0,16},{8,24},{16,0},{24,8},{1,17},{9,25},{17,1},{25,9},{2,18},{10... | collective-permute-start | bytes 4718600 | tf_op jit(solution)/shard_map/ppermute | solution.py:422
  676.9 78.9 %collective-permute-start.49 = (f32[7,1024]{1,0:T(8,128)S(1)}, f32[7,1024]{1,0:T(8,128)S(1)}, u32[]{:S(2)}, u32[]{:S(2)}) collective-permute-start(f32[7,1024]{1,0:T(8,128)S(1)} %fusion.196), channel_id=1, source_target_pairs={{0,1},{1,0},{2,3},{3,2},{4,5},{5,4},{6,7},{7,6},{8,9},{9,8},{10,11... | collective-permute-start | bytes 86024 | tf_op jit(solution)/shard_map/ppermute | solution.py:427
  754.5 59.8 %collective-permute-start.41 = (bf16[4,8,32,1024]{3,2,1,0:T(8,128)(2,1)}, bf16[4,8,32,1024]{3,2,1,0:T(8,128)(2,1)}, u32[]{:S(2)}, u32[]{:S(2)}) collective-permute-start(bf16[4,8,32,1024]{3,2,1,0:T(8,128)(2,1)} %dynamic-slice_bitcast_fusion.3), channel_id=1, source_target_pairs={{0,1},{1,0},{2,3},{3,2},{4,5},{5,4},{6,7},{7,6},{8,9},{9,8},{10,11... | collective-permute-start | bytes 6291464 | tf_op jit(solution)/shard_map/ppermute | solution.py:427
  758.4 53.7 %collective-permute-start.38 = (bf16[2,128,1024]{2,1,0:T(8,128)(2,1)}, bf16[2,128,1024]{2,1,0:T(8,128)(2,1)}, u32[]{:S(2)}, u32[]{:S(2)}) collective-permute-start(bf16[2,128,1024]{2,1,0:T(8,128)(2,1)} %slice_bitcast_fusion.124), channel_id=1, source_target_pairs={{0,1},{1,0},{2,3},{3,2},{4,5},{5,4},{6,7},{7,6},{8,9},{9,8},{10,11... | collective-permute-start | bytes 1572872 | tf_op jit(solution)/shard_map/ppermute | solution.py:427
  761.7 20.3 %collective-permute-start.52 = (bf16[1,32,4096]{2,1,0:T(8,128)(2,1)}, bf16[1,32,4096]{2,1,0:T(8,128)(2,1)}, u32[]{:S(2)}, u32[]{:S(2)}) collective-permute-start(bf16[1,32,4096]{2,1,0:T(8,128)(2,1)} %get-tuple-element.567), channel_id=1, source_target_pairs={{0,4},{1,5},{2,6},{3,7},{4,0},{5,1},{6,2},{7,3},{8,12},{9,13},{10,... | collective-permute-start | bytes 786440 | tf_op jit(solution)/shard_map/ppermute | solution.py:427
  784.3 36.5 %collective-permute-start.37 = (bf16[2,128,1024]{2,1,0:T(8,128)(2,1)S(1)}, bf16[2,128,1024]{2,1,0:T(8,128)(2,1)S(1)}, u32[]{:S(2)}, u32[]{:S(2)}) collective-permute-start(bf16[2,128,1024]{2,1,0:T(8,128)(2,1)S(1)} %get-tuple-element.544), channel_id=1, source_target_pairs={{0,6},{1,7},{2,4},{3,5},{4,2},{5,3},{6,0},{7,1},{8,14},{9,15},{10,... | collective-permute-start | bytes 1572872 | tf_op jit(solution)/shard_map/ppermute | solution.py:427
  786.3 67.6 %collective-permute-start.36 = (bf16[2,128,1024]{2,1,0:T(8,128)(2,1)S(1)}, bf16[2,128,1024]{2,1,0:T(8,128)(2,1)S(1)}, u32[]{:S(2)}, u32[]{:S(2)}) collective-permute-start(bf16[2,128,1024]{2,1,0:T(8,128)(2,1)S(1)} %get-tuple-element.545), channel_id=1, source_target_pairs={{0,4},{1,5},{2,6},{3,7},{4,0},{5,1},{6,2},{7,3},{8,12},{9,13},{10,... | collective-permute-start | bytes 1572872 | tf_op jit(solution)/shard_map/ppermute | solution.py:427
  786.3 67.6 %collective-permute-start.35 = (bf16[2,128,1024]{2,1,0:T(8,128)(2,1)S(1)}, bf16[2,128,1024]{2,1,0:T(8,128)(2,1)S(1)}, u32[]{:S(2)}, u32[]{:S(2)}) collective-permute-start(bf16[2,128,1024]{2,1,0:T(8,128)(2,1)S(1)} %get-tuple-element.543), channel_id=1, source_target_pairs={{0,2},{1,3},{2,0},{3,1},{4,6},{5,7},{6,4},{7,5},{8,10},{9,11},{10,... | collective-permute-start | bytes 1572872 | tf_op jit(solution)/shard_map/ppermute | solution.py:427
  817.1 39.5 %collective-permute-start.44 = (bf16[8,32,1024]{2,1,0:T(8,128)(2,1)S(1)}, bf16[8,32,1024]{2,1,0:T(8,128)(2,1)S(1)}, u32[]{:S(2)}, u32[]{:S(2)}) collective-permute-start(bf16[8,32,1024]{2,1,0:T(8,128)(2,1)S(1)} %get-tuple-element.541), channel_id=1, source_target_pairs={{0,6},{1,7},{2,4},{3,5},{4,2},{5,3},{6,0},{7,1},{8,14},{9,15},{10,... | collective-permute-start | bytes 1572872 | tf_op jit(solution)/shard_map/ppermute | solution.py:427
  820.8 52.4 %collective-permute-start.43 = (bf16[8,32,1024]{2,1,0:T(8,128)(2,1)S(1)}, bf16[8,32,1024]{2,1,0:T(8,128)(2,1)S(1)}, u32[]{:S(2)}, u32[]{:S(2)}) collective-permute-start(bf16[8,32,1024]{2,1,0:T(8,128)(2,1)S(1)} %get-tuple-element.542), channel_id=1, source_target_pairs={{0,4},{1,5},{2,6},{3,7},{4,0},{5,1},{6,2},{7,3},{8,12},{9,13},{10,... | collective-permute-start | bytes 1572872 | tf_op jit(solution)/shard_map/ppermute | solution.py:427
  820.8 52.3 %collective-permute-start.42 = (bf16[8,32,1024]{2,1,0:T(8,128)(2,1)S(1)}, bf16[8,32,1024]{2,1,0:T(8,128)(2,1)S(1)}, u32[]{:S(2)}, u32[]{:S(2)}) collective-permute-start(bf16[8,32,1024]{2,1,0:T(8,128)(2,1)S(1)} %get-tuple-element.540), channel_id=1, source_target_pairs={{0,2},{1,3},{2,0},{3,1},{4,6},{5,7},{6,4},{7,5},{8,10},{9,11},{10,... | collective-permute-start | bytes 1572872 | tf_op jit(solution)/shard_map/ppermute | solution.py:427
  (137 other events, 1761.3 us)
